TPU v7x, 32 devices: a whole 2x2x4 slice. The times are simulated.
32 devices in a mesh: gx: 8 (over z, x), gy: 4 (over y, core).
Axes of the slice: x: 2, y: 2, z: 4, core: 2. Of those that a mesh axis runs over, the one named last changes fastest.
Arguments:
- f_in: float32 [19, 16, 128, 512], P(None, None, 'gx', 'gy')
- rotor_place: int32 [40, 3], replicated, may hold values from 0 to 15, as said below
- marker_cell: int32 [40, 8192], replicated, may hold values from 16384 to 505663, as said below
- pitch_phase: int32 [40, 2], replicated, may hold values from 0 to 63
- blade_area: float32 [8, 4, 2, 8192], P('gx', 'gy'), may hold values from 0.3 to 1.2
- blade_twist: float32 [8, 4, 2, 8192], P('gx', 'gy'), may hold values from -0.6 to 0.6
- blade_speed: float32 [8, 4, 2, 8192], P('gx', 'gy'), may hold values from 1.5 to 3
- blade_angle: float32 [8, 4, 2, 8192], P('gx', 'gy'), may hold values from -3.14 to 3.14, as said below
- filt_in: float32 [8, 4, 2, 3, 8192], P('gx', 'gy'), may hold values from -1.5 to 1.5
Outputs:
- f_out: float32 [19, 16, 128, 512], P(None, None, 'gx', 'gy')
- loads_out: float32 [8, 4, 2, 3, 8192], P('gx', 'gy')
- filt_out: float32 [8, 4, 2, 3, 8192], P('gx', 'gy')
Inputs may be any that keep to these rules, and one draw needn't show every extreme that they name: `rotor_place`: column 0 is a streamwise tile holding at most 5 rotors, some exactly 5; column 1 a plane 0 to 15; column 2 the owner's spanwise tile. Every streamwise tile holds 2 or more rotors; one owner holds at most 2 rotors, exactly 2 in every streamwise tile. `marker_cell`: all stencil cells of one rotor lie within two neighbouring spanwise tiles and within levels 0 to 15; a rotor's stencils may cover one or two tiles. `blade_angle`: azimuths in radians.
All inputs are finite; a program needn't handle non-finite values.
Results may differ from a plain program's by a relative error of at most 0.0003.
Values sent between devices are 32-bit elements; how exact they have to be, the bound alone decides.
No kernel may reach another device: no remote copies, remote signals or barrier semaphores. Data moves between devices by JAX's collectives and lax.ppermute only.
A program may use at most 128 MiB of HBM per device.

v0:
```python
import math

import jax
import jax.numpy as jnp
import numpy as np
from jax import lax
from jax.sharding import PartitionSpec as P

PHASES = 64


LATTICE_DIRS = np.array(
    [
        [0, 0, 0],
        [1, 0, 0],
        [-1, 0, 0],
        [0, 1, 0],
        [0, -1, 0],
        [0, 0, 1],
        [0, 0, -1],
        [1, 1, 0],
        [-1, -1, 0],
        [1, -1, 0],
        [-1, 1, 0],
        [1, 0, 1],
        [-1, 0, -1],
        [1, 0, -1],
        [-1, 0, 1],
        [0, 1, 1],
        [0, -1, -1],
        [0, 1, -1],
        [0, -1, 1],
    ]
)
OPPOSITE = [0, 2, 1, 4, 3, 6, 5, 8, 7, 10, 9, 12, 11, 14, 13, 16, 15, 18, 17]
LATTICE_WEIGHTS = np.array([1.0 / 3.0] + [1.0 / 18.0] * 6 + [1.0 / 36.0] * 12)
OMEGA = 1.0 / 0.6
SPREAD = 0.01
MIX = 0.5
PITCH_AMP = 0.2


def extended(block, sides, width):
    for axis, dim in sides:
        count = lax.axis_size(axis)
        forward = [(i, i + 1) for i in range(count - 1)]
        forward.append((count - 1, 0))
        backward = [(target, source) for source, target in forward]
        low = lax.ppermute(
            lax.slice_in_dim(block, block.shape[dim] - width, None, axis=dim), axis, forward
        )
        high = lax.ppermute(lax.slice_in_dim(block, 0, width, axis=dim), axis, backward)
        block = jnp.concatenate([low, block, high], axis=dim)
    return block


def peskin(offsets):
    distance = jnp.abs(offsets)
    near_arg = jnp.maximum(1.0 + 4.0 * distance - 4.0 * distance * distance, 1.0)
    far_arg = jnp.maximum(-7.0 + 12.0 * distance - 4.0 * distance * distance, 1.0)
    near_part = (3.0 - 2.0 * distance + jnp.sqrt(near_arg)) / 8.0
    far_part = (5.0 - 2.0 * distance - jnp.sqrt(far_arg)) / 8.0
    return jnp.where(distance <= 1.0, near_part, far_part)


def dense_rows(anchor, weights, width, start):
    column = jnp.arange(width, dtype=jnp.int32)[None, :] + start
    gap = column - anchor[:, None]
    summed = jnp.zeros(gap.shape, jnp.float32)
    for corner in range(4):
        summed = summed + jnp.where(gap == corner, weights[corner][:, None], 0.0)
    return summed


def stencil_tables(cell_codes, levels, width, start):
    fraction_z = (cell_codes % 8).astype(jnp.float32) / 8.0
    fraction_y = (cell_codes // 8 % 8).astype(jnp.float32) / 8.0
    cell_z = cell_codes // 64 % levels
    cell_y = cell_codes // (64 * levels)
    weights_y = [peskin(corner - 1.0 - fraction_y) for corner in range(4)]
    weights_z = [peskin(corner - 1.0 - fraction_z) for corner in range(4)]
    across = dense_rows(cell_y, weights_y, width, start)
    upward = dense_rows(cell_z, weights_z, levels, jnp.int32(0))
    return (across, upward)


def sample_section(section, across, upward):
    levels = section.shape[1]
    width = section.shape[2]
    flattened = jnp.transpose(section, (2, 0, 1)).reshape(width, 3 * levels)
    partial_value = jnp.dot(
        across, flattened, precision=lax.Precision.HIGHEST, preferred_element_type=jnp.float32
    )
    partial_value = partial_value.reshape(across.shape[0], 3, levels)
    return jnp.transpose(jnp.sum(partial_value * upward[:, None, :], axis=2))


def spread_section(marker_loads, across, upward):
    markers = upward.shape[0]
    levels = upward.shape[1]
    weighted = (upward[:, None, :] * jnp.transpose(marker_loads)[:, :, None]).reshape(
        markers, 3 * levels
    )
    section = lax.dot_general(
        weighted,
        across,
        (((0,), (0,)), ((), ())),
        precision=lax.Precision.HIGHEST,
        preferred_element_type=jnp.float32,
    )
    return -SPREAD * section.reshape(3, levels, across.shape[1])


def pitch_angles(phases):
    return PITCH_AMP * jnp.sin(2.0 * math.pi * phases.astype(jnp.float32) / PHASES)


def blade_loads(filtered, area, twist, speed, angle, pitch):
    axial_speed = filtered[..., 0, :]
    sin_t = jnp.sin(angle)
    cos_t = jnp.cos(angle)
    tangent = speed + sin_t * filtered[..., 1, :] - cos_t * filtered[..., 2, :]
    square = axial_speed * axial_speed + tangent * tangent
    magnitude = jnp.sqrt(square)
    sin_p = axial_speed / magnitude
    cos_p = tangent / magnitude
    blade_pitch = twist + pitch
    sin_a = sin_p * jnp.cos(blade_pitch) - cos_p * jnp.sin(blade_pitch)
    cos_a = cos_p * jnp.cos(blade_pitch) + sin_p * jnp.sin(blade_pitch)
    lift_coef = 2.0 * math.pi * sin_a * cos_a
    drag_coef = 0.02 + sin_a * sin_a
    dynamic = 0.5 * area * square
    normal = dynamic * (lift_coef * cos_p + drag_coef * sin_p)
    tangential = dynamic * (lift_coef * sin_p - drag_coef * cos_p)
    return jnp.stack([normal, -tangential * sin_t, tangential * cos_t], axis=-2)


def velocity(populations):
    lattice = jnp.asarray(LATTICE_DIRS, jnp.float32)
    density = jnp.sum(populations, axis=0)
    parts = [
        jnp.sum(populations * lattice[:, axis][:, None, None, None], axis=0) / density
        for axis in range(3)
    ]
    return jnp.stack(parts)


def collide(populations, force_field):
    lattice = jnp.asarray(LATTICE_DIRS, jnp.float32)
    weights = jnp.asarray(LATTICE_WEIGHTS, jnp.float32)[:, None, None, None]
    density = jnp.sum(populations, axis=0)
    columns = [lattice[:, axis][:, None, None, None] for axis in range(3)]
    parts = [
        (jnp.sum(populations * columns[axis], axis=0) + 0.5 * force_field[axis]) / density
        for axis in range(3)
    ]
    project = (
        columns[0] * parts[0][None] + columns[1] * parts[1][None] + columns[2] * parts[2][None]
    )
    force_proj = (
        columns[0] * force_field[0][None]
        + columns[1] * force_field[1][None]
        + columns[2] * force_field[2][None]
    )
    speed_sq = parts[0] * parts[0] + parts[1] * parts[1] + parts[2] * parts[2]
    work_rate = parts[0] * force_field[0] + parts[1] * force_field[1] + parts[2] * force_field[2]
    equilibrium = (
        weights
        * density[None]
        * (1.0 + 3.0 * project + 4.5 * project * project - 1.5 * speed_sq[None])
    )
    source = (
        (1.0 - 0.5 * OMEGA)
        * weights
        * (3.0 * (force_proj - work_rate[None]) + 9.0 * project * force_proj)
    )
    return populations - OMEGA * (populations - equilibrium) + source


def stream(padded, collided):
    x_cells = collided.shape[2]
    y_cells = collided.shape[3]
    outgoing = []
    for direction in range(19):
        shift_x = int(LATTICE_DIRS[direction, 0])
        shift_y = int(LATTICE_DIRS[direction, 1])
        shift_z = int(LATTICE_DIRS[direction, 2])
        pulled = padded[
            direction, :, 1 - shift_x : 1 - shift_x + x_cells, 1 - shift_y : 1 - shift_y + y_cells
        ]
        mirror = collided[OPPOSITE[direction]]
        if shift_z == 1:
            pulled = jnp.concatenate([mirror[:1], pulled[:-1]], axis=0)
        elif shift_z == -1:
            pulled = jnp.concatenate([pulled[1:], mirror[-1:]], axis=0)
        outgoing.append(pulled)
    return jnp.stack(outgoing)


def with_ghosts(collided):
    padded = extended(collided, (("gx", 2), ("gy", 3)), 1)
    return padded


def local(
    f_in,
    rotor_place,
    marker_cell,
    pitch_phase,
    blade_area,
    blade_twist,
    blade_speed,
    blade_angle,
    filt_in,
):
    levels = f_in.shape[1]
    x_cells = f_in.shape[2]
    y_cells = f_in.shape[3]
    rotors = rotor_place.shape[0]
    step_count = pitch_phase.shape[1]
    owned_count = filt_in.shape[2]
    spread_x = lax.axis_size("gx")
    row_slots = (rotors + spread_x - 1) // spread_x
    here_x = lax.axis_index("gx")
    here_y = lax.axis_index("gy")
    street = rotor_place[:, 0]
    plane_x = rotor_place[:, 1]
    owner_y = rotor_place[:, 2]
    rotor_ids = jnp.arange(rotors, dtype=jnp.int32)
    earlier = rotor_ids[None, :] < rotor_ids[:, None]
    same_row = street[:, None] == street[None, :]
    row_rank = jnp.sum((earlier & same_row).astype(jnp.int32), axis=1)
    same_owner = same_row & (owner_y[:, None] == owner_y[None, :])
    owner_rank = jnp.sum((earlier & same_owner).astype(jnp.int32), axis=1)
    slot_ids = jnp.arange(row_slots, dtype=jnp.int32)
    slot_pick = ((street[None, :] == here_x) & (row_rank[None, :] == slot_ids[:, None])).astype(
        jnp.int32
    )
    slot_valid = jnp.sum(slot_pick, axis=1)
    slot_rotor = jnp.sum(slot_pick * rotor_ids[None, :], axis=1)
    slot_codes = jnp.take(marker_cell, slot_rotor, axis=0)
    slot_plane = jnp.take(plane_x, slot_rotor)
    slot_pitch = pitch_angles(jnp.take(pitch_phase, slot_rotor, axis=0))
    owned_here = (jnp.take(owner_y, slot_rotor) == here_y) & (slot_valid > 0)
    owned_ids = jnp.arange(owned_count, dtype=jnp.int32)
    own_pick = (
        owned_here[None, :] & (jnp.take(owner_rank, slot_rotor)[None, :] == owned_ids[:, None])
    ).astype(jnp.float32)
    valid_float = slot_valid.astype(jnp.float32)
    start_y = here_y * y_cells
    tables = []
    for slot_index in range(row_slots):
        across, upward = stencil_tables(slot_codes[slot_index], levels, y_cells, start_y)
        tables.append((across * valid_float[slot_index], upward))
    x_ids = jnp.arange(x_cells, dtype=jnp.int32)
    filtered = filt_in[0, 0]
    own_pitch = jnp.sum(own_pick[:, :, None] * slot_pitch[None], axis=1)
    populations = f_in
    for step_index in range(step_count):
        field_speed = velocity(populations)
        samples = jnp.stack(
            [
                sample_section(
                    lax.dynamic_index_in_dim(
                        field_speed, slot_plane[slot_index], 2, keepdims=False
                    ),
                    tables[slot_index][0],
                    tables[slot_index][1],
                )
                for slot_index in range(row_slots)
            ]
        )
        sampled = lax.psum(samples, "gy")
        own_sampled = jnp.sum(own_pick[:, :, None, None] * sampled[None], axis=1)
        filtered = filtered + MIX * (own_sampled - filtered)
        own_loads = blade_loads(
            filtered,
            blade_area[0, 0],
            blade_twist[0, 0],
            blade_speed[0, 0],
            blade_angle[0, 0],
            own_pitch[:, step_index][:, None],
        )
        row_loads = jnp.sum(own_pick[:, :, None, None] * own_loads[:, None], axis=0)
        load_rows = lax.psum(row_loads, "gy")
        force_field = jnp.zeros((3, levels, x_cells, y_cells), jnp.float32)
        for slot_index in range(row_slots):
            section = spread_section(
                load_rows[slot_index], tables[slot_index][0], tables[slot_index][1]
            )
            plane_mask = (x_ids == slot_plane[slot_index]).astype(jnp.float32)
            force_field = force_field + section[:, :, None, :] * plane_mask[None, None, :, None]
        collided = collide(populations, force_field)
        populations = stream(with_ghosts(collided), collided)
    has_rotor = jnp.sum(own_pick, axis=1)[:, None, None]
    loads_out = own_loads * has_rotor
    filt_out = filtered * has_rotor
    return (populations, loads_out[None, None], filt_out[None, None])


def solution(mesh):
    in_specs = (
        P(None, None, "gx", "gy"),
        P(),
        P(),
        P(),
        P("gx", "gy", None, None),
        P("gx", "gy", None, None),
        P("gx", "gy", None, None),
        P("gx", "gy", None, None),
        P("gx", "gy", None, None, None),
    )
    out_specs = (
        P(None, None, "gx", "gy"),
        P("gx", "gy", None, None, None),
        P("gx", "gy", None, None, None),
    )
    return jax.shard_map(local, mesh=mesh, in_specs=in_specs, out_specs=out_specs, check_vma=False)
```

profile of v0, /device:TPU:0, one launch (start us, length us, event | category | flops | bytes accessed | tf_op | source)
XLA Modules:
  0.0 558.7 jit_solution(14589763447734236276)
XLA Ops:
  29.9 16.4 %fusion.64 = f32[8192,3]{0,1:T(4,128)S(1)} fusion(f32[3,16,128]{2,1,0:T(8,128)S(1)} %bitcast.761, f32[]{:T(128)} %bitcast.8, f32[8192]{0:T(1024)S(1)} %get-tuple-element.212, f32[8192]{0:T(1024)S(1)} %get-tuple-element.211, f32[8192]{0:T(1024)S(1)} %get-tuple-element.210, f32[8192]{0:T(1024)S(1)} %get-tuple-element.208, s32[8192]{0:T(1024)S(1)} %get-tuple-element.203, ...), kind=kOutput, calls=%fused_computation.114 | convolution fusion | flops 618373120 | bytes 811524 | tf_op jit(solution)/shard_map/dot_general | solution.py:91
  46.6 17.1 %fusion.67 = f32[8192,3]{0,1:T(4,128)S(1)} fusion(f32[3,16,128]{2,1,0:T(8,128)S(1)} %bitcast.755, f32[]{:T(128)} %bitcast.23, f32[8192]{0:T(1024)S(1)} %copy-done.147, f32[8192]{0:T(1024)S(1)} %copy-done.143, f32[8192]{0:T(1024)S(1)} %copy-done.139, f32[8192]{0:T(1024)S(1)} %get-tuple-element.197, s32[8192]{0:T(1024)S(1)} %get-tuple-element.192, ...), kind=kOutput, calls=%fused_computation.115 | convolution fusion | flops 618373120 | bytes 811524 | tf_op jit(solution)/shard_map/dot_general | solution.py:91
  64.1 16.4 %fusion.70 = f32[8192,3]{0,1:T(4,128)S(1)} fusion(f32[3,16,128]{2,1,0:T(8,128)S(1)} %bitcast.754, f32[]{:T(128)} %bitcast.34, f32[8192]{0:T(1024)S(1)} %copy-done.135, f32[8192]{0:T(1024)S(1)} %copy-done.131, f32[8192]{0:T(1024)S(1)} %get-tuple-element.188, f32[8192]{0:T(1024)S(1)} %get-tuple-element.186, s32[8192]{0:T(1024)S(1)} %get-tuple-element.181, ...), kind=kOutput, calls=%fused_computation.116 | convolution fusion | flops 618373120 | bytes 811524 | tf_op jit(solution)/shard_map/dot_general | solution.py:91
  80.9 16.5 %fusion.73 = f32[8192,3]{0,1:T(4,128)S(1)} fusion(f32[3,16,128]{2,1,0:T(8,128)S(1)} %bitcast.753, f32[]{:T(128)} %bitcast.45, f32[8192]{0:T(1024)S(1)} %get-tuple-element.179, f32[8192]{0:T(1024)S(1)} %get-tuple-element.178, f32[8192]{0:T(1024)S(1)} %get-tuple-element.177, f32[8192]{0:T(1024)S(1)} %get-tuple-element.175, s32[8192]{0:T(1024)S(1)} %get-tuple-element.170, ...), kind=kOutput, calls=%fused_computation.117 | convolution fusion | flops 618373120 | bytes 811524 | tf_op jit(solution)/shard_map/dot_general | solution.py:91
  97.8 16.5 %fusion.76 = f32[8192,3]{0,1:T(4,128)S(1)} fusion(f32[3,16,128]{2,1,0:T(8,128)S(1)} %bitcast.752, f32[]{:T(128)} %bitcast.56, f32[8192]{0:T(1024)S(1)} %copy-done.111, f32[8192]{0:T(1024)S(1)} %copy-done.107, f32[8192]{0:T(1024)S(1)} %copy-done.103, f32[8192]{0:T(1024)S(1)} %get-tuple-element.167, s32[8192]{0:T(1024)S(1)} %get-tuple-element.162, ...), kind=kOutput, calls=%fused_computation.118 | convolution fusion | flops 618373120 | bytes 811524 | tf_op jit(solution)/shard_map/dot_general | solution.py:91
  121.8 30.1 %all-reduce.5.cloned.1.call-done = f32[5,3,8192]{2,1,0:T(4,128)} async-done(((f32[5,3,8192]{2,1,0:T(4,128)}), f32[5,3,8192]{2,1,0:T(4,128)}) %all-reduce.5.cloned.1.call-update) | async-done | bytes 491536 | tf_op jit(solution)/shard_map/psum | solution.py:273
  160.9 31.9 %all-reduce.7.cloned.1.call-done = f32[5,3,8192]{2,1,0:T(4,128)} async-done(((f32[5,3,8192]{2,1,0:T(4,128)}), f32[5,3,8192]{2,1,0:T(4,128)}) %all-reduce.7.cloned.1.call-update) | async-done | bytes 491536 | tf_op jit(solution)/shard_map/psum | solution.py:285
  194.2 8.7 %fusion.94 = f32[3,16,128]{2,1,0:T(8,128)S(1)} fusion(f32[]{:T(128)} %bitcast.8, f32[8192]{0:T(1024)} %copy-done.100, f32[8192]{0:T(1024)} %copy-done.97, f32[8192]{0:T(1024)} %copy-done.94, f32[8192]{0:T(1024)S(1)} %copy-done.59, s32[8192]{0:T(1024)S(1)} %copy-done.55, s32[128]{0:T(128)S(1)} %copy-done.187, f32[8192,3]{0,1:T(4,128)S(1)} %get-tuple-element.126, ...), kind=kOutput, calls=%fused_computation.124 | convolution fusion | flops 618010624 | bytes 811524 | tf_op jit(solution)/shard_map/dot_general | solution.py:104
  203.0 7.9 %fusion.134 = f32[3,16,128]{2,1,0:T(8,128)S(1)} fusion(f32[]{:T(128)} %bitcast.56, f32[8192]{0:T(1024)S(1)} %copy-done.112, f32[8192]{0:T(1024)S(1)} %copy-done.108, f32[8192]{0:T(1024)S(1)} %copy-done.104, f32[8192]{0:T(1024)S(1)} %copy-done.91, s32[8192]{0:T(1024)S(1)} %copy-done.79, s32[128]{0:T(128)S(1)} %copy-done.187, ...), kind=kOutput, calls=%fused_computation.132 | convolution fusion | flops 618010624 | bytes 811524 | tf_op jit(solution)/shard_map/dot_general | solution.py:104
  211.0 8.0 %fusion.124 = f32[3,16,128]{2,1,0:T(8,128)S(1)} fusion(f32[]{:T(128)} %bitcast.45, f32[8192]{0:T(1024)S(1)} %copy-done.124, f32[8192]{0:T(1024)S(1)} %copy-done.120, f32[8192]{0:T(1024)S(1)} %copy-done.116, f32[8192]{0:T(1024)S(1)} %copy-done.87, s32[8192]{0:T(1024)S(1)} %copy-done.71, s32[128]{0:T(128)S(1)} %copy-done.187, ...), kind=kOutput, calls=%fused_computation.130 | convolution fusion | flops 618010624 | bytes 811524 | tf_op jit(solution)/shard_map/dot_general | solution.py:104
  219.0 8.3 %fusion.114 = f32[3,16,128]{2,1,0:T(8,128)S(1)} fusion(f32[]{:T(128)} %bitcast.34, f32[8192]{0:T(1024)S(1)} %copy-done.136, f32[8192]{0:T(1024)S(1)} %copy-done.132, f32[8192]{0:T(1024)S(1)} %copy-done.128, f32[8192]{0:T(1024)S(1)} %copy-done.83, s32[8192]{0:T(1024)S(1)} %copy-done.67, s32[128]{0:T(128)S(1)} %copy-done.187, ...), kind=kOutput, calls=%fused_computation.128 | convolution fusion | flops 618010624 | bytes 811524 | tf_op jit(solution)/shard_map/dot_general | solution.py:104
  227.5 7.9 %fusion.104 = f32[3,16,128]{2,1,0:T(8,128)S(1)} fusion(f32[]{:T(128)} %bitcast.23, f32[8192]{0:T(1024)S(1)} %copy-done.148, f32[8192]{0:T(1024)S(1)} %copy-done.144, f32[8192]{0:T(1024)S(1)} %copy-done.140, f32[8192]{0:T(1024)S(1)} %copy-done.75, s32[8192]{0:T(1024)S(1)} %copy-done.63, s32[128]{0:T(128)S(1)} %copy-done.187, ...), kind=kOutput, calls=%fused_computation.126 | convolution fusion | flops 618010624 | bytes 811524 | tf_op jit(solution)/shard_map/dot_general | solution.py:104
  292.0 16.4 %fusion.88 = f32[8192,3]{0,1:T(4,128)S(1)} fusion(f32[3,16,128]{2,1,0:T(8,128)S(1)} %bitcast.760, f32[]{:T(128)} %bitcast.45, f32[8192]{0:T(1024)S(1)} %copy-done.125, f32[8192]{0:T(1024)S(1)} %copy-done.121, f32[8192]{0:T(1024)S(1)} %copy-done.117, f32[8192]{0:T(1024)S(1)} %copy-done.88, s32[8192]{0:T(1024)S(1)} %copy-done.72, s32[128]{0:T(128)S(1)} %copy-done.188, ...), kind=kOutput, calls=%fused_computation.122 | convolution fusion | flops 618373120 | bytes 811524 | tf_op jit(solution)/shard_map/dot_general | solution.py:91
  308.6 16.4 %fusion.85 = f32[8192,3]{0,1:T(4,128)S(1)} fusion(f32[3,16,128]{2,1,0:T(8,128)S(1)} %bitcast.759, f32[]{:T(128)} %bitcast.34, f32[8192]{0:T(1024)S(1)} %copy-done.137, f32[8192]{0:T(1024)S(1)} %copy-done.133, f32[8192]{0:T(1024)S(1)} %copy-done.129, f32[8192]{0:T(1024)S(1)} %copy-done.84, s32[8192]{0:T(1024)S(1)} %copy-done.68, s32[128]{0:T(128)S(1)} %copy-done.188, ...), kind=kOutput, calls=%fused_computation.121 | convolution fusion | flops 618373120 | bytes 811524 | tf_op jit(solution)/shard_map/dot_general | solution.py:91
  325.2 16.4 %fusion.82 = f32[8192,3]{0,1:T(4,128)S(1)} fusion(f32[3,16,128]{2,1,0:T(8,128)S(1)} %bitcast.758, f32[]{:T(128)} %bitcast.23, f32[8192]{0:T(1024)S(1)} %copy-done.149, f32[8192]{0:T(1024)S(1)} %copy-done.145, f32[8192]{0:T(1024)S(1)} %copy-done.141, f32[8192]{0:T(1024)S(1)} %copy-done.76, s32[8192]{0:T(1024)S(1)} %copy-done.64, s32[128]{0:T(128)S(1)} %copy-done.188, ...), kind=kOutput, calls=%fused_computation.120 | convolution fusion | flops 618373120 | bytes 811524 | tf_op jit(solution)/shard_map/dot_general | solution.py:91
  341.6 16.4 %fusion.79 = f32[8192,3]{0,1:T(4,128)S(1)} fusion(f32[3,16,128]{2,1,0:T(8,128)S(1)} %bitcast.757, f32[]{:T(128)} %bitcast.8, f32[8192]{0:T(1024)S(1)} %copy-done.101, f32[8192]{0:T(1024)S(1)} %copy-done.98, f32[8192]{0:T(1024)S(1)} %copy-done.95, f32[8192]{0:T(1024)S(1)} %copy-done.60, s32[8192]{0:T(1024)S(1)} %copy-done.56, s32[128]{0:T(128)S(1)} %copy-done.188, ...), kind=kOutput, calls=%fused_computation.119 | convolution fusion | flops 618373120 | bytes 811524 | tf_op jit(solution)/shard_map/dot_general | solution.py:91
  358.1 16.3 %fusion.91 = f32[8192,3]{0,1:T(4,128)S(1)} fusion(f32[3,16,128]{2,1,0:T(8,128)S(1)} %bitcast.756, f32[]{:T(128)} %bitcast.56, f32[8192]{0:T(1024)S(1)} %copy-done.113, f32[8192]{0:T(1024)S(1)} %copy-done.109, f32[8192]{0:T(1024)S(1)} %copy-done.105, f32[8192]{0:T(1024)S(1)} %copy-done.92, s32[8192]{0:T(1024)S(1)} %copy-done.80, s32[128]{0:T(128)S(1)} %copy-done.188, ...), kind=kOutput, calls=%fused_computation.123 | convolution fusion | flops 618373120 | bytes 811524 | tf_op jit(solution)/shard_map/dot_general | solution.py:91
  376.2 31.6 %all-reduce.9.cloned.1.call-done = f32[5,3,8192]{2,1,0:T(4,128)} async-done(((f32[5,3,8192]{2,1,0:T(4,128)}), f32[5,3,8192]{2,1,0:T(4,128)}) %all-reduce.9.cloned.1.call-update) | async-done | bytes 491536 | tf_op jit(solution)/shard_map/psum | solution.py:273
  415.8 32.9 %all-reduce.11.cloned.1.call-done = f32[5,3,8192]{2,1,0:T(4,128)} async-done(((f32[5,3,8192]{2,1,0:T(4,128)}), f32[5,3,8192]{2,1,0:T(4,128)}) %all-reduce.11.cloned.1.call-update) | async-done | bytes 491536 | tf_op jit(solution)/shard_map/psum | solution.py:285
  450.0 7.9 %fusion.109 = f32[3,16,128]{2,1,0:T(8,128)S(1)} fusion(f32[]{:T(128)} %bitcast.23, f32[8192]{0:T(1024)S(1)} %copy-done.150, f32[8192]{0:T(1024)S(1)} %copy-done.146, f32[8192]{0:T(1024)S(1)} %copy-done.142, f32[8192]{0:T(1024)S(1)} %copy-done.77, s32[8192]{0:T(1024)S(1)} %copy-done.65, s32[128]{0:T(128)S(1)} %copy-done.189, ...), kind=kOutput, calls=%fused_computation.127 | convolution fusion | flops 618010624 | bytes 811524 | tf_op jit(solution)/shard_map/dot_general | solution.py:104
  458.1 8.0 %fusion.119 = f32[3,16,128]{2,1,0:T(8,128)S(1)} fusion(f32[]{:T(128)} %bitcast.34, f32[8192]{0:T(1024)S(1)} %copy-done.138, f32[8192]{0:T(1024)S(1)} %copy-done.134, f32[8192]{0:T(1024)S(1)} %copy-done.130, f32[8192]{0:T(1024)S(1)} %copy-done.85, s32[8192]{0:T(1024)S(1)} %copy-done.69, s32[128]{0:T(128)S(1)} %copy-done.189, ...), kind=kOutput, calls=%fused_computation.129 | convolution fusion | flops 618010624 | bytes 811524 | tf_op jit(solution)/shard_map/dot_general | solution.py:104
  466.1 8.1 %fusion.129 = f32[3,16,128]{2,1,0:T(8,128)S(1)} fusion(f32[]{:T(128)} %bitcast.45, f32[8192]{0:T(1024)S(1)} %copy-done.126, f32[8192]{0:T(1024)S(1)} %copy-done.122, f32[8192]{0:T(1024)S(1)} %copy-done.118, f32[8192]{0:T(1024)S(1)} %copy-done.89, s32[8192]{0:T(1024)S(1)} %copy-done.73, s32[128]{0:T(128)S(1)} %copy-done.189, ...), kind=kOutput, calls=%fused_computation.131 | convolution fusion | flops 618010624 | bytes 811524 | tf_op jit(solution)/shard_map/dot_general | solution.py:104
  474.4 7.9 %fusion.139 = f32[3,16,128]{2,1,0:T(8,128)S(1)} fusion(f32[]{:T(128)} %bitcast.56, f32[8192]{0:T(1024)S(1)} %copy-done.114, f32[8192]{0:T(1024)S(1)} %copy-done.110, f32[8192]{0:T(1024)S(1)} %copy-done.106, f32[8192]{0:T(1024)S(1)} %copy-done.93, s32[8192]{0:T(1024)S(1)} %copy-done.81, s32[128]{0:T(128)S(1)} %copy-done.189, ...), kind=kOutput, calls=%fused_computation.133 | convolution fusion | flops 618010624 | bytes 811524 | tf_op jit(solution)/shard_map/dot_general | solution.py:104
  482.4 8.1 %fusion.99 = f32[3,16,128]{2,1,0:T(8,128)S(1)} fusion(f32[]{:T(128)} %bitcast.8, f32[8192]{0:T(1024)S(1)} %copy-done.102, f32[8192]{0:T(1024)S(1)} %copy-done.99, f32[8192]{0:T(1024)S(1)} %copy-done.96, f32[8192]{0:T(1024)S(1)} %copy-done.61, s32[8192]{0:T(1024)S(1)} %copy-done.57, s32[128]{0:T(128)S(1)} %copy-done.189, ...), kind=kOutput, calls=%fused_computation.125 | convolution fusion | flops 618010624 | bytes 811524 | tf_op jit(solution)/shard_map/dot_general | solution.py:104
  (561 shorter events, 159.6 us)
Async XLA Ops:
  7.2 144.7 %all-reduce.5.cloned.1.call-start = ((), (), s32[]{:S(2)}) async-start(), calls=%async_computation | async-start | bytes 1310720 | tf_op jit(solution)/shard_map/psum | solution.py:273
  11.0 105.9 %copy-start.161 = (pred[5]{0:T(512)(128)(4,1)}, pred[5]{0:T(512)(128)(4,1)S(1)}, u32[]{:S(2)}) copy-start(pred[5]{0:T(512)(128)(4,1)S(1)} %get-tuple-element.66) | copy-start | bytes 19
  20.3 77.4 %copy-start.78 = (s32[8192]{0:T(1024)}, s32[8192]{0:T(1024)S(1)}, u32[]{:S(2)}) copy-start(s32[8192]{0:T(1024)S(1)} %get-tuple-element.162) | copy-start | bytes 98308
  20.5 77.2 %copy-start.90 = (f32[8192]{0:T(1024)}, f32[8192]{0:T(1024)S(1)}, u32[]{:S(2)}) copy-start(f32[8192]{0:T(1024)S(1)} %get-tuple-element.167) | copy-start | bytes 98308
  29.7 164.4 %copy-start.28 = (f32[8192,16]{0,1:T(8,128)}, f32[8192,16]{0,1:T(8,128)S(1)}, u32[]{:S(2)}) copy-start(f32[8192,16]{0,1:T(8,128)S(1)} %select_add_fusion.4) | copy-start | bytes 1572868
  46.5 180.8 %copy-start.30 = (f32[8192,16]{0,1:T(8,128)}, f32[8192,16]{0,1:T(8,128)S(1)}, u32[]{:S(2)}) copy-start(f32[8192,16]{0,1:T(8,128)S(1)} %select_add_fusion.3) | copy-start | bytes 1572868
  114.4 79.7 %copy-start.55 = (s32[8192]{0:T(1024)S(1)}, s32[8192]{0:T(1024)}, u32[]{:S(2)}) copy-start(s32[8192]{0:T(1024)} %copy-done.54) | copy-start | bytes 98308
  114.4 79.7 %copy-start.59 = (f32[8192]{0:T(1024)S(1)}, f32[8192]{0:T(1024)}, u32[]{:S(2)}) copy-start(f32[8192]{0:T(1024)} %copy-done.58) | copy-start | bytes 98308
  114.4 79.7 %copy-start.187 = (s32[128]{0:T(128)S(1)}, s32[128]{0:T(128)}, u32[]{:S(2)}) copy-start(s32[128]{0:T(128)} %copy-done.185) | copy-start | bytes 1540
  115.2 77.6 %all-reduce.7.cloned.1.call-start = ((), (), s32[]{:S(2)}) async-start(), calls=%async_computation.1 | async-start | bytes 1310720 | tf_op jit(solution)/shard_map/psum | solution.py:285
  116.9 118.5 %copy-start.169 = (f32[16]{0:T(128)}, f32[16]{0:T(128)S(1)}, u32[]{:S(2)}) copy-start(f32[16]{0:T(128)S(1)} %compare_convert_fusion.1) | copy-start | bytes 196
  120.8 114.6 %copy-start.171 = (f32[16]{0:T(128)}, f32[16]{0:T(128)S(1)}, u32[]{:S(2)}) copy-start(f32[16]{0:T(128)S(1)} %compare_convert_fusion) | copy-start | bytes 196
  158.9 248.9 %all-reduce.9.cloned.1.call-start = ((), (), s32[]{:S(2)}) async-start(), calls=%async_computation.2 | async-start | bytes 1310720 | tf_op jit(solution)/shard_map/psum | solution.py:273
  159.6 75.8 %copy-start.173 = (f32[16]{0:T(128)}, f32[16]{0:T(128)S(1)}, u32[]{:S(2)}) copy-start(f32[16]{0:T(128)S(1)} %compare_convert_fusion.2) | copy-start | bytes 196
  160.2 75.2 %copy-start.175 = (f32[16]{0:T(128)}, f32[16]{0:T(128)S(1)}, u32[]{:S(2)}) copy-start(f32[16]{0:T(128)S(1)} %compare_convert_fusion.3) | copy-start | bytes 196
  240.5 7.0 %collective-permute-start.1 = (f32[19,16,1,128]{3,2,1,0:T(1,128)S(1)}, f32[19,16,1,128]{3,2,1,0:T(1,128)S(1)}, u32[]{:S(2)}, u32[]{:S(2)}) collective-permute-start(f32[19,16,1,128]{3,2,1,0:T(1,128)S(1)} %get-tuple-element.119), channel_id=1, source_target_pairs={{4,0},{8,4},{12,8},{16,12},{20,16},{24,20},{28,24},{0,28},{5,1},{9... | collective-permute-start | bytes 466952 | tf_op jit(solution)/shard_map/ppermute | solution.py:52
  244.8 8.1 %collective-permute-start = (f32[19,16,1,128]{3,2,1,0:T(1,128)S(1)}, f32[19,16,1,128]{3,2,1,0:T(1,128)S(1)}, u32[]{:S(2)}, u32[]{:S(2)}) collective-permute-start(f32[19,16,1,128]{3,2,1,0:T(1,128)S(1)} %get-tuple-element.120), channel_id=1, source_target_pairs={{0,4},{4,8},{8,12},{12,16},{16,20},{20,24},{24,28},{28,0},{1,5},{5... | collective-permute-start | bytes 466952 | tf_op jit(solution)/shard_map/ppermute | solution.py:49
  266.2 10.5 %collective-permute-start.2 = (f32[19,16,18,1]{0,1,3,2:T(8,128)}, f32[19,16,18,1]{0,1,3,2:T(8,128)}, u32[]{:S(2)}, u32[]{:S(2)}) collective-permute-start(f32[19,16,18,1]{0,1,3,2:T(8,128)} %copy.173), channel_id=1, source_target_pairs={{0,1},{1,2},{2,3},{3,0},{4,5},{5,6},{6,7},{7,4},{8,9},{9,10},{10,1... | collective-permute-start | bytes 65672 | tf_op jit(solution)/shard_map/ppermute | solution.py:49
  266.2 4.7 collective-permute-start.3
  375.6 73.0 %all-reduce.11.cloned.1.call-start = ((), (), s32[]{:S(2)}) async-start(), calls=%async_computation.3 | async-start | bytes 1310720 | tf_op jit(solution)/shard_map/psum | solution.py:285
  495.9 7.0 %collective-permute-start.5 = (f32[19,16,1,128]{3,2,1,0:T(1,128)S(1)}, f32[19,16,1,128]{3,2,1,0:T(1,128)S(1)}, u32[]{:S(2)}, u32[]{:S(2)}) collective-permute-start(f32[19,16,1,128]{3,2,1,0:T(1,128)S(1)} %get-tuple-element.104), channel_id=1, source_target_pairs={{4,0},{8,4},{12,8},{16,12},{20,16},{24,20},{28,24},{0,28},{5,1},{9... | collective-permute-start | bytes 466952 | tf_op jit(solution)/shard_map/ppermute | solution.py:52
  500.1 7.9 %collective-permute-start.4 = (f32[19,16,1,128]{3,2,1,0:T(1,128)S(1)}, f32[19,16,1,128]{3,2,1,0:T(1,128)S(1)}, u32[]{:S(2)}, u32[]{:S(2)}) collective-permute-start(f32[19,16,1,128]{3,2,1,0:T(1,128)S(1)} %get-tuple-element.105), channel_id=1, source_target_pairs={{0,4},{4,8},{8,12},{12,16},{16,20},{20,24},{24,28},{28,0},{1,5},{5... | collective-permute-start | bytes 466952 | tf_op jit(solution)/shard_map/ppermute | solution.py:49
  520.7 10.5 %collective-permute-start.6 = (f32[19,16,18,1]{0,1,3,2:T(8,128)S(1)}, f32[19,16,18,1]{0,1,3,2:T(8,128)}, u32[]{:S(2)}, u32[]{:S(2)}) collective-permute-start(f32[19,16,18,1]{0,1,3,2:T(8,128)S(1)} %copy.177), channel_id=1, source_target_pairs={{0,1},{1,2},{2,3},{3,0},{4,5},{5,6},{6,7},{7,4},{8,9},{9,10},{10,1... | collective-permute-start | bytes 65672 | tf_op jit(solution)/shard_map/ppermute | solution.py:49
  520.8 4.7 collective-permute-start.7
  (178 other events, 3086.6 us)
Sparse Core Ops, SparseCore 0:
  115.4 36.5 all-reduce.4
  159.0 33.7 all-reduce.6
  375.7 32.0 all-reduce.8
  414.8 33.7 all-reduce.10
where the time goes:
time: 568 us; the launch traced here: 559 us
  matrix products  245 us (43%)
  waiting for transfers between devices  144 us (25%)
  local copies, waits for them, and re-layouts  70.1 us (12%)
  other arithmetic  59 us (10%)
  between operations  27.2 us (5%)
  starting transfers between devices  12.9 us (2%)
    dot_general x10, matrix products, sample_section(): jnp.dot(across, flattened, precision=lax.Precision.HIGHEST, preferred_ele...  165 us
    dot_general x10, matrix products, spread_section(): lax.dot_general(weighted, across, (((0,), (0,)), ((), ())), precision=lax...  80.6 us
    psum x2, waiting for transfers between devices, local(): load_rows = lax.psum(row_loads, 'gy')  64.8 us
    psum x2, waiting for transfers between devices, local(): sampled = lax.psum(samples, 'gy')  61.6 us
    unnamed x34, other arithmetic  19.7 us
    slice x6, local copies, waits for them, and re-layouts, extended(): lax.slice_in_dim(block, 0, width, axis=dim)  17.6 us
    ppermute x4, starting transfers between devices, extended(): lax.ppermute(lax.slice_in_dim(block, 0, width, axis=dim), axis, backward)  11.9 us
    ppermute x2, local copies, waits for them, and re-layouts, extended(): lax.ppermute(lax.slice_in_dim(block, block.shape[dim] - width, None, axis...  11.5 us
  transfers between devices with their start and end apart: 12, of which 10 were waited for; matrix products, arithmetic and copies ran while one was open for 4% of the time, Pallas kernels for 0%

commit v1 on v0

v1 whole, which is shorter than its diff:
```python
import math

import jax
import jax.numpy as jnp
from jax import lax
from jax.experimental import pallas as pl
from jax.experimental.pallas import tpu as pltpu
from jax.sharding import PartitionSpec as P

PHASES = 64
PAIRS = [
    (1, 0, 0),
    (0, 1, 0),
    (0, 0, 1),
    (1, 1, 0),
    (1, -1, 0),
    (1, 0, 1),
    (1, 0, -1),
    (0, 1, 1),
    (0, 1, -1),
]
DIRS = [(0, 0, 0)]
for along in PAIRS:
    DIRS.append(along)
    DIRS.append(tuple(-part for part in along))
OPPOSITE = [0] + [q + 1 if q % 2 else q - 1 for q in range(1, 19)]
PLUS = [q for q in range(19) if DIRS[q][0] == 1]
MINUS = [q for q in range(19) if DIRS[q][0] == -1]
SIDEWAYS = [q for q in range(19) if DIRS[q][1] != 0]
OMEGA = 1.0 / 0.6
KEEP = 1.0 - OMEGA
GUO = 1.0 - 0.5 * OMEGA
SPREAD = 0.01
MIX = 0.5
PITCH_AMP = 0.2
LANES = 128
F32 = jnp.float32
BF16 = jnp.bfloat16
VMEM_LIMIT = 8 * 1024 * 1024


def iota(shape, axis):
    return lax.broadcasted_iota(jnp.int32, shape, axis)


def aligned(value, by):
    return value if isinstance(value, int) else pl.multiple_of(value, by)


def wrapped(value):
    return value % LANES if isinstance(value, int) else lax.rem(value, LANES)


def moments(f):
    sums = [f[2 * k + 1] + f[2 * k + 2] for k in range(9)]
    gaps = [f[2 * k + 1] - f[2 * k + 2] for k in range(9)]
    density = f[0]
    for part in sums:
        density = density + part
    momentum = []
    for axis in range(3):
        total = None
        for k in range(9):
            sign = PAIRS[k][axis]
            if sign == 0:
                continue
            if total is None:
                total = gaps[k]
            else:
                total = total + gaps[k] if sign > 0 else total - gaps[k]
        momentum.append(total)
    return density, momentum


def collide(f, force, wanted):
    density, momentum = moments(f)
    inverse = 1.0 / density
    v = [(momentum[a] + 0.5 * force[a]) * inverse for a in range(3)]
    relaxed = OMEGA * density
    square = v[0] * v[0] + v[1] * v[1] + v[2] * v[2]
    work = v[0] * force[0] + v[1] * force[1] + v[2] * force[2]
    base = relaxed * (1.0 - 1.5 * square) - (3.0 * GUO) * work
    drive = [relaxed * v[a] + GUO * force[a] for a in range(3)]
    bend = [(4.5 * relaxed) * v[a] + (9.0 * GUO) * force[a] for a in range(3)]
    post = {}
    if 0 in wanted:
        post[0] = KEEP * f[0] + base * (1.0 / 3.0)
    scaled = {}
    for weight in (18.0, 36.0):
        scaled[weight] = (
            base * (1.0 / weight),
            [part * (3.0 / weight) for part in drive],
            [part * (1.0 / weight) for part in bend],
        )

    def along(k, parts):
        total = None
        for axis in range(3):
            sign = PAIRS[k][axis]
            if sign == 0:
                continue
            if total is None:
                total = parts[axis]
            else:
                total = total + parts[axis] if sign > 0 else total - parts[axis]
        return total

    for k in range(9):
        if 2 * k + 1 not in wanted and 2 * k + 2 not in wanted:
            continue
        level, drives, bends = scaled[18.0 if k < 3 else 36.0]
        even = level + along(k, v) * along(k, bends)
        odd = along(k, drives)
        if 2 * k + 1 in wanted:
            post[2 * k + 1] = KEEP * f[2 * k + 1] + (even + odd)
        if 2 * k + 2 in wanted:
            post[2 * k + 2] = KEEP * f[2 * k + 2] + (even - odd)
    return post


def outside(q, levels, rows):
    if DIRS[q][2] == 1:
        return rows == 0
    if DIRS[q][2] == -1:
        return rows == levels - 1
    return None


class Shape:
    def __init__(self, f_in, rotor_place, marker_cell, pitch_phase, filt_in):
        self.levels = f_in.shape[1]
        self.xs = f_in.shape[2]
        self.rotors = rotor_place.shape[0]
        self.steps = pitch_phase.shape[1]
        self.markers = marker_cell.shape[1]
        self.slots = filt_in.shape[2]
        self.tiles = lax.axis_size("gy")
        self.groups = self.markers // LANES
        self.section = self.slots * 3 * self.levels


def in_vmem(x):
    return pltpu.with_memory_space_constraint(x, pltpu.VMEM)


def in_smem(x):
    return pltpu.with_memory_space_constraint(x, pltpu.SMEM)


VM = pl.BlockSpec(memory_space=pltpu.VMEM)
SM = pl.BlockSpec(memory_space=pltpu.SMEM)
HB = pl.BlockSpec(memory_space=pl.ANY)
PARAMS = pltpu.CompilerParams(vmem_limit_bytes=VMEM_LIMIT)


def plan_kernel(sh, place, plan, count):
    row = lax.axis_index("gx")
    me = lax.axis_index("gy")
    for k in range(sh.tiles * sh.slots + sh.slots):
        plan[k] = -1
    for k in range(sh.tiles):
        count[k] = 0

    def visit(rotor, carry):
        @pl.when(place[rotor, 0] == row)
        def _():
            owner = place[rotor, 2]
            slot = count[owner]
            count[owner] = slot + 1
            plan[owner * sh.slots + slot] = place[rotor, 1]

            @pl.when(owner == me)
            def _():
                plan[sh.tiles * sh.slots + slot] = rotor

        return carry

    lax.fori_loop(0, sh.rotors, visit, 0)


def make_plan(sh, rotor_place):
    size = sh.tiles * sh.slots + sh.slots
    return pl.pallas_call(
        lambda *refs: plan_kernel(sh, *refs),
        out_shape=pltpu.SMEM((size,), jnp.int32),
        in_specs=[SM],
        out_specs=SM,
        scratch_shapes=[pltpu.SMEM((sh.tiles,), jnp.int32)],
        name="plan",
    )(rotor_place)


def plane_of(sh, f, x, low, high):
    rows = iota((sh.levels, LANES), 0)
    planes = []
    for q in range(19):
        value = f[q, pl.ds(x, sh.levels, stride=sh.xs), :]
        if low is not None and DIRS[q][0] != 0:
            if DIRS[q][0] == 1:
                other, at = low[PLUS.index(q)], 0
            else:
                other, at = high[MINUS.index(q)], sh.xs - 1
            here = jnp.asarray(x == at)
            skip = outside(q, sh.levels, rows)
            use = here if skip is None else jnp.logical_and(here, jnp.logical_not(skip))
            value = jnp.where(use, other, value)
        planes.append(value)
    return planes


def pre_kernel(sh, has_edges, *refs):
    plan, f = refs[:2]
    low, high = refs[2:4] if has_edges else (None, None)
    outs = refs[4:] if has_edges else refs[2:]
    me = lax.axis_index("gy")
    for shift in range(sh.tiles):
        owner = lax.rem(me + shift, sh.tiles)
        for slot in range(sh.slots):
            x = plan[owner * sh.slots + slot]

            @pl.when(x >= 0)
            def _():
                planes = plane_of(sh, f, x, low, high)
                density, momentum = moments(planes)
                inverse = 1.0 / density
                for axis in range(3):
                    at = (slot * 3 + axis) * sh.levels
                    outs[shift][at : at + sh.levels, :] = momentum[axis] * inverse

            @pl.when(x < 0)
            def _():
                at = slot * 3 * sh.levels
                outs[shift][at : at + 3 * sh.levels, :] = jnp.zeros((3 * sh.levels, LANES), F32)


def make_sections(sh, plan, f, edges):
    return pl.pallas_call(
        lambda *refs: pre_kernel(sh, bool(edges), *refs),
        out_shape=[pltpu.VMEM((sh.section, LANES), F32)] * sh.tiles,
        in_specs=[SM] + [VM] * (1 + len(edges)),
        out_specs=[VM] * sh.tiles,
        compiler_params=PARAMS,
        name="sections",
    )(plan, f, *edges)


def column_kernel(sh, has_edges, *refs):
    f = refs[0]
    low, high = refs[1:3] if has_edges else (None, None)
    outs = refs[-2:]
    lanes = iota((sh.xs, LANES), 1)
    xrows = iota((sh.xs, LANES), 0)
    per = LANES // sh.levels
    groups = (19 + per - 1) // per
    for side, edge in ((0, 0), (1, LANES - 1)):
        for group in range(groups):
            total = jnp.zeros((sh.xs, LANES), F32)
            for q in range(group * per, min(19, (group + 1) * per)):
                for z in range(sh.levels):
                    tile = f[q, z * sh.xs : (z + 1) * sh.xs, :]
                    if has_edges and DIRS[q][0] != 0:
                        blocked = (DIRS[q][2] == 1 and z == 0) or (
                            DIRS[q][2] == -1 and z == sh.levels - 1
                        )
                        if not blocked:
                            if DIRS[q][0] == 1:
                                tile = jnp.where(xrows == 0, low[PLUS.index(q), z : z + 1, :], tile)
                            else:
                                tile = jnp.where(
                                    xrows == sh.xs - 1, high[MINUS.index(q), z : z + 1, :], tile
                                )
                    column = jnp.broadcast_to(tile[:, edge : edge + 1], (sh.xs, LANES))
                    total = jnp.where(lanes == (q % per) * sh.levels + z, column, total)
            outs[side][group * sh.xs : (group + 1) * sh.xs, :] = total
    zlanes = iota((sh.levels, LANES), 1)
    at = groups * sh.xs
    corners = [jnp.zeros((sh.levels, LANES), F32) for side in range(2)]
    for which, x in ((0, 0), (1, sh.xs - 1)):
        planes = plane_of(sh, f, x, low, high)
        for q in range(19):
            for side, edge in ((0, 0), (1, LANES - 1)):
                column = jnp.broadcast_to(planes[q][:, edge : edge + 1], (sh.levels, LANES))
                corners[side] = jnp.where(zlanes == 2 * q + which, column, corners[side])
    for side in range(2):
        outs[side][at : at + sh.levels, :] = corners[side]


def make_columns(sh, f, edges):
    per = LANES // sh.levels
    groups = (19 + per - 1) // per
    rows = groups * sh.xs + sh.levels
    return pl.pallas_call(
        lambda *refs: column_kernel(sh, bool(edges), *refs),
        out_shape=[pltpu.VMEM((rows, LANES), F32)] * 2,
        in_specs=[VM] * (1 + len(edges)),
        out_specs=[VM] * 2,
        compiler_params=PARAMS,
        name="columns",
    )(f, *edges)


def peskin(offsets):
    distance = jnp.abs(offsets)
    near_arg = jnp.maximum(1.0 + 4.0 * distance - 4.0 * distance * distance, 1.0)
    far_arg = jnp.maximum(-7.0 + 12.0 * distance - 4.0 * distance * distance, 1.0)
    near = distance <= 1.0
    root = jnp.sqrt(jnp.where(near, near_arg, far_arg))
    return (jnp.where(near, 3.0, 5.0) - 2.0 * distance + jnp.where(near, root, -root)) * 0.125


TABLE_CHUNK = 256


def table_kernel(sh, plan, cells, across, upward, info, codes, sem):
    ids = [plan[sh.tiles * sh.slots + slot] for slot in range(sh.slots)]
    copies = []
    for slot in range(sh.slots):
        first = pl.multiple_of(jnp.maximum(ids[slot], 0) // 8 * 8, 8)
        copy = pltpu.make_async_copy(cells.at[pl.ds(first, 8), :], codes.at[slot], sem.at[slot])
        copy.start()
        copies.append(copy)
    width = TABLE_CHUNK
    corner = iota((8, width), 0)
    spanwise = corner < 4
    place = (corner % 4).astype(F32) - 1.0
    ycells = iota((LANES, width), 0).astype(F32).astype(BF16)
    zcells = iota((sh.levels, width), 0)
    zero = jnp.zeros((LANES, width), BF16)
    for slot in range(sh.slots):
        copies[slot].wait()

        @pl.when(ids[slot] >= 0)
        def _():
            row = ids[slot] % 8
            every = codes[slot, pl.ds(row, 1), :] // (64 * sh.levels)
            lowest = jnp.min(every)
            highest = jnp.max(every)
            narrow = highest - lowest + 4 <= LANES
            start = jnp.where(narrow, lowest, lowest // LANES * LANES)
            info[2 * slot] = start
            info[2 * slot + 1] = jnp.where(narrow, 1, 2)

            def chunk(window, at):
                code = codes[slot, pl.ds(row, 1), pl.ds(at, width)]
                cell = code // (64 * sh.levels) - start - window * LANES
                level = code // 64 % sh.levels
                eighths = jnp.where(spanwise, code // 8 % 8, code % 8)
                weights = peskin(place - eighths.astype(F32) * 0.125)
                top = weights.astype(BF16)
                rest = (weights - top.astype(F32)).astype(BF16)
                tall = jnp.zeros((sh.levels, width), F32)
                for j in range(4):
                    tall = jnp.where(zcells == level + j, weights[4 + j : 5 + j, :], tall)
                upward[slot, :, pl.ds(at, width)] = tall
                wide = [zero, zero]
                for j in range(4):
                    here = ycells == (cell + j).astype(F32).astype(BF16)
                    for part, source in ((0, top), (1, rest)):
                        wide[part] = jnp.where(here, source[j : j + 1, :], wide[part])
                for part in range(2):
                    across[slot, window, part * LANES : (part + 1) * LANES, pl.ds(at, width)] = wide[
                        part
                    ]

            def sweep(window):
                def body(i, carry):
                    chunk(window, pl.multiple_of(i * width, width))
                    return carry

                lax.fori_loop(0, sh.markers // width, body, 0)

            sweep(0)

            @pl.when(jnp.logical_not(narrow))
            def _():
                sweep(1)


def make_tables(sh, plan, marker_cell):
    return pl.pallas_call(
        lambda *refs: table_kernel(sh, *refs),
        out_shape=[
            pltpu.VMEM((sh.slots, 2, 2 * LANES, sh.markers), BF16),
            pltpu.VMEM((sh.slots, sh.levels, sh.markers), F32),
            pltpu.SMEM((2 * sh.slots,), jnp.int32),
        ],
        in_specs=[SM, HB],
        out_specs=[VM, VM, SM],
        scratch_shapes=[
            pltpu.VMEM((sh.slots, 8, sh.markers), jnp.int32),
            pltpu.SemaphoreType.DMA((sh.slots,)),
        ],
        compiler_params=PARAMS,
        name="tables",
    )(plan, marker_cell)


def blade_kernel(sh, plan, phases, area, twist, speed, angle, filt, blades, filtered):
    rows = sh.slots * sh.groups

    def dense(read, write):
        for slot in range(sh.slots):
            for group in range(sh.groups):
                write(slot * sh.groups + group, read(slot, group * LANES))

    def keep(k):
        def write(row, value):
            blades[k, row : row + 1, :] = value

        return write

    for k, source in ((0, area), (1, speed), (2, angle), (3, twist)):
        dense(lambda slot, at: source[slot : slot + 1, at : at + LANES], keep(k))
    for axis in range(3):

        def write(row, value):
            filtered[axis, row : row + 1, :] = value

        dense(lambda slot, at: filt[slot, axis : axis + 1, at : at + LANES], write)
    around = blades[2]
    turned = blades[3]
    blades[2] = jnp.sin(around)
    blades[3] = jnp.cos(around)
    sin_twist = jnp.sin(turned)
    cos_twist = jnp.cos(turned)
    owner = iota((rows, LANES), 0) // sh.groups
    for step in range(sh.steps):
        phase = jnp.zeros((rows, LANES), F32)
        for slot in range(sh.slots):
            rotor = jnp.maximum(plan[sh.tiles * sh.slots + slot], 0)
            phase = jnp.where(owner == slot, phases[rotor, step].astype(F32), phase)
        pitch = PITCH_AMP * jnp.sin((2.0 * math.pi / PHASES) * phase)
        sin_pitch = jnp.sin(pitch)
        cos_pitch = jnp.cos(pitch)
        blades[4 + 2 * step] = sin_twist * cos_pitch + cos_twist * sin_pitch
        blades[5 + 2 * step] = cos_twist * cos_pitch - sin_twist * sin_pitch


def make_blades(sh, plan, phases, area, twist, speed, angle, filt):
    rows = sh.slots * sh.groups
    return pl.pallas_call(
        lambda *refs: blade_kernel(sh, *refs),
        out_shape=[
            pltpu.VMEM((4 + 2 * sh.steps, rows, LANES), F32),
            pltpu.VMEM((3, rows, LANES), F32),
        ],
        in_specs=[SM, SM] + [VM] * 5,
        out_specs=[VM, VM],
        compiler_params=PARAMS,
        name="blades",
    )(plan, phases, area, twist, speed, angle, filt)


SAMPLE_CHUNK = 512
SPREAD_CHUNK = 1024


def split(value):
    top = value.astype(BF16)
    return top, (value - top.astype(F32)).astype(BF16)


def marker_kernel(sh, step, plan, info, across, upward, blades, filt_old, *refs):
    sections = refs[: sh.tiles]
    filt_new, loads = refs[sh.tiles : sh.tiles + 2]
    forces = refs[sh.tiles + 2 : 2 * sh.tiles + 2]
    around, sampled, weighted, spread = refs[2 * sh.tiles + 2 :]
    me = lax.axis_index("gy")
    tall = 3 * sh.levels
    for shift in range(sh.tiles):
        around[lax.rem(me + sh.tiles - shift, sh.tiles)] = sections[shift][...]
    spread[...] = jnp.zeros(spread.shape, F32)

    def window_of(slot, window):
        start = info[2 * slot] + window * LANES
        tile = start // LANES
        return tile, jnp.minimum(tile + 1, sh.tiles - 1), start - tile * LANES

    def windows(slot, body):
        @pl.when(plan[sh.tiles * sh.slots + slot] >= 0)
        def _():
            body(0)

            @pl.when(info[2 * slot + 1] > 1)
            def _():
                body(1)

    for slot in range(sh.slots):
        rows = pl.ds(slot * tall, tall)

        def sample(window):
            tile, after, offset = window_of(slot, window)
            both = jnp.concatenate([around[tile, rows, :], around[after, rows, :]], axis=1)
            seen = pltpu.roll(both, lax.rem(2 * LANES - offset, 2 * LANES), 1)[:, :LANES]
            top, rest = split(seen)
            left = jnp.concatenate([top, rest], axis=0)
            left = jnp.concatenate([left, left], axis=1)

            def chunk(i, carry):
                at = pl.multiple_of(i * SAMPLE_CHUNK, SAMPLE_CHUNK)
                value = jnp.dot(
                    left,
                    across[slot, window, :, pl.ds(at, SAMPLE_CHUNK)],
                    preferred_element_type=F32,
                )
                value = value[:tall] + value[tall:]
                heights = upward[slot, :, pl.ds(at, SAMPLE_CHUNK)]
                for axis in range(3):
                    part = jnp.sum(
                        value[axis * sh.levels : (axis + 1) * sh.levels] * heights,
                        axis=0,
                        keepdims=True,
                    )
                    for group in range(SAMPLE_CHUNK // LANES):
                        row = slot * sh.groups + i * (SAMPLE_CHUNK // LANES) + group
                        piece = part[:, group * LANES : (group + 1) * LANES]
                        if window:
                            piece = piece + sampled[axis, pl.ds(row, 1), :]
                        sampled[axis, pl.ds(row, 1), :] = piece
                return carry

            lax.fori_loop(0, sh.markers // SAMPLE_CHUNK, chunk, 0)

        windows(slot, sample)

    felt = []
    for axis in range(3):
        old = filt_old[axis]
        value = old + MIX * (sampled[axis] - old)
        filt_new[axis] = value
        felt.append(value)
    sin_t = blades[2]
    cos_t = blades[3]
    tangent = blades[1] + sin_t * felt[1] - cos_t * felt[2]
    square = felt[0] * felt[0] + tangent * tangent
    inverse = 1.0 / jnp.sqrt(square)
    sin_p = felt[0] * inverse
    cos_p = tangent * inverse
    sin_b = blades[4 + 2 * step]
    cos_b = blades[5 + 2 * step]
    sin_a = sin_p * cos_b - cos_p * sin_b
    cos_a = cos_p * cos_b + sin_p * sin_b
    lift = (2.0 * math.pi) * sin_a * cos_a
    drag = 0.02 + sin_a * sin_a
    dynamic = 0.5 * blades[0] * square
    around_axis = dynamic * (lift * sin_p - drag * cos_p)
    loads[0] = dynamic * (lift * cos_p + drag * sin_p)
    loads[1] = -around_axis * sin_t
    loads[2] = around_axis * cos_t

    for slot in range(sh.slots):
        rows = pl.ds(slot * tall, tall)

        def spread_out(window):
            tile, after, offset = window_of(slot, window)

            def chunk(i, total):
                at = pl.multiple_of(i * SPREAD_CHUNK, SPREAD_CHUNK)
                for group in range(SPREAD_CHUNK // LANES):
                    heights = upward[slot, :, pl.ds(at + group * LANES, LANES)]
                    row = slot * sh.groups + i * (SPREAD_CHUNK // LANES) + group
                    parts = [heights * loads[axis, pl.ds(row, 1), :] for axis in range(3)]
                    top, rest = split(jnp.concatenate(parts, axis=0))
                    weighted[:tall, group * LANES : (group + 1) * LANES] = top
                    weighted[tall:, group * LANES : (group + 1) * LANES] = rest
                return total + lax.dot_general(
                    weighted[...],
                    across[slot, window, :, pl.ds(at, SPREAD_CHUNK)],
                    (((1,), (1,)), ((), ())),
                    preferred_element_type=F32,
                )

            total = lax.fori_loop(
                0,
                sh.markers // SPREAD_CHUNK,
                chunk,
                jnp.zeros((2 * tall, 2 * LANES), F32),
            )
            total = total[:tall] + total[tall:]
            total = -SPREAD * (total[:, :LANES] + total[:, LANES:])
            both = jnp.concatenate([total, jnp.zeros((tall, LANES), F32)], axis=1)
            both = pltpu.roll(both, offset, 1)
            spread[tile, rows, :] = spread[tile, rows, :] + both[:, :LANES]
            spread[after, rows, :] = spread[after, rows, :] + both[:, LANES:]

        windows(slot, spread_out)

    lanes = iota((sh.levels, LANES), 1)
    for shift in range(sh.tiles):
        tile = lax.rem(me + shift, sh.tiles)
        forces[shift][: sh.section, :] = spread[tile]
        before = lax.rem(tile + sh.tiles - 1, sh.tiles)
        after = lax.rem(tile + 1, sh.tiles)
        ghosts = jnp.zeros((sh.levels, LANES), F32)
        for k in range(3 * sh.slots):
            at = pl.ds(k * sh.levels, sh.levels)
            left = jnp.broadcast_to(spread[before, at, :][:, LANES - 1 :], (sh.levels, LANES))
            right = jnp.broadcast_to(spread[after, at, :][:, :1], (sh.levels, LANES))
            ghosts = jnp.where(lanes == 2 * k, left, ghosts)
            ghosts = jnp.where(lanes == 2 * k + 1, right, ghosts)
        forces[shift][sh.section :, :] = ghosts


def do_markers(sh, step, plan, info, across, upward, blades, filt, sections):
    rows = sh.slots * sh.groups
    dense = pltpu.VMEM((3, rows, LANES), F32)
    force = pltpu.VMEM((sh.section + sh.levels, LANES), F32)
    out = pl.pallas_call(
        lambda *refs: marker_kernel(sh, step, *refs),
        out_shape=[dense, dense] + [force] * sh.tiles,
        in_specs=[SM, SM] + [VM] * (4 + sh.tiles),
        out_specs=[VM] * (2 + sh.tiles),
        scratch_shapes=[
            pltpu.VMEM((sh.tiles, sh.section, LANES), F32),
            pltpu.VMEM((3, rows, LANES), F32),
            pltpu.VMEM((6 * sh.levels, SPREAD_CHUNK), BF16),
            pltpu.VMEM((sh.tiles, sh.section, LANES), F32),
        ],
        compiler_params=PARAMS,
        name="markers",
    )(plan, info, across, upward, blades, filt, *sections)
    return out[0], out[1], out[2:]


def edge_kernel(sh, has_edges, plan, f, *refs):
    low, high = refs[:2] if has_edges else (None, None)
    refs = refs[2 * has_edges :]
    left, right = refs[:2]
    forces = refs[2 : 2 + sh.tiles]
    outs = refs[2 + sh.tiles :]
    me = lax.axis_index("gy")
    lanes = iota((sh.levels, LANES), 1)
    groups = (left.shape[0] - sh.levels) // sh.xs
    corner_rows = pl.ds(groups * sh.xs, sh.levels)
    blank = jnp.zeros((sh.levels, LANES), F32)
    planes_at = (0, sh.xs - 1)
    corner = []
    from_left = left[corner_rows, :]
    from_right = right[corner_rows, :]
    for q in range(19):
        a = pltpu.roll(from_left, (LANES - 2 * q) % LANES, 1)
        b = pltpu.roll(from_right, (LANES + 2 - 2 * q) % LANES, 1)
        corner.append(jnp.where(lanes < 2, a, jnp.where(lanes < 4, b, 1.0)))
    corner_force = [blank, blank, blank]
    edge_force = [[blank, blank, blank], [blank, blank, blank]]
    for shift in range(sh.tiles):
        owner = lax.rem(me + sh.tiles - shift, sh.tiles)
        ghosts = forces[shift][sh.section :, :]
        for slot in range(sh.slots):
            x = plan[owner * sh.slots + slot]
            for axis in range(3):
                k = slot * 3 + axis
                piece = forces[shift][k * sh.levels : (k + 1) * sh.levels, :]
                for which in range(2):
                    here = jnp.asarray(x == planes_at[which])
                    edge_force[which][axis] = edge_force[which][axis] + jnp.where(here, piece, 0.0)
                    for side in range(2):
                        lane = 2 * side + which
                        moved = pltpu.roll(ghosts, (lane - 2 * k - side) % LANES, 1)
                        corner_force[axis] = corner_force[axis] + jnp.where(
                            jnp.logical_and(here, lanes == lane), moved, 0.0
                        )
    corner_post = collide(corner, corner_force, [q for q in PLUS + MINUS if DIRS[q][1]])
    for which, wanted in ((1, PLUS), (0, MINUS)):
        planes = plane_of(sh, f, planes_at[which], low, high)
        post = collide(planes, edge_force[which], wanted)
        out = outs[0] if which else outs[1]
        for k, q in enumerate(wanted):
            value = post[q]
            if DIRS[q][1] == 1:
                value = pltpu.roll(value, 1, 1)
                ghost = pltpu.roll(corner_post[q], (LANES - which) % LANES, 1)
                value = jnp.where(lanes == 0, ghost, value)
            elif DIRS[q][1] == -1:
                value = pltpu.roll(value, LANES - 1, 1)
                ghost = pltpu.roll(corner_post[q], (LANES - 1 - 2 - which) % LANES, 1)
                value = jnp.where(lanes == LANES - 1, ghost, value)
            if DIRS[q][2]:
                value = pltpu.roll(value, DIRS[q][2] % sh.levels, 0)
            out[k] = value


def make_edges(sh, plan, f, edges, columns, forces):
    return pl.pallas_call(
        lambda *refs: edge_kernel(sh, bool(edges), *refs),
        out_shape=[pltpu.VMEM((len(PLUS), sh.levels, LANES), F32)] * 2,
        in_specs=[SM] + [VM] * (3 + len(edges) + sh.tiles),
        out_specs=[VM] * 2,
        compiler_params=PARAMS,
        name="edges",
    )(plan, f, *edges, *columns, *forces)


def collide_kernel(sh, has_edges, last, plan, f, *refs):
    low, high = refs[:2] if has_edges else (None, None)
    refs = refs[2 * has_edges :]
    left, right = refs[:2]
    forces = refs[2 : 2 + sh.tiles]
    out = refs[2 + sh.tiles]
    kept = refs[3 + sh.tiles] if last else None
    field, ghost_posts = refs[-2:]
    me = lax.axis_index("gy")
    xs = sh.xs
    lanes = iota((xs, LANES), 1)
    xrows = iota((xs, LANES), 0)
    per = LANES // sh.levels
    field[...] = jnp.zeros(field.shape, F32)
    ghost_force = [jnp.zeros((xs, LANES), F32) for axis in range(3)]
    for shift in range(sh.tiles):
        owner = lax.rem(me + sh.tiles - shift, sh.tiles)
        ghosts = jnp.transpose(
            jnp.concatenate(
                [
                    forces[shift][sh.section :, :],
                    jnp.zeros((LANES - sh.levels, LANES), F32),
                ],
                axis=0,
            )
        )
        for slot in range(sh.slots):
            x = plan[owner * sh.slots + slot]

            @pl.when(x >= 0)
            def _():
                for axis in range(3):
                    k = slot * 3 + axis
                    at = pl.ds(x, sh.levels, stride=xs)
                    field[axis, at, :] = (
                        field[axis, at, :] + forces[shift][k * sh.levels : (k + 1) * sh.levels, :]
                    )

            for axis in range(3):
                k = slot * 3 + axis
                far = pltpu.roll(ghosts[2 * k + 1 : 2 * k + 2, :], sh.levels, 1)
                piece = ghosts[2 * k : 2 * k + 1, :] + far
                ghost_force[axis] = ghost_force[axis] + jnp.where(xrows == x, piece, 0.0)

    ghost = []
    for q in range(19):
        at = pl.ds(q // per * xs, xs)
        shift = (q % per) * sh.levels
        a = pltpu.roll(left[at, :], (LANES - shift) % LANES, 1)
        b = pltpu.roll(right[at, :], (LANES + sh.levels - shift) % LANES, 1)
        ghost.append(
            jnp.where(lanes < sh.levels, a, jnp.where(lanes < 2 * sh.levels, b, 1.0))
        )
    posted = collide(ghost, ghost_force, SIDEWAYS)
    for k, q in enumerate(SIDEWAYS):
        ghost_posts[k] = posted[q]

    def level(z, bottom, top):
        at = aligned(z * xs, xs)
        here = []
        for q in range(19):
            tile = f[q, pl.ds(at, xs), :]
            if has_edges and DIRS[q][0] != 0:
                blocked = (DIRS[q][2] == 1 and bottom) or (DIRS[q][2] == -1 and top)
                if not blocked:
                    if DIRS[q][0] == 1:
                        tile = jnp.where(xrows == 0, low[PLUS.index(q), pl.ds(z, 1), :], tile)
                    else:
                        tile = jnp.where(
                            xrows == xs - 1, high[MINUS.index(q), pl.ds(z, 1), :], tile
                        )
            here.append(tile)
        force = [field[axis, pl.ds(at, xs), :] for axis in range(3)]
        post = collide(here, force, range(19))
        for q in range(19):
            dx, dy, dz = DIRS[q]
            value = post[q]
            if (dz == 1 and top) or (dz == -1 and bottom):
                to, target = OPPOSITE[q], z
            else:
                to, target = q, z + dz
                if dy == 1:
                    value = pltpu.roll(value, 1, 1)
                    other = pltpu.roll(
                        ghost_posts[SIDEWAYS.index(q)], wrapped(LANES - z), 1
                    )
                    value = jnp.where(lanes == 0, other, value)
                elif dy == -1:
                    value = pltpu.roll(value, LANES - 1, 1)
                    other = pltpu.roll(
                        ghost_posts[SIDEWAYS.index(q)], LANES - 1 - sh.levels - z, 1
                    )
                    value = jnp.where(lanes == LANES - 1, other, value)
                if dx:
                    value = pltpu.roll(value, dx % xs, 0)
            row = aligned(target * xs, xs)
            out[to, pl.ds(row, xs), :] = value
            if last and DIRS[to][0] == 1:
                kept[PLUS.index(to), pl.ds(target, 1)] = value[None, :8]
            if last and DIRS[to][0] == -1:
                kept[len(PLUS) + MINUS.index(to), pl.ds(target, 1)] = value[None, xs - 8 :]

    level(0, True, False)

    def middle(z, carry):
        level(z, False, False)
        return carry

    lax.fori_loop(1, sh.levels - 1, middle, 0)
    level(sh.levels - 1, False, True)


def do_collide(sh, last, plan, f, edges, columns, forces):
    shape = (19, sh.levels * sh.xs, LANES)
    if last:
        out_shape = [
            jax.ShapeDtypeStruct(shape, F32),
            pltpu.VMEM((2 * len(PLUS), sh.levels, 8, LANES), F32),
        ]
    else:
        out_shape = [pltpu.VMEM(shape, F32)]
    return pl.pallas_call(
        lambda *refs: collide_kernel(sh, bool(edges), last, *refs),
        out_shape=out_shape,
        in_specs=[SM] + [VM] * (3 + len(edges) + sh.tiles),
        out_specs=[VM] * len(out_shape),
        scratch_shapes=[
            pltpu.VMEM((3, sh.levels * sh.xs, LANES), F32),
            pltpu.VMEM((len(SIDEWAYS), sh.xs, LANES), F32),
        ],
        compiler_params=PARAMS,
        name="collide",
    )(plan, f, *edges, *columns, *forces)


def finish_kernel(sh, kept, low, high, f_old, f, merged, sem):
    del f_old
    rows = iota((8, LANES), 0)
    copies = []
    for side, dirs, edge in ((0, PLUS, low), (1, MINUS, high)):
        at_row = 0 if side == 0 else 7
        for k, q in enumerate(dirs):
            index = side * len(PLUS) + k
            for z in range(sh.levels):
                value = kept[index, z]
                blocked = (DIRS[q][2] == 1 and z == 0) or (
                    DIRS[q][2] == -1 and z == sh.levels - 1
                )
                if not blocked:
                    value = jnp.where(rows == at_row, edge[k, z : z + 1, :], value)
                merged[index, z] = value
            first = 0 if side == 0 else sh.xs - 8
            copy = pltpu.make_async_copy(
                merged.at[index], f.at[q, :, first : first + 8, :], sem.at[index]
            )
            copy.start()
            copies.append(copy)
    for copy in copies:
        copy.wait()


def finish(sh, f, kept, edges):
    f = f.reshape(19, sh.levels, sh.xs, LANES)
    return pl.pallas_call(
        lambda *refs: finish_kernel(sh, *refs),
        out_shape=jax.ShapeDtypeStruct(f.shape, F32),
        in_specs=[VM, VM, VM, HB],
        out_specs=HB,
        scratch_shapes=[
            pltpu.VMEM((2 * len(PLUS), sh.levels, 8, LANES), F32),
            pltpu.SemaphoreType.DMA((2 * len(PLUS),)),
        ],
        input_output_aliases={3: 0},
        compiler_params=PARAMS,
        name="finish",
    )(kept, *edges, f)


def output_kernel(sh, plan, loads, filt, loads_out, filt_out):
    for slot in range(sh.slots):
        used = plan[sh.tiles * sh.slots + slot] >= 0
        for source, target in ((loads, loads_out), (filt, filt_out)):
            for axis in range(3):
                for group in range(sh.groups):
                    row = slot * sh.groups + group
                    value = jnp.where(used, source[axis, row : row + 1, :], 0.0)
                    target[slot, axis : axis + 1, group * LANES : (group + 1) * LANES] = value


def make_outputs(sh, plan, loads, filt):
    shape = jax.ShapeDtypeStruct((sh.slots, 3, sh.markers), F32)
    return pl.pallas_call(
        lambda *refs: output_kernel(sh, *refs),
        out_shape=[shape, shape],
        in_specs=[SM, VM, VM],
        out_specs=[VM, VM],
        compiler_params=PARAMS,
        name="outputs",
    )(plan, loads, filt)


def shifted(x, axis, by):
    count = lax.axis_size(axis)
    return lax.ppermute(x, axis, [(i, (i + by) % count) for i in range(count)])


def local(
    f_in,
    rotor_place,
    marker_cell,
    pitch_phase,
    blade_area,
    blade_twist,
    blade_speed,
    blade_angle,
    filt_in,
):
    sh = Shape(f_in, rotor_place, marker_cell, pitch_phase, filt_in)
    f = in_vmem(f_in.reshape(19, sh.levels * sh.xs, LANES))
    plan = in_smem(make_plan(sh, rotor_place))
    edges = ()
    filt = None
    for step in range(sh.steps):
        last = step == sh.steps - 1
        sections = make_sections(sh, plan, f, edges)
        sections = [sections[0]] + [
            shifted(sections[by], "gy", by) for by in range(1, sh.tiles)
        ]
        columns = make_columns(sh, f, edges)
        columns = (shifted(columns[1], "gy", 1), shifted(columns[0], "gy", -1))
        if step == 0:
            across, upward, info = make_tables(sh, plan, marker_cell)
            across, upward, info = in_vmem(across), in_vmem(upward), in_smem(info)
            blades, filt = make_blades(
                sh,
                plan,
                pitch_phase,
                blade_area[0, 0],
                blade_twist[0, 0],
                blade_speed[0, 0],
                blade_angle[0, 0],
                filt_in[0, 0],
            )
            blades = in_vmem(blades)
        filt, loads, forces = do_markers(
            sh,
            step,
            plan,
            info,
            across,
            upward,
            blades,
            in_vmem(filt),
            [in_vmem(section) for section in sections],
        )
        forces = [forces[0]] + [shifted(forces[by], "gy", by) for by in range(1, sh.tiles)]
        forces = [in_vmem(force) for force in forces]
        columns = [in_vmem(column) for column in columns]
        sent = make_edges(sh, plan, f, edges, columns, forces)
        new_edges = (shifted(sent[0], "gx", 1), shifted(sent[1], "gx", -1))
        done = do_collide(sh, last, plan, f, edges, columns, forces)
        edges = tuple(in_vmem(edge) for edge in new_edges)
        if last:
            f = finish(sh, done[0], in_vmem(done[1]), edges)
        else:
            f = in_vmem(done[0])
    loads_out, filt_out = make_outputs(sh, plan, in_vmem(loads), in_vmem(filt))
    return f, loads_out[None, None], filt_out[None, None]


def solution(mesh):
    in_specs = (
        P(None, None, "gx", "gy"),
        P(),
        P(),
        P(),
        P("gx", "gy", None, None),
        P("gx", "gy", None, None),
        P("gx", "gy", None, None),
        P("gx", "gy", None, None),
        P("gx", "gy", None, None, None),
    )
    out_specs = (
        P(None, None, "gx", "gy"),
        P("gx", "gy", None, None, None),
        P("gx", "gy", None, None, None),
    )
    return jax.shard_map(local, mesh=mesh, in_specs=in_specs, out_specs=out_specs, check_vma=False)
```

time: 568 us -> 96.6 us (0.17); the launches traced: 559 us -> 96.1 us
  matrix products: 245 us -> 0 us
  waiting for transfers between devices: 144 us -> 5.68 us
  other arithmetic: 59 us -> 0.01 us
  local copies, waits for them, and re-layouts: 70.1 us -> 16.5 us
  starting transfers between devices: 12.9 us -> 53.6 us
  between operations: 27.2 us -> 0.92 us
  Pallas kernels: 0 us -> 19.3 us
    dot_general x20 -> x0, matrix products: 245 us -> none  [the longest x10 165 us: sample_section(): jnp.dot(across, flattened, precision=lax.Precision.HIGHEST, preferred_ele...]
    psum x4 -> x0, waiting for transfers between devices: 126 us -> none  [the longest x2 64.8 us: local(): load_rows = lax.psum(row_loads, 'gy')]
    ppermute x8 -> x20, starting transfers between devices: 12.2 us -> 53.6 us  [shifted(): return lax.ppermute(x, axis, [(i, (i + by) % count) for i in range(count)])]
    slice x14 -> x0, local copies, waits for them, and re-layouts: 28 us -> none  [the longest x6 17.6 us: extended(): lax.slice_in_dim(block, 0, width, axis=dim)]
    ppermute x4 -> x0, local copies, waits for them, and re-layouts: 23 us -> none  [the longest x2 11.5 us: extended(): lax.ppermute(lax.slice_in_dim(block, block.shape[dim] - width, None, axis...]
    unnamed x34 -> x1, other arithmetic: 19.7 us -> 0.01 us
    pallas_call x0 -> x15, Pallas kernels: none -> 19.3 us  [the longest x2 7.71 us: do_collide(): pl.pallas_call(lambda *refs: collide_kernel(sh, bool(edges), last, *refs)...]
    ppermute x8 -> x20, waiting for transfers between devices: 17.5 us -> 5.68 us  [shifted(): return lax.ppermute(x, axis, [(i, (i + by) % count) for i in range(count)])]
  transfers between devices with their start and end apart: 12 -> 20, of which waited for: 10 -> 4; matrix products, arithmetic and copies ran while one was open for 4% -> 2% of each run, Pallas kernels for 0% -> 14%
where the time goes in v1:
time: 96.6 us; the launch traced here: 96.1 us
  starting transfers between devices  53.6 us (55%)
  Pallas kernels  19.3 us (20%)
  local copies, waits for them, and re-layouts  16.5 us (17%)
  waiting for transfers between devices  5.68 us (6%)
    ppermute x20, starting transfers between devices, shifted(): return lax.ppermute(x, axis, [(i, (i + by) % count) for i in range(count)])  53.6 us
    unnamed x35, local copies, waits for them, and re-layouts  16.5 us
    pallas_call x2, Pallas kernels, do_collide(): pl.pallas_call(lambda *refs: collide_kernel(sh, bool(edges), last, *refs)...  7.71 us
    ppermute x20, waiting for transfers between devices, shifted(): return lax.ppermute(x, axis, [(i, (i + by) % count) for i in range(count)])  5.68 us
    pallas_call x2, Pallas kernels, make_columns(): pl.pallas_call(lambda *refs: column_kernel(sh, bool(edges), *refs), out_s...  3.21 us
  transfers between devices with their start and end apart: 20, of which 4 were waited for; matrix products, arithmetic and copies ran while one was open for 2% of the time, Pallas kernels for 14%

profile of v1, /device:TPU:0, one launch (start us, length us, event | category | flops | bytes accessed | tf_op | source)
XLA Modules:
  0.0 96.1 jit_solution(9568269423384088576)
XLA Ops:
  2.0 1.8 %plan.1.refs_0_ = s32[10]{0:T(128)S(4)} custom-call(s32[40,3]{1,0:T(8,128)} %copy.13.refs_0_), custom_call_target="tpu_custom_call" | custom-call | tf_op jit(solution)/shard_map/plan/pallas_call | solution.py:183
  3.8 1.7 %copy-done.2 = f32[19,16,16,128]{3,2,1,0:T(8,128)S(1)} copy-done((f32[19,16,16,128]{3,2,1,0:T(8,128)S(1)}, f32[19,16,16,128]{3,2,1,0:T(8,128)}, u32[]{:S(2)}) %copy-start.2) | copy-done | bytes 2490392
  6.6 2.6 %collective-permute-start.3 = (f32[96,128]{1,0:T(8,128)S(1)}, f32[96,128]{1,0:T(8,128)S(1)}, u32[]{:S(2)}, u32[]{:S(2)}) collective-permute-start(f32[96,128]{1,0:T(8,128)S(1)} %get-tuple-element.48), channel_id=1, source_target_pairs={{0,2},{1,3},{2,0},{3,1},{4,6},{5,7},{6,4},{7,5},{8,10},{9,11},{10,... | collective-permute-start | bytes 147464 | tf_op jit(solution)/shard_map/ppermute | solution.py:897
  9.2 1.4 %collective-permute-start.4 = (f32[96,128]{1,0:T(8,128)S(1)}, f32[96,128]{1,0:T(8,128)S(1)}, u32[]{:S(2)}, u32[]{:S(2)}) collective-permute-start(f32[96,128]{1,0:T(8,128)S(1)} %get-tuple-element.49), channel_id=1, source_target_pairs={{0,3},{1,0},{2,1},{3,2},{4,7},{5,4},{6,5},{7,6},{8,11},{9,8},{10,9... | collective-permute-start | bytes 147464 | tf_op jit(solution)/shard_map/ppermute | solution.py:897
  10.7 5.7 %copy-done = bf16[2,2,256,8192]{3,2,1,0:T(8,128)(2,1)} copy-done((bf16[2,2,256,8192]{3,2,1,0:T(8,128)(2,1)}, bf16[2,2,256,8192]{3,2,1,0:T(8,128)(2,1)S(1)}, u32[]{:S(2)}) %copy-start) | copy-done | bytes 16777240
  16.7 1.9 %blades.1 = (f32[8,128,128]{2,1,0:T(8,128)S(1)}, f32[3,128,128]{2,1,0:T(8,128)S(1)}) custom-call(s32[10]{0:T(128)S(4)} %plan.1.refs_0_, s32[40,2]{1,0:T(8,128)S(1)} %copy.15.refs_1_, f32[2,8192]{1,0:T(2,128)S(1)} %bitcast.20, f32[2,8192]{1,0:T(2,128)S(1)} %bitcast.21, f32[2,8192]{1,0:T(2,128)S(1)} %bitcast.22, f32[2,8192]{1,0:T(2,128)S(1)} %bitcast.23, ...), custom_call_target="tpu_custom_call" | custom-call | tf_op jit(solution)/shard_map/blades/pallas_call | solution.py:441
  18.6 5.8 %copy-done.1 = bf16[2,2,256,8192]{3,2,1,0:T(8,128)(2,1)S(1)} copy-done((bf16[2,2,256,8192]{3,2,1,0:T(8,128)(2,1)S(1)}, bf16[2,2,256,8192]{3,2,1,0:T(8,128)(2,1)}, u32[]{:S(2)}) %copy-start.1) | copy-done | bytes 16777240
  25.4 16.7 %collective-permute-start.5 = (f32[112,128]{1,0:T(8,128)S(1)}, f32[112,128]{1,0:T(8,128)S(1)}, u32[]{:S(2)}, u32[]{:S(2)}) collective-permute-start(f32[112,128]{1,0:T(8,128)S(1)} %get-tuple-element.51), channel_id=1, source_target_pairs={{0,1},{1,2},{2,3},{3,0},{4,5},{5,6},{6,7},{7,4},{8,9},{9,10},{10,1... | collective-permute-start | bytes 172040 | tf_op jit(solution)/shard_map/ppermute | solution.py:897
  43.3 1.4 %collective-permute-start.7 = (f32[112,128]{1,0:T(8,128)S(1)}, f32[112,128]{1,0:T(8,128)S(1)}, u32[]{:S(2)}, u32[]{:S(2)}) collective-permute-start(f32[112,128]{1,0:T(8,128)S(1)} %get-tuple-element.53), channel_id=1, source_target_pairs={{0,3},{1,0},{2,1},{3,2},{4,7},{5,4},{6,5},{7,6},{8,11},{9,8},{10,9... | collective-permute-start | bytes 172040 | tf_op jit(solution)/shard_map/ppermute | solution.py:897
  44.7 1.6 %columns.2 = (f32[64,128]{1,0:T(8,128)S(1)}, f32[64,128]{1,0:T(8,128)S(1)}) custom-call(f32[19,256,128]{2,1,0:T(8,128)S(1)} %bitcast.14), custom_call_target="tpu_custom_call" | custom-call | tf_op jit(solution)/shard_map/columns/pallas_call | solution.py:292
  46.3 1.7 %collective-permute-start.1 = (f32[64,128]{1,0:T(8,128)S(1)}, f32[64,128]{1,0:T(8,128)S(1)}, u32[]{:S(2)}, u32[]{:S(2)}) collective-permute-start(f32[64,128]{1,0:T(8,128)S(1)} %get-tuple-element.40), channel_id=1, source_target_pairs={{0,3},{1,0},{2,1},{3,2},{4,7},{5,4},{6,5},{7,6},{8,11},{9,8},{10,9... | collective-permute-start | bytes 98312 | tf_op jit(solution)/shard_map/ppermute | solution.py:897
  48.1 1.6 %collective-permute-done.refs_2_ = f32[64,128]{1,0:T(8,128)S(1)} collective-permute-done((f32[64,128]{1,0:T(8,128)S(1)}, f32[64,128]{1,0:T(8,128)S(1)}, u32[]{:S(2)}, u32[]{:S(2)}) %collective-permute-start) | collective-permute-done | bytes 32800 | tf_op jit(solution)/shard_map/ppermute | solution.py:897
  50.2 1.5 %collective-permute-start.8 = (f32[5,16,128]{2,1,0:T(8,128)S(1)}, f32[5,16,128]{2,1,0:T(8,128)S(1)}, u32[]{:S(2)}, u32[]{:S(2)}) collective-permute-start(f32[5,16,128]{2,1,0:T(8,128)S(1)} %get-tuple-element.54), channel_id=1, source_target_pairs={{0,4},{4,8},{8,12},{12,16},{16,20},{20,24},{24,28},{28,0},{1,5},{5... | collective-permute-start | bytes 122888 | tf_op jit(solution)/shard_map/ppermute | solution.py:897
  51.7 3.2 %collective-permute-start.9 = (f32[5,16,128]{2,1,0:T(8,128)S(1)}, f32[5,16,128]{2,1,0:T(8,128)S(1)}, u32[]{:S(2)}, u32[]{:S(2)}) collective-permute-start(f32[5,16,128]{2,1,0:T(8,128)S(1)} %get-tuple-element.55), channel_id=1, source_target_pairs={{0,28},{4,0},{8,4},{12,8},{16,12},{20,16},{24,20},{28,24},{1,29},{... | collective-permute-start | bytes 122888 | tf_op jit(solution)/shard_map/ppermute | solution.py:897
  54.9 3.1 %collide.2.refs_0_.refs_1_ = f32[19,256,128]{2,1,0:T(8,128)S(1)} custom-call(s32[10]{0:T(128)S(4)} %plan.1.refs_0_, f32[19,256,128]{2,1,0:T(8,128)S(1)} %bitcast.16, f32[64,128]{1,0:T(8,128)S(1)} %collective-permute-done.refs_2_, f32[64,128]{1,0:T(8,128)S(1)} %collective-permute-done.1.refs_3_, f32[112,128]{1,0:T(8,128)S(1)} %get-tuple-element.50.refs_4_, ...), custom_call_target="tpu_custom_call" | custom-call | tf_op jit(solution)/shard_map/collide/pallas_call | solution.py:815
  58.6 1.5 %collective-permute-start.12 = (f32[96,128]{1,0:T(8,128)S(1)}, f32[96,128]{1,0:T(8,128)S(1)}, u32[]{:S(2)}, u32[]{:S(2)}) collective-permute-start(f32[96,128]{1,0:T(8,128)S(1)} %get-tuple-element.60), channel_id=1, source_target_pairs={{0,1},{1,2},{2,3},{3,0},{4,5},{5,6},{6,7},{7,4},{8,9},{9,10},{10,1... | collective-permute-start | bytes 147464 | tf_op jit(solution)/shard_map/ppermute | solution.py:897
  62.2 2.0 %collective-permute-done.13.refs_8_ = f32[96,128]{1,0:T(8,128)S(1)} collective-permute-done((f32[96,128]{1,0:T(8,128)S(1)}, f32[96,128]{1,0:T(8,128)S(1)}, u32[]{:S(2)}, u32[]{:S(2)}) %collective-permute-start.13) | collective-permute-done | bytes 49184 | tf_op jit(solution)/shard_map/ppermute | solution.py:897
  64.6 11.9 %collective-permute-start.15 = (f32[112,128]{1,0:T(8,128)S(1)}, f32[112,128]{1,0:T(8,128)S(1)}, u32[]{:S(2)}, u32[]{:S(2)}) collective-permute-start(f32[112,128]{1,0:T(8,128)S(1)} %get-tuple-element.64), channel_id=1, source_target_pairs={{0,1},{1,2},{2,3},{3,0},{4,5},{5,6},{6,7},{7,4},{8,9},{9,10},{10,1... | collective-permute-start | bytes 172040 | tf_op jit(solution)/shard_map/ppermute | solution.py:897
  76.9 1.4 %collective-permute-start.17 = (f32[112,128]{1,0:T(8,128)S(1)}, f32[112,128]{1,0:T(8,128)S(1)}, u32[]{:S(2)}, u32[]{:S(2)}) collective-permute-start(f32[112,128]{1,0:T(8,128)S(1)} %get-tuple-element.66), channel_id=1, source_target_pairs={{0,3},{1,0},{2,1},{3,2},{4,7},{5,4},{6,5},{7,6},{8,11},{9,8},{10,9... | collective-permute-start | bytes 172040 | tf_op jit(solution)/shard_map/ppermute | solution.py:897
  78.3 1.6 %columns.3 = (f32[64,128]{1,0:T(8,128)S(1)}, f32[64,128]{1,0:T(8,128)S(1)}) custom-call(f32[19,256,128]{2,1,0:T(8,128)S(1)} %collide.2.refs_0_.refs_1_, f32[5,16,128]{2,1,0:T(8,128)S(1)} %collective-permute-done.8.refs_1_.refs_2_, f32[5,16,128]{2,1,0:T(8,128)S(1)} %collective-permute-done.9.refs_2_.refs_3_), custom_call_target="tpu_custom_call" | custom-call | tf_op jit(solution)/shard_map/columns/pallas_call | solution.py:292
  80.0 1.7 %collective-permute-start.11 = (f32[64,128]{1,0:T(8,128)S(1)}, f32[64,128]{1,0:T(8,128)S(1)}, u32[]{:S(2)}, u32[]{:S(2)}) collective-permute-start(f32[64,128]{1,0:T(8,128)S(1)} %get-tuple-element.57), channel_id=1, source_target_pairs={{0,3},{1,0},{2,1},{3,2},{4,7},{5,4},{6,5},{7,6},{8,11},{9,8},{10,9... | collective-permute-start | bytes 98312 | tf_op jit(solution)/shard_map/ppermute | solution.py:897
  81.7 1.6 %collective-permute-done.10.refs_4_ = f32[64,128]{1,0:T(8,128)S(1)} collective-permute-done((f32[64,128]{1,0:T(8,128)S(1)}, f32[64,128]{1,0:T(8,128)S(1)}, u32[]{:S(2)}, u32[]{:S(2)}) %collective-permute-start.10) | collective-permute-done | bytes 32800 | tf_op jit(solution)/shard_map/ppermute | solution.py:897
  83.8 4.7 %collective-permute-start.19 = (f32[5,16,128]{2,1,0:T(8,128)S(1)}, f32[5,16,128]{2,1,0:T(8,128)S(1)}, u32[]{:S(2)}, u32[]{:S(2)}) collective-permute-start(f32[5,16,128]{2,1,0:T(8,128)S(1)} %get-tuple-element.69), channel_id=1, source_target_pairs={{0,28},{4,0},{8,4},{12,8},{16,12},{20,16},{24,20},{28,24},{1,29},{... | collective-permute-start | bytes 122888 | tf_op jit(solution)/shard_map/ppermute | solution.py:897
  90.5 4.6 %collide.3 = (f32[19,256,128]{2,1,0:T(8,128)}, f32[10,16,8,128]{3,2,1,0:T(8,128)S(1)}) custom-call(s32[10]{0:T(128)S(4)} %plan.1.refs_0_, f32[19,256,128]{2,1,0:T(8,128)S(1)} %collide.2.refs_0_.refs_1_, f32[5,16,128]{2,1,0:T(8,128)S(1)} %collective-permute-done.8.refs_1_.refs_2_, f32[5,16,128]{2,1,0:T(8,128)S(1)} %collective-permute-done.9.refs_2_.refs_3_, ...), custom_call_target="tpu_custom_call" | custom-call | tf_op jit(solution)/shard_map/collide/pallas_call | solution.py:815
  (67 shorter events, 12.4 us)
Async XLA Ops:
  6.1 12.5 %collective-permute-start.2 = (f32[96,128]{1,0:T(8,128)S(1)}, f32[96,128]{1,0:T(8,128)S(1)}, u32[]{:S(2)}, u32[]{:S(2)}) collective-permute-start(f32[96,128]{1,0:T(8,128)S(1)} %get-tuple-element.47), channel_id=1, source_target_pairs={{0,1},{1,2},{2,3},{3,0},{4,5},{5,6},{6,7},{7,4},{8,9},{9,10},{10,1... | collective-permute-start | bytes 147464 | tf_op jit(solution)/shard_map/ppermute | solution.py:897
  6.6 12.0 %collective-permute-start.3 = (f32[96,128]{1,0:T(8,128)S(1)}, f32[96,128]{1,0:T(8,128)S(1)}, u32[]{:S(2)}, u32[]{:S(2)}) collective-permute-start(f32[96,128]{1,0:T(8,128)S(1)} %get-tuple-element.48), channel_id=1, source_target_pairs={{0,2},{1,3},{2,0},{3,1},{4,6},{5,7},{6,4},{7,5},{8,10},{9,11},{10,... | collective-permute-start | bytes 147464 | tf_op jit(solution)/shard_map/ppermute | solution.py:897
  9.2 9.4 %collective-permute-start.4 = (f32[96,128]{1,0:T(8,128)S(1)}, f32[96,128]{1,0:T(8,128)S(1)}, u32[]{:S(2)}, u32[]{:S(2)}) collective-permute-start(f32[96,128]{1,0:T(8,128)S(1)} %get-tuple-element.49), channel_id=1, source_target_pairs={{0,3},{1,0},{2,1},{3,2},{4,7},{5,4},{6,5},{7,6},{8,11},{9,8},{10,9... | collective-permute-start | bytes 147464 | tf_op jit(solution)/shard_map/ppermute | solution.py:897
  24.4 20.3 %copy-start.3 = (f32[19,16,16,128]{3,2,1,0:T(8,128)S(1)}, f32[19,16,16,128]{3,2,1,0:T(8,128)}, u32[]{:S(2)}) copy-start(f32[19,16,16,128]{3,2,1,0:T(8,128)} %param.9) | copy-start | bytes 7471108
  24.4 39.8 %slice-start = ((s8[16777216]{0:T(1024)(128)(4,1)}), s8[4194304]{0:T(1024)(128)(4,1)S(1)}, s32[]{:S(2)}) async-start(s8[16777216]{0:T(1024)(128)(4,1)} %bitcast.11), calls=%async_computation | async-start | bytes 8388608
  24.4 39.8 %slice-start.1 = ((s8[16777216]{0:T(1024)(128)(4,1)}), s8[4194304]{0:T(1024)(128)(4,1)S(1)}, s32[]{:S(2)}) async-start(s8[16777216]{0:T(1024)(128)(4,1)} %bitcast.11), calls=%async_computation.1 | async-start | bytes 8388608
  24.4 39.8 %slice-start.2 = ((s8[16777216]{0:T(1024)(128)(4,1)}), s8[4194304]{0:T(1024)(128)(4,1)S(1)}, s32[]{:S(2)}) async-start(s8[16777216]{0:T(1024)(128)(4,1)} %bitcast.11), calls=%async_computation.2 | async-start | bytes 8388608
  25.4 24.3 %collective-permute-start.5 = (f32[112,128]{1,0:T(8,128)S(1)}, f32[112,128]{1,0:T(8,128)S(1)}, u32[]{:S(2)}, u32[]{:S(2)}) collective-permute-start(f32[112,128]{1,0:T(8,128)S(1)} %get-tuple-element.51), channel_id=1, source_target_pairs={{0,1},{1,2},{2,3},{3,0},{4,5},{5,6},{6,7},{7,4},{8,9},{9,10},{10,1... | collective-permute-start | bytes 172040 | tf_op jit(solution)/shard_map/ppermute | solution.py:897
  42.0 7.6 %collective-permute-start.6 = (f32[112,128]{1,0:T(8,128)S(1)}, f32[112,128]{1,0:T(8,128)S(1)}, u32[]{:S(2)}, u32[]{:S(2)}) collective-permute-start(f32[112,128]{1,0:T(8,128)S(1)} %get-tuple-element.52), channel_id=1, source_target_pairs={{0,2},{1,3},{2,0},{3,1},{4,6},{5,7},{6,4},{7,5},{8,10},{9,11},{10,... | collective-permute-start | bytes 172040 | tf_op jit(solution)/shard_map/ppermute | solution.py:897
  43.3 6.4 %collective-permute-start.7 = (f32[112,128]{1,0:T(8,128)S(1)}, f32[112,128]{1,0:T(8,128)S(1)}, u32[]{:S(2)}, u32[]{:S(2)}) collective-permute-start(f32[112,128]{1,0:T(8,128)S(1)} %get-tuple-element.53), channel_id=1, source_target_pairs={{0,3},{1,0},{2,1},{3,2},{4,7},{5,4},{6,5},{7,6},{8,11},{9,8},{10,9... | collective-permute-start | bytes 172040 | tf_op jit(solution)/shard_map/ppermute | solution.py:897
  46.3 3.4 %collective-permute-start = (f32[64,128]{1,0:T(8,128)S(1)}, f32[64,128]{1,0:T(8,128)S(1)}, u32[]{:S(2)}, u32[]{:S(2)}) collective-permute-start(f32[64,128]{1,0:T(8,128)S(1)} %get-tuple-element.39), channel_id=1, source_target_pairs={{0,1},{1,2},{2,3},{3,0},{4,5},{5,6},{6,7},{7,4},{8,9},{9,10},{10,1... | collective-permute-start | bytes 98312 | tf_op jit(solution)/shard_map/ppermute | solution.py:897
  46.3 3.3 %collective-permute-start.1 = (f32[64,128]{1,0:T(8,128)S(1)}, f32[64,128]{1,0:T(8,128)S(1)}, u32[]{:S(2)}, u32[]{:S(2)}) collective-permute-start(f32[64,128]{1,0:T(8,128)S(1)} %get-tuple-element.40), channel_id=1, source_target_pairs={{0,3},{1,0},{2,1},{3,2},{4,7},{5,4},{6,5},{7,6},{8,11},{9,8},{10,9... | collective-permute-start | bytes 98312 | tf_op jit(solution)/shard_map/ppermute | solution.py:897
  50.2 7.9 %collective-permute-start.8 = (f32[5,16,128]{2,1,0:T(8,128)S(1)}, f32[5,16,128]{2,1,0:T(8,128)S(1)}, u32[]{:S(2)}, u32[]{:S(2)}) collective-permute-start(f32[5,16,128]{2,1,0:T(8,128)S(1)} %get-tuple-element.54), channel_id=1, source_target_pairs={{0,4},{4,8},{8,12},{12,16},{16,20},{20,24},{24,28},{28,0},{1,5},{5... | collective-permute-start | bytes 122888 | tf_op jit(solution)/shard_map/ppermute | solution.py:897
  51.7 6.3 %collective-permute-start.9 = (f32[5,16,128]{2,1,0:T(8,128)S(1)}, f32[5,16,128]{2,1,0:T(8,128)S(1)}, u32[]{:S(2)}, u32[]{:S(2)}) collective-permute-start(f32[5,16,128]{2,1,0:T(8,128)S(1)} %get-tuple-element.55), channel_id=1, source_target_pairs={{0,28},{4,0},{8,4},{12,8},{16,12},{20,16},{24,20},{28,24},{1,29},{... | collective-permute-start | bytes 122888 | tf_op jit(solution)/shard_map/ppermute | solution.py:897
  58.6 3.6 %collective-permute-start.12 = (f32[96,128]{1,0:T(8,128)S(1)}, f32[96,128]{1,0:T(8,128)S(1)}, u32[]{:S(2)}, u32[]{:S(2)}) collective-permute-start(f32[96,128]{1,0:T(8,128)S(1)} %get-tuple-element.60), channel_id=1, source_target_pairs={{0,1},{1,2},{2,3},{3,0},{4,5},{5,6},{6,7},{7,4},{8,9},{9,10},{10,1... | collective-permute-start | bytes 147464 | tf_op jit(solution)/shard_map/ppermute | solution.py:897
  60.1 4.1 %collective-permute-start.13 = (f32[96,128]{1,0:T(8,128)S(1)}, f32[96,128]{1,0:T(8,128)S(1)}, u32[]{:S(2)}, u32[]{:S(2)}) collective-permute-start(f32[96,128]{1,0:T(8,128)S(1)} %get-tuple-element.61), channel_id=1, source_target_pairs={{0,2},{1,3},{2,0},{3,1},{4,6},{5,7},{6,4},{7,5},{8,10},{9,11},{10,... | collective-permute-start | bytes 147464 | tf_op jit(solution)/shard_map/ppermute | solution.py:897
  60.4 3.7 %collective-permute-start.14 = (f32[96,128]{1,0:T(8,128)S(1)}, f32[96,128]{1,0:T(8,128)S(1)}, u32[]{:S(2)}, u32[]{:S(2)}) collective-permute-start(f32[96,128]{1,0:T(8,128)S(1)} %get-tuple-element.62), channel_id=1, source_target_pairs={{0,3},{1,0},{2,1},{3,2},{4,7},{5,4},{6,5},{7,6},{8,11},{9,8},{10,9... | collective-permute-start | bytes 147464 | tf_op jit(solution)/shard_map/ppermute | solution.py:897
  64.6 18.7 %collective-permute-start.15 = (f32[112,128]{1,0:T(8,128)S(1)}, f32[112,128]{1,0:T(8,128)S(1)}, u32[]{:S(2)}, u32[]{:S(2)}) collective-permute-start(f32[112,128]{1,0:T(8,128)S(1)} %get-tuple-element.64), channel_id=1, source_target_pairs={{0,1},{1,2},{2,3},{3,0},{4,5},{5,6},{6,7},{7,4},{8,9},{9,10},{10,1... | collective-permute-start | bytes 172040 | tf_op jit(solution)/shard_map/ppermute | solution.py:897
  76.5 6.8 %collective-permute-start.16 = (f32[112,128]{1,0:T(8,128)S(1)}, f32[112,128]{1,0:T(8,128)S(1)}, u32[]{:S(2)}, u32[]{:S(2)}) collective-permute-start(f32[112,128]{1,0:T(8,128)S(1)} %get-tuple-element.65), channel_id=1, source_target_pairs={{0,2},{1,3},{2,0},{3,1},{4,6},{5,7},{6,4},{7,5},{8,10},{9,11},{10,... | collective-permute-start | bytes 172040 | tf_op jit(solution)/shard_map/ppermute | solution.py:897
  76.9 6.5 %collective-permute-start.17 = (f32[112,128]{1,0:T(8,128)S(1)}, f32[112,128]{1,0:T(8,128)S(1)}, u32[]{:S(2)}, u32[]{:S(2)}) collective-permute-start(f32[112,128]{1,0:T(8,128)S(1)} %get-tuple-element.66), channel_id=1, source_target_pairs={{0,3},{1,0},{2,1},{3,2},{4,7},{5,4},{6,5},{7,6},{8,11},{9,8},{10,9... | collective-permute-start | bytes 172040 | tf_op jit(solution)/shard_map/ppermute | solution.py:897
  79.9 3.4 %collective-permute-start.10 = (f32[64,128]{1,0:T(8,128)S(1)}, f32[64,128]{1,0:T(8,128)S(1)}, u32[]{:S(2)}, u32[]{:S(2)}) collective-permute-start(f32[64,128]{1,0:T(8,128)S(1)} %get-tuple-element.56), channel_id=1, source_target_pairs={{0,1},{1,2},{2,3},{3,0},{4,5},{5,6},{6,7},{7,4},{8,9},{9,10},{10,1... | collective-permute-start | bytes 98312 | tf_op jit(solution)/shard_map/ppermute | solution.py:897
  80.0 3.3 %collective-permute-start.11 = (f32[64,128]{1,0:T(8,128)S(1)}, f32[64,128]{1,0:T(8,128)S(1)}, u32[]{:S(2)}, u32[]{:S(2)}) collective-permute-start(f32[64,128]{1,0:T(8,128)S(1)} %get-tuple-element.57), channel_id=1, source_target_pairs={{0,3},{1,0},{2,1},{3,2},{4,7},{5,4},{6,5},{7,6},{8,11},{9,8},{10,9... | collective-permute-start | bytes 98312 | tf_op jit(solution)/shard_map/ppermute | solution.py:897
  83.8 11.3 %collective-permute-start.18 = (f32[5,16,128]{2,1,0:T(8,128)S(1)}, f32[5,16,128]{2,1,0:T(8,128)S(1)}, u32[]{:S(2)}, u32[]{:S(2)}) collective-permute-start(f32[5,16,128]{2,1,0:T(8,128)S(1)} %get-tuple-element.68), channel_id=1, source_target_pairs={{0,4},{4,8},{8,12},{12,16},{16,20},{20,24},{24,28},{28,0},{1,5},{5... | collective-permute-start | bytes 122888 | tf_op jit(solution)/shard_map/ppermute | solution.py:897
  83.8 11.3 %collective-permute-start.19 = (f32[5,16,128]{2,1,0:T(8,128)S(1)}, f32[5,16,128]{2,1,0:T(8,128)S(1)}, u32[]{:S(2)}, u32[]{:S(2)}) collective-permute-start(f32[5,16,128]{2,1,0:T(8,128)S(1)} %get-tuple-element.69), channel_id=1, source_target_pairs={{0,28},{4,0},{8,4},{12,8},{16,12},{20,16},{24,20},{28,24},{1,29},{... | collective-permute-start | bytes 122888 | tf_op jit(solution)/shard_map/ppermute | solution.py:897
  (11 other events, 104.2 us)

commit v2 on v1

--- a/solution.py
+++ b/solution.py
@@ -75,13 +75,20 @@
 def collide(f, force, wanted):
     density, momentum = moments(f)
     inverse = 1.0 / density
-    v = [(momentum[a] + 0.5 * force[a]) * inverse for a in range(3)]
     relaxed = OMEGA * density
-    square = v[0] * v[0] + v[1] * v[1] + v[2] * v[2]
-    work = v[0] * force[0] + v[1] * force[1] + v[2] * force[2]
-    base = relaxed * (1.0 - 1.5 * square) - (3.0 * GUO) * work
-    drive = [relaxed * v[a] + GUO * force[a] for a in range(3)]
-    bend = [(4.5 * relaxed) * v[a] + (9.0 * GUO) * force[a] for a in range(3)]
+    if force is None:
+        v = [momentum[a] * inverse for a in range(3)]
+        square = v[0] * v[0] + v[1] * v[1] + v[2] * v[2]
+        base = relaxed * (1.0 - 1.5 * square)
+        drive = [OMEGA * momentum[a] for a in range(3)]
+        bend = [4.5 * part for part in drive]
+    else:
+        v = [(momentum[a] + 0.5 * force[a]) * inverse for a in range(3)]
+        square = v[0] * v[0] + v[1] * v[1] + v[2] * v[2]
+        work = v[0] * force[0] + v[1] * force[1] + v[2] * force[2]
+        base = relaxed * (1.0 - 1.5 * square) - (3.0 * GUO) * work
+        drive = [relaxed * v[a] + GUO * force[a] for a in range(3)]
+        bend = [(4.5 * relaxed) * v[a] + (9.0 * GUO) * force[a] for a in range(3)]
     post = {}
     if 0 in wanted:
         post[0] = KEEP * f[0] + base * (1.0 / 3.0)
@@ -153,41 +160,29 @@
 PARAMS = pltpu.CompilerParams(vmem_limit_bytes=VMEM_LIMIT)
 
 
-def plan_kernel(sh, place, plan, count):
+def write_plan(sh, place, plan):
     row = lax.axis_index("gx")
-    me = lax.axis_index("gy")
-    for k in range(sh.tiles * sh.slots + sh.slots):
-        plan[k] = -1
-    for k in range(sh.tiles):
-        count[k] = 0
-
-    def visit(rotor, carry):
-        @pl.when(place[rotor, 0] == row)
-        def _():
-            owner = place[rotor, 2]
-            slot = count[owner]
-            count[owner] = slot + 1
-            plan[owner * sh.slots + slot] = place[rotor, 1]
-
-            @pl.when(owner == me)
-            def _():
-                plan[sh.tiles * sh.slots + slot] = rotor
-
-        return carry
-
-    lax.fori_loop(0, sh.rotors, visit, 0)
-
-
-def make_plan(sh, rotor_place):
-    size = sh.tiles * sh.slots + sh.slots
-    return pl.pallas_call(
-        lambda *refs: plan_kernel(sh, *refs),
-        out_shape=pltpu.SMEM((size,), jnp.int32),
-        in_specs=[SM],
-        out_specs=SM,
-        scratch_shapes=[pltpu.SMEM((sh.tiles,), jnp.int32)],
-        name="plan",
-    )(rotor_place)
+    shape = (sh.tiles, sh.rotors)
+    mine = jnp.logical_and(place[2:3, :] == iota(shape, 0), place[0:1, :] == row)
+    keys = iota(shape, 1) * sh.xs + place[1:2, :]
+    none = sh.rotors * sh.xs
+    last = jnp.full((sh.tiles, 1), -1, jnp.int32)
+    for slot in range(sh.slots):
+        left = jnp.logical_and(mine, keys > last)
+        last = jnp.min(jnp.where(left, keys, none), axis=1, keepdims=True)
+        for owner in range(sh.tiles):
+            key = last[owner, 0]
+            plan[owner * sh.slots + slot] = jnp.where(key < none, key, -1)
+
+
+def plane_at(sh, plan, owner, slot):
+    key = plan[owner * sh.slots + slot]
+    return jnp.where(key < 0, -1, lax.rem(key, sh.xs))
+
+
+def rotor_at(sh, plan, slot):
+    key = plan[lax.axis_index("gy") * sh.slots + slot]
+    return jnp.where(key < 0, -1, lax.div(key, sh.xs))
 
 
 def plane_of(sh, f, x, low, high):
@@ -208,15 +203,12 @@
     return planes
 
 
-def pre_kernel(sh, has_edges, *refs):
-    plan, f = refs[:2]
-    low, high = refs[2:4] if has_edges else (None, None)
-    outs = refs[4:] if has_edges else refs[2:]
+def write_sections(sh, plan, f, low, high, outs):
     me = lax.axis_index("gy")
     for shift in range(sh.tiles):
         owner = lax.rem(me + shift, sh.tiles)
         for slot in range(sh.slots):
-            x = plan[owner * sh.slots + slot]
+            x = plane_at(sh, plan, owner, slot)
 
             @pl.when(x >= 0)
             def _():
@@ -233,11 +225,37 @@
                 outs[shift][at : at + 3 * sh.levels, :] = jnp.zeros((3 * sh.levels, LANES), F32)
 
 
+def start_kernel(sh, place, f_in, plan, f, *refs):
+    outs, sem = refs[:-1], refs[-1]
+    copy = pltpu.make_async_copy(f_in, f, sem)
+    copy.start()
+    write_plan(sh, place, plan)
+    copy.wait()
+    write_sections(sh, plan, f, None, None, outs)
+
+
+def start(sh, rotor_place, f_in):
+    out = pl.pallas_call(
+        lambda *refs: start_kernel(sh, *refs),
+        out_shape=[
+            pltpu.SMEM((sh.tiles * sh.slots,), jnp.int32),
+            pltpu.VMEM((19, sh.levels * sh.xs, LANES), F32),
+        ]
+        + [pltpu.VMEM((sh.section, LANES), F32)] * sh.tiles,
+        in_specs=[VM, HB],
+        out_specs=[SM] + [VM] * (1 + sh.tiles),
+        scratch_shapes=[pltpu.SemaphoreType.DMA],
+        compiler_params=PARAMS,
+        name="start",
+    )(jnp.transpose(rotor_place), f_in.reshape(19, sh.levels * sh.xs, LANES))
+    return in_smem(out[0]), in_vmem(out[1]), out[2:]
+
+
 def make_sections(sh, plan, f, edges):
     return pl.pallas_call(
-        lambda *refs: pre_kernel(sh, bool(edges), *refs),
+        lambda plan, f, low, high, *outs: write_sections(sh, plan, f, low, high, outs),
         out_shape=[pltpu.VMEM((sh.section, LANES), F32)] * sh.tiles,
-        in_specs=[SM] + [VM] * (1 + len(edges)),
+        in_specs=[SM] + [VM] * 3,
         out_specs=[VM] * sh.tiles,
         compiler_params=PARAMS,
         name="sections",
@@ -308,24 +326,24 @@
     return (jnp.where(near, 3.0, 5.0) - 2.0 * distance + jnp.where(near, root, -root)) * 0.125
 
 
-TABLE_CHUNK = 256
-
-
-def table_kernel(sh, plan, cells, across, upward, info, codes, sem):
-    ids = [plan[sh.tiles * sh.slots + slot] for slot in range(sh.slots)]
+TABLE_CHUNK = 1024
+
+
+def table_kernel(sh, plan, cells, after, across, upward, info, codes, sem):
+    del after
+    ids = [rotor_at(sh, plan, slot) for slot in range(sh.slots)]
     copies = []
     for slot in range(sh.slots):
         first = pl.multiple_of(jnp.maximum(ids[slot], 0) // 8 * 8, 8)
         copy = pltpu.make_async_copy(cells.at[pl.ds(first, 8), :], codes.at[slot], sem.at[slot])
         copy.start()
         copies.append(copy)
-    width = TABLE_CHUNK
+    width = min(TABLE_CHUNK, sh.markers)
     corner = iota((8, width), 0)
     spanwise = corner < 4
     place = (corner % 4).astype(F32) - 1.0
-    ycells = iota((LANES, width), 0).astype(F32).astype(BF16)
-    zcells = iota((sh.levels, width), 0)
-    zero = jnp.zeros((LANES, width), BF16)
+    ycells = iota((LANES, LANES), 0).astype(F32).astype(BF16)
+    zcells = iota((sh.levels, LANES), 0)
     for slot in range(sh.slots):
         copies[slot].wait()
 
@@ -342,25 +360,29 @@
 
             def chunk(window, at):
                 code = codes[slot, pl.ds(row, 1), pl.ds(at, width)]
-                cell = code // (64 * sh.levels) - start - window * LANES
-                level = code // 64 % sh.levels
+                cells_y = code // (64 * sh.levels) - start - window * LANES
+                levels = code // 64 % sh.levels
                 eighths = jnp.where(spanwise, code // 8 % 8, code % 8)
                 weights = peskin(place - eighths.astype(F32) * 0.125)
                 top = weights.astype(BF16)
                 rest = (weights - top.astype(F32)).astype(BF16)
-                tall = jnp.zeros((sh.levels, width), F32)
-                for j in range(4):
-                    tall = jnp.where(zcells == level + j, weights[4 + j : 5 + j, :], tall)
-                upward[slot, :, pl.ds(at, width)] = tall
-                wide = [zero, zero]
-                for j in range(4):
-                    here = ycells == (cell + j).astype(F32).astype(BF16)
-                    for part, source in ((0, top), (1, rest)):
-                        wide[part] = jnp.where(here, source[j : j + 1, :], wide[part])
-                for part in range(2):
-                    across[slot, window, part * LANES : (part + 1) * LANES, pl.ds(at, width)] = wide[
-                        part
-                    ]
+                cells_y = cells_y.astype(F32)
+                for group in range(width // LANES):
+                    lanes = slice(group * LANES, (group + 1) * LANES)
+                    to = pl.ds(at + group * LANES, LANES)
+                    tall = jnp.zeros((sh.levels, LANES), F32)
+                    for j in range(4):
+                        tall = jnp.where(
+                            zcells == levels[:, lanes] + j, weights[4 + j : 5 + j, lanes], tall
+                        )
+                    upward[slot, :, to] = tall
+                    wide = [jnp.zeros((LANES, LANES), BF16)] * 2
+                    for j in range(4):
+                        here = ycells == (cells_y[:, lanes] + float(j)).astype(BF16)
+                        for part, source in ((0, top), (1, rest)):
+                            wide[part] = jnp.where(here, source[j : j + 1, lanes], wide[part])
+                    for part in range(2):
+                        across[slot, window, part * LANES : (part + 1) * LANES, to] = wide[part]
 
             def sweep(window):
                 def body(i, carry):
@@ -376,15 +398,15 @@
                 sweep(1)
 
 
-def make_tables(sh, plan, marker_cell):
-    return pl.pallas_call(
+def make_tables(sh, plan, marker_cell, after):
+    across, upward, info = pl.pallas_call(
         lambda *refs: table_kernel(sh, *refs),
         out_shape=[
             pltpu.VMEM((sh.slots, 2, 2 * LANES, sh.markers), BF16),
             pltpu.VMEM((sh.slots, sh.levels, sh.markers), F32),
             pltpu.SMEM((2 * sh.slots,), jnp.int32),
         ],
-        in_specs=[SM, HB],
+        in_specs=[SM, HB, VM],
         out_specs=[VM, VM, SM],
         scratch_shapes=[
             pltpu.VMEM((sh.slots, 8, sh.markers), jnp.int32),
@@ -392,67 +414,53 @@
         ],
         compiler_params=PARAMS,
         name="tables",
-    )(plan, marker_cell)
-
-
-def blade_kernel(sh, plan, phases, area, twist, speed, angle, filt, blades, filtered):
-    rows = sh.slots * sh.groups
-
-    def dense(read, write):
+    )(plan, marker_cell, after)
+    return in_vmem(across), in_vmem(upward), in_smem(info)
+
+
+def blade_kernel(sh, plan, phases, twist, angle, after, blades):
+    del after
+    blades[0] = jnp.sin(angle[...])
+    blades[1] = jnp.cos(angle[...])
+    sin_twist = jnp.sin(twist[...])
+    cos_twist = jnp.cos(twist[...])
+    owner = iota((1, LANES), 1)
+    rows = iota((sh.slots * sh.groups, LANES), 0) % sh.slots
+    phase = jnp.zeros((1, LANES), F32)
+    for step in range(sh.steps):
         for slot in range(sh.slots):
-            for group in range(sh.groups):
-                write(slot * sh.groups + group, read(slot, group * LANES))
-
-    def keep(k):
-        def write(row, value):
-            blades[k, row : row + 1, :] = value
-
-        return write
-
-    for k, source in ((0, area), (1, speed), (2, angle), (3, twist)):
-        dense(lambda slot, at: source[slot : slot + 1, at : at + LANES], keep(k))
-    for axis in range(3):
-
-        def write(row, value):
-            filtered[axis, row : row + 1, :] = value
-
-        dense(lambda slot, at: filt[slot, axis : axis + 1, at : at + LANES], write)
-    around = blades[2]
-    turned = blades[3]
-    blades[2] = jnp.sin(around)
-    blades[3] = jnp.cos(around)
-    sin_twist = jnp.sin(turned)
-    cos_twist = jnp.cos(turned)
-    owner = iota((rows, LANES), 0) // sh.groups
+            rotor = jnp.maximum(rotor_at(sh, plan, slot), 0)
+            here = owner == step * sh.slots + slot
+            phase = jnp.where(here, phases[step, rotor].astype(F32), phase)
+    pitch = PITCH_AMP * jnp.sin((2.0 * math.pi / PHASES) * phase)
+    sin_pitch = jnp.sin(pitch)
+    cos_pitch = jnp.cos(pitch)
     for step in range(sh.steps):
-        phase = jnp.zeros((rows, LANES), F32)
-        for slot in range(sh.slots):
-            rotor = jnp.maximum(plan[sh.tiles * sh.slots + slot], 0)
-            phase = jnp.where(owner == slot, phases[rotor, step].astype(F32), phase)
-        pitch = PITCH_AMP * jnp.sin((2.0 * math.pi / PHASES) * phase)
-        sin_pitch = jnp.sin(pitch)
-        cos_pitch = jnp.cos(pitch)
-        blades[4 + 2 * step] = sin_twist * cos_pitch + cos_twist * sin_pitch
-        blades[5 + 2 * step] = cos_twist * cos_pitch - sin_twist * sin_pitch
-
-
-def make_blades(sh, plan, phases, area, twist, speed, angle, filt):
+        parts = []
+        for part in (sin_pitch, cos_pitch):
+            total = jnp.zeros((sh.slots * sh.groups, LANES), F32)
+            for slot in range(sh.slots):
+                lane = step * sh.slots + slot
+                total = jnp.where(rows == slot, part[:, lane : lane + 1], total)
+            parts.append(total)
+        blades[2 + 2 * step] = sin_twist * parts[1] + cos_twist * parts[0]
+        blades[3 + 2 * step] = cos_twist * parts[1] - sin_twist * parts[0]
+
+
+def make_blades(sh, plan, phases, twist, angle, after):
     rows = sh.slots * sh.groups
     return pl.pallas_call(
         lambda *refs: blade_kernel(sh, *refs),
-        out_shape=[
-            pltpu.VMEM((4 + 2 * sh.steps, rows, LANES), F32),
-            pltpu.VMEM((3, rows, LANES), F32),
-        ],
-        in_specs=[SM, SM] + [VM] * 5,
-        out_specs=[VM, VM],
+        out_shape=pltpu.VMEM((2 + 2 * sh.steps, rows, LANES), F32),
+        in_specs=[SM, SM, VM, VM, VM],
+        out_specs=VM,
         compiler_params=PARAMS,
         name="blades",
-    )(plan, phases, area, twist, speed, angle, filt)
-
-
-SAMPLE_CHUNK = 512
-SPREAD_CHUNK = 1024
+    )(plan, jnp.transpose(phases), twist, angle, after)
+
+
+SAMPLE_CHUNK = 4096
+SPREAD_CHUNK = 4096
 
 
 def split(value):
@@ -460,7 +468,9 @@
     return top, (value - top.astype(F32)).astype(BF16)
 
 
-def marker_kernel(sh, step, plan, info, across, upward, blades, filt_old, *refs):
+def marker_kernel(
+    sh, step, plan, info, across, upward, area, speed, blades, filt_old, west, east, *refs
+):
     sections = refs[: sh.tiles]
     filt_new, loads = refs[sh.tiles : sh.tiles + 2]
     forces = refs[sh.tiles + 2 : 2 * sh.tiles + 2]
@@ -477,7 +487,7 @@
         return tile, jnp.minimum(tile + 1, sh.tiles - 1), start - tile * LANES
 
     def windows(slot, body):
-        @pl.when(plan[sh.tiles * sh.slots + slot] >= 0)
+        @pl.when(rotor_at(sh, plan, slot) >= 0)
         def _():
             body(0)
 
@@ -512,7 +522,7 @@
                         keepdims=True,
                     )
                     for group in range(SAMPLE_CHUNK // LANES):
-                        row = slot * sh.groups + i * (SAMPLE_CHUNK // LANES) + group
+                        row = (i * (SAMPLE_CHUNK // LANES) + group) * sh.slots + slot
                         piece = part[:, group * LANES : (group + 1) * LANES]
                         if window:
                             piece = piece + sampled[axis, pl.ds(row, 1), :]
@@ -529,20 +539,20 @@
         value = old + MIX * (sampled[axis] - old)
         filt_new[axis] = value
         felt.append(value)
-    sin_t = blades[2]
-    cos_t = blades[3]
-    tangent = blades[1] + sin_t * felt[1] - cos_t * felt[2]
+    sin_t = blades[0]
+    cos_t = blades[1]
+    tangent = speed[...] + sin_t * felt[1] - cos_t * felt[2]
     square = felt[0] * felt[0] + tangent * tangent
     inverse = 1.0 / jnp.sqrt(square)
     sin_p = felt[0] * inverse
     cos_p = tangent * inverse
-    sin_b = blades[4 + 2 * step]
-    cos_b = blades[5 + 2 * step]
+    sin_b = blades[2 + 2 * step]
+    cos_b = blades[3 + 2 * step]
     sin_a = sin_p * cos_b - cos_p * sin_b
     cos_a = cos_p * cos_b + sin_p * sin_b
     lift = (2.0 * math.pi) * sin_a * cos_a
     drag = 0.02 + sin_a * sin_a
-    dynamic = 0.5 * blades[0] * square
+    dynamic = 0.5 * area[...] * square
     around_axis = dynamic * (lift * sin_p - drag * cos_p)
     loads[0] = dynamic * (lift * cos_p + drag * sin_p)
     loads[1] = -around_axis * sin_t
@@ -558,7 +568,7 @@
                 at = pl.multiple_of(i * SPREAD_CHUNK, SPREAD_CHUNK)
                 for group in range(SPREAD_CHUNK // LANES):
                     heights = upward[slot, :, pl.ds(at + group * LANES, LANES)]
-                    row = slot * sh.groups + i * (SPREAD_CHUNK // LANES) + group
+                    row = (i * (SPREAD_CHUNK // LANES) + group) * sh.slots + slot
                     parts = [heights * loads[axis, pl.ds(row, 1), :] for axis in range(3)]
                     top, rest = split(jnp.concatenate(parts, axis=0))
                     weighted[:tall, group * LANES : (group + 1) * LANES] = top
@@ -598,17 +608,25 @@
             right = jnp.broadcast_to(spread[after, at, :][:, :1], (sh.levels, LANES))
             ghosts = jnp.where(lanes == 2 * k, left, ghosts)
             ghosts = jnp.where(lanes == 2 * k + 1, right, ghosts)
-        forces[shift][sh.section :, :] = ghosts
-
-
-def do_markers(sh, step, plan, info, across, upward, blades, filt, sections):
+        forces[shift][sh.section : sh.section + sh.levels, :] = ghosts
+    forces[1][sh.section + sh.levels :, :] = east[...]
+    forces[sh.tiles - 1][sh.section + sh.levels :, :] = west[...]
+
+
+def do_markers(sh, step, plan, tables, fixed, blades, filt, columns, sections):
+    across, upward, info = tables
     rows = sh.slots * sh.groups
     dense = pltpu.VMEM((3, rows, LANES), F32)
-    force = pltpu.VMEM((sh.section + sh.levels, LANES), F32)
+    plain = sh.section + sh.levels
+    extra = columns[0].shape[0]
+    forces = [
+        pltpu.VMEM((plain + (extra if by in (1, sh.tiles - 1) else 0), LANES), F32)
+        for by in range(sh.tiles)
+    ]
     out = pl.pallas_call(
         lambda *refs: marker_kernel(sh, step, *refs),
-        out_shape=[dense, dense] + [force] * sh.tiles,
-        in_specs=[SM, SM] + [VM] * (4 + sh.tiles),
+        out_shape=[dense, dense] + forces,
+        in_specs=[SM, SM] + [VM] * (8 + sh.tiles),
         out_specs=[VM] * (2 + sh.tiles),
         scratch_shapes=[
             pltpu.VMEM((sh.tiles, sh.section, LANES), F32),
@@ -618,25 +636,25 @@
         ],
         compiler_params=PARAMS,
         name="markers",
-    )(plan, info, across, upward, blades, filt, *sections)
-    return out[0], out[1], out[2:]
+    )(plan, info, across, upward, *fixed, blades, filt, *columns, *sections)
+    return in_vmem(out[0]), in_vmem(out[1]), out[2:]
 
 
 def edge_kernel(sh, has_edges, plan, f, *refs):
     low, high = refs[:2] if has_edges else (None, None)
     refs = refs[2 * has_edges :]
-    left, right = refs[:2]
-    forces = refs[2 : 2 + sh.tiles]
-    outs = refs[2 + sh.tiles :]
+    forces = refs[: sh.tiles]
+    outs = refs[sh.tiles + 1 :]
+    first = sh.section + sh.levels
     me = lax.axis_index("gy")
     lanes = iota((sh.levels, LANES), 1)
-    groups = (left.shape[0] - sh.levels) // sh.xs
-    corner_rows = pl.ds(groups * sh.xs, sh.levels)
+    per = LANES // sh.levels
+    corner_rows = pl.ds(first + (19 + per - 1) // per * sh.xs, sh.levels)
     blank = jnp.zeros((sh.levels, LANES), F32)
     planes_at = (0, sh.xs - 1)
     corner = []
-    from_left = left[corner_rows, :]
-    from_right = right[corner_rows, :]
+    from_left = forces[1][corner_rows, :]
+    from_right = forces[sh.tiles - 1][corner_rows, :]
     for q in range(19):
         a = pltpu.roll(from_left, (LANES - 2 * q) % LANES, 1)
         b = pltpu.roll(from_right, (LANES + 2 - 2 * q) % LANES, 1)
@@ -645,9 +663,9 @@
     edge_force = [[blank, blank, blank], [blank, blank, blank]]
     for shift in range(sh.tiles):
         owner = lax.rem(me + sh.tiles - shift, sh.tiles)
-        ghosts = forces[shift][sh.section :, :]
+        ghosts = forces[shift][sh.section : sh.section + sh.levels, :]
         for slot in range(sh.slots):
-            x = plan[owner * sh.slots + slot]
+            x = plane_at(sh, plan, owner, slot)
             for axis in range(3):
                 k = slot * 3 + axis
                 piece = forces[shift][k * sh.levels : (k + 1) * sh.levels, :]
@@ -680,73 +698,32 @@
             out[k] = value
 
 
-def make_edges(sh, plan, f, edges, columns, forces):
+def make_edges(sh, plan, f, edges, forces, after):
     return pl.pallas_call(
         lambda *refs: edge_kernel(sh, bool(edges), *refs),
         out_shape=[pltpu.VMEM((len(PLUS), sh.levels, LANES), F32)] * 2,
-        in_specs=[SM] + [VM] * (3 + len(edges) + sh.tiles),
+        in_specs=[SM] + [VM] * (2 + len(edges) + sh.tiles),
         out_specs=[VM] * 2,
         compiler_params=PARAMS,
         name="edges",
-    )(plan, f, *edges, *columns, *forces)
-
-
-def collide_kernel(sh, has_edges, last, plan, f, *refs):
+    )(plan, f, *edges, *forces, after)
+
+
+def bulk_kernel(sh, has_edges, last, plan, f, *refs):
     low, high = refs[:2] if has_edges else (None, None)
     refs = refs[2 * has_edges :]
-    left, right = refs[:2]
-    forces = refs[2 : 2 + sh.tiles]
-    out = refs[2 + sh.tiles]
-    kept = refs[3 + sh.tiles] if last else None
-    field, ghost_posts = refs[-2:]
-    me = lax.axis_index("gy")
+    loads, filt, out = refs[:3]
     xs = sh.xs
-    lanes = iota((xs, LANES), 1)
     xrows = iota((xs, LANES), 0)
-    per = LANES // sh.levels
-    field[...] = jnp.zeros(field.shape, F32)
-    ghost_force = [jnp.zeros((xs, LANES), F32) for axis in range(3)]
-    for shift in range(sh.tiles):
-        owner = lax.rem(me + sh.tiles - shift, sh.tiles)
-        ghosts = jnp.transpose(
-            jnp.concatenate(
-                [
-                    forces[shift][sh.section :, :],
-                    jnp.zeros((LANES - sh.levels, LANES), F32),
-                ],
-                axis=0,
-            )
-        )
+    if last:
+        rows = iota((sh.slots * sh.groups, LANES), 0) % sh.slots
+        used = jnp.zeros((sh.slots * sh.groups, LANES), jnp.int32)
         for slot in range(sh.slots):
-            x = plan[owner * sh.slots + slot]
-
-            @pl.when(x >= 0)
-            def _():
-                for axis in range(3):
-                    k = slot * 3 + axis
-                    at = pl.ds(x, sh.levels, stride=xs)
-                    field[axis, at, :] = (
-                        field[axis, at, :] + forces[shift][k * sh.levels : (k + 1) * sh.levels, :]
-                    )
-
+            there = (rotor_at(sh, plan, slot) >= 0).astype(jnp.int32)
+            used = jnp.where(rows == slot, there, used)
+        for source, target in ((loads, refs[3]), (filt, refs[4])):
             for axis in range(3):
-                k = slot * 3 + axis
-                far = pltpu.roll(ghosts[2 * k + 1 : 2 * k + 2, :], sh.levels, 1)
-                piece = ghosts[2 * k : 2 * k + 1, :] + far
-                ghost_force[axis] = ghost_force[axis] + jnp.where(xrows == x, piece, 0.0)
-
-    ghost = []
-    for q in range(19):
-        at = pl.ds(q // per * xs, xs)
-        shift = (q % per) * sh.levels
-        a = pltpu.roll(left[at, :], (LANES - shift) % LANES, 1)
-        b = pltpu.roll(right[at, :], (LANES + sh.levels - shift) % LANES, 1)
-        ghost.append(
-            jnp.where(lanes < sh.levels, a, jnp.where(lanes < 2 * sh.levels, b, 1.0))
-        )
-    posted = collide(ghost, ghost_force, SIDEWAYS)
-    for k, q in enumerate(SIDEWAYS):
-        ghost_posts[k] = posted[q]
+                target[axis] = jnp.where(used > 0, source[axis], 0.0)
 
     def level(z, bottom, top):
         at = aligned(z * xs, xs)
@@ -763,8 +740,7 @@
                             xrows == xs - 1, high[MINUS.index(q), pl.ds(z, 1), :], tile
                         )
             here.append(tile)
-        force = [field[axis, pl.ds(at, xs), :] for axis in range(3)]
-        post = collide(here, force, range(19))
+        post = collide(here, None, range(19))
         for q in range(19):
             dx, dy, dz = DIRS[q]
             value = post[q]
@@ -772,26 +748,11 @@
                 to, target = OPPOSITE[q], z
             else:
                 to, target = q, z + dz
-                if dy == 1:
-                    value = pltpu.roll(value, 1, 1)
-                    other = pltpu.roll(
-                        ghost_posts[SIDEWAYS.index(q)], wrapped(LANES - z), 1
-                    )
-                    value = jnp.where(lanes == 0, other, value)
-                elif dy == -1:
-                    value = pltpu.roll(value, LANES - 1, 1)
-                    other = pltpu.roll(
-                        ghost_posts[SIDEWAYS.index(q)], LANES - 1 - sh.levels - z, 1
-                    )
-                    value = jnp.where(lanes == LANES - 1, other, value)
+                if dy:
+                    value = pltpu.roll(value, dy % LANES, 1)
                 if dx:
                     value = pltpu.roll(value, dx % xs, 0)
-            row = aligned(target * xs, xs)
-            out[to, pl.ds(row, xs), :] = value
-            if last and DIRS[to][0] == 1:
-                kept[PLUS.index(to), pl.ds(target, 1)] = value[None, :8]
-            if last and DIRS[to][0] == -1:
-                kept[len(PLUS) + MINUS.index(to), pl.ds(target, 1)] = value[None, xs - 8 :]
+            out[to, pl.ds(aligned(target * xs, xs), xs), :] = value
 
     level(0, True, False)
 
@@ -803,46 +764,171 @@
     level(sh.levels - 1, False, True)
 
 
-def do_collide(sh, last, plan, f, edges, columns, forces):
-    shape = (19, sh.levels * sh.xs, LANES)
+def do_bulk(sh, last, plan, f, edges, loads, filt):
+    out_shape = [pltpu.VMEM((19, sh.levels * sh.xs, LANES), F32)]
     if last:
-        out_shape = [
-            jax.ShapeDtypeStruct(shape, F32),
-            pltpu.VMEM((2 * len(PLUS), sh.levels, 8, LANES), F32),
-        ]
-    else:
-        out_shape = [pltpu.VMEM(shape, F32)]
+        out_shape += [jax.ShapeDtypeStruct(loads.shape, F32)] * 2
     return pl.pallas_call(
-        lambda *refs: collide_kernel(sh, bool(edges), last, *refs),
+        lambda *refs: bulk_kernel(sh, bool(edges), last, *refs),
         out_shape=out_shape,
-        in_specs=[SM] + [VM] * (3 + len(edges) + sh.tiles),
+        in_specs=[SM] + [VM] * (3 + len(edges)),
         out_specs=[VM] * len(out_shape),
+        compiler_params=PARAMS,
+        name="bulk",
+    )(plan, f, *edges, loads, filt)
+
+
+def patch_kernel(sh, has_edges, last, plan, f, *refs):
+    low, high = refs[:2] if has_edges else (None, None)
+    refs = refs[2 * has_edges :]
+    forces = refs[: sh.tiles]
+    out = refs[sh.tiles + 1]
+    field, ghost_posts = refs[-3:-1]
+    sem = refs[-1]
+    me = lax.axis_index("gy")
+    xs = sh.xs
+    lanes = iota((xs, LANES), 1)
+    xrows = iota((xs, LANES), 0)
+    per = LANES // sh.levels
+    field[...] = jnp.zeros(field.shape, F32)
+    ghost_force = [jnp.zeros((xs, LANES), F32) for axis in range(3)]
+    for shift in range(sh.tiles):
+        owner = lax.rem(me + sh.tiles - shift, sh.tiles)
+        ghosts = jnp.transpose(
+            jnp.concatenate(
+                [
+                    forces[shift][sh.section : sh.section + sh.levels, :],
+                    jnp.zeros((LANES - sh.levels, LANES), F32),
+                ],
+                axis=0,
+            )
+        )
+        for slot in range(sh.slots):
+            x = plane_at(sh, plan, owner, slot)
+
+            @pl.when(x >= 0)
+            def _():
+                for axis in range(3):
+                    k = slot * 3 + axis
+                    at = pl.ds(x, sh.levels, stride=xs)
+                    field[axis, at, :] = (
+                        field[axis, at, :] + forces[shift][k * sh.levels : (k + 1) * sh.levels, :]
+                    )
+
+            for axis in range(3):
+                k = slot * 3 + axis
+                far = pltpu.roll(ghosts[2 * k + 1 : 2 * k + 2, :], sh.levels, 1)
+                piece = ghosts[2 * k : 2 * k + 1, :] + far
+                ghost_force[axis] = ghost_force[axis] + jnp.where(xrows == x, piece, 0.0)
+
+    ghost = []
+    left, right = forces[1], forces[sh.tiles - 1]
+    for q in range(19):
+        at = pl.ds(sh.section + sh.levels + q // per * xs, xs)
+        shift = (q % per) * sh.levels
+        a = pltpu.roll(left[at, :], (LANES - shift) % LANES, 1)
+        b = pltpu.roll(right[at, :], (LANES + sh.levels - shift) % LANES, 1)
+        ghost.append(jnp.where(lanes < sh.levels, a, jnp.where(lanes < 2 * sh.levels, b, 1.0)))
+    posted = collide(ghost, ghost_force, SIDEWAYS)
+    for k, q in enumerate(SIDEWAYS):
+        value = posted[q]
+        if DIRS[q][0]:
+            value = pltpu.roll(value, DIRS[q][0] % xs, 0)
+        ghost_posts[k] = value
+
+    def plane(k, carry):
+        key = plan[k]
+
+        @pl.when(key >= 0)
+        def _():
+            x = lax.rem(key, xs)
+            here = plane_of(sh, f, x, low, high)
+            force = [field[axis, pl.ds(x, sh.levels, stride=xs), :] for axis in range(3)]
+            post = collide(here, force, range(19))
+            rows = sh.levels - 1
+            for q in range(19):
+                dx, dy, dz = DIRS[q]
+                value = post[q]
+                moved = pltpu.roll(value, dy % LANES, 1) if dy else value
+
+                def put(dx=dx, dz=dz, q=q, moved=moved):
+                    if dz == 0:
+                        out[q, pl.ds(x + dx, sh.levels, stride=xs), :] = moved
+                    elif dz == 1:
+                        out[q, pl.ds(x + dx + xs, rows, stride=xs), :] = moved[:rows]
+                    else:
+                        out[q, pl.ds(x + dx, rows, stride=xs), :] = moved[1:]
+
+                if dx:
+                    pl.when(x != (xs - 1 if dx == 1 else 0))(put)
+                else:
+                    put()
+                if dz == 1:
+                    out[OPPOSITE[q], pl.ds(x + rows * xs, 1), :] = value[rows:]
+                elif dz == -1:
+                    out[OPPOSITE[q], pl.ds(x, 1), :] = value[:1]
+
+        return carry
+
+    lax.fori_loop(0, sh.tiles * sh.slots, plane, 0)
+
+    for k, q in enumerate(SIDEWAYS):
+        dy, dz = DIRS[q][1:]
+        for z in range(sh.levels):
+            if not 0 <= z - dz < sh.levels:
+                continue
+            at = pl.ds(z * xs, xs)
+            value = out[q, at, :]
+            if dy == 1:
+                other = pltpu.roll(ghost_posts[k], (LANES - z + dz) % LANES, 1)
+                value = jnp.where(lanes == 0, other, value)
+            else:
+                other = pltpu.roll(ghost_posts[k], LANES - 1 - sh.levels - z + dz, 1)
+                value = jnp.where(lanes == LANES - 1, other, value)
+            out[q, at, :] = value
+    if last:
+        copy = pltpu.make_async_copy(out, refs[sh.tiles + 2], sem)
+        copy.start()
+        copy.wait()
+
+
+def do_patch(sh, last, plan, f, edges, forces, bulk):
+    out_shape = [pltpu.VMEM(bulk.shape, F32)]
+    if last:
+        out_shape.append(jax.ShapeDtypeStruct(bulk.shape, F32))
+    return pl.pallas_call(
+        lambda *refs: patch_kernel(sh, bool(edges), last, *refs),
+        out_shape=out_shape,
+        in_specs=[SM] + [VM] * (2 + len(edges) + sh.tiles),
+        out_specs=[VM] + [HB] * last,
         scratch_shapes=[
             pltpu.VMEM((3, sh.levels * sh.xs, LANES), F32),
             pltpu.VMEM((len(SIDEWAYS), sh.xs, LANES), F32),
+            pltpu.SemaphoreType.DMA,
         ],
+        input_output_aliases={2 + len(edges) + sh.tiles: 0},
         compiler_params=PARAMS,
-        name="collide",
-    )(plan, f, *edges, *columns, *forces)
-
-
-def finish_kernel(sh, kept, low, high, f_old, f, merged, sem):
+        name="patch",
+    )(plan, f, *edges, *forces, bulk)
+
+
+def finish_kernel(sh, held, low, high, f_old, f, merged, sem):
     del f_old
     rows = iota((8, LANES), 0)
     copies = []
     for side, dirs, edge in ((0, PLUS, low), (1, MINUS, high)):
         at_row = 0 if side == 0 else 7
+        first = 0 if side == 0 else sh.xs - 8
         for k, q in enumerate(dirs):
             index = side * len(PLUS) + k
             for z in range(sh.levels):
-                value = kept[index, z]
+                value = held[q, z * sh.xs + first : z * sh.xs + first + 8, :]
                 blocked = (DIRS[q][2] == 1 and z == 0) or (
                     DIRS[q][2] == -1 and z == sh.levels - 1
                 )
                 if not blocked:
                     value = jnp.where(rows == at_row, edge[k, z : z + 1, :], value)
                 merged[index, z] = value
-            first = 0 if side == 0 else sh.xs - 8
             copy = pltpu.make_async_copy(
                 merged.at[index], f.at[q, :, first : first + 8, :], sem.at[index]
             )
@@ -852,7 +938,7 @@
         copy.wait()
 
 
-def finish(sh, f, kept, edges):
+def finish(sh, held, f, edges):
     f = f.reshape(19, sh.levels, sh.xs, LANES)
     return pl.pallas_call(
         lambda *refs: finish_kernel(sh, *refs),
@@ -866,30 +952,19 @@
         input_output_aliases={3: 0},
         compiler_params=PARAMS,
         name="finish",
-    )(kept, *edges, f)
-
-
-def output_kernel(sh, plan, loads, filt, loads_out, filt_out):
-    for slot in range(sh.slots):
-        used = plan[sh.tiles * sh.slots + slot] >= 0
-        for source, target in ((loads, loads_out), (filt, filt_out)):
-            for axis in range(3):
-                for group in range(sh.groups):
-                    row = slot * sh.groups + group
-                    value = jnp.where(used, source[axis, row : row + 1, :], 0.0)
-                    target[slot, axis : axis + 1, group * LANES : (group + 1) * LANES] = value
-
-
-def make_outputs(sh, plan, loads, filt):
-    shape = jax.ShapeDtypeStruct((sh.slots, 3, sh.markers), F32)
-    return pl.pallas_call(
-        lambda *refs: output_kernel(sh, *refs),
-        out_shape=[shape, shape],
-        in_specs=[SM, VM, VM],
-        out_specs=[VM, VM],
-        compiler_params=PARAMS,
-        name="outputs",
-    )(plan, loads, filt)
+    )(held, *edges, f)
+
+
+def by_group(sh, x):
+    head = x.shape[:-2]
+    x = x.reshape(*head, sh.slots, sh.groups, LANES)
+    return jnp.swapaxes(x, -3, -2).reshape(*head, sh.slots * sh.groups, LANES)
+
+
+def by_slot(sh, x):
+    head = x.shape[:-2]
+    x = x.reshape(*head, sh.groups, sh.slots, LANES)
+    return jnp.swapaxes(x, -3, -2).reshape(*head, sh.slots, sh.markers)
 
 
 def shifted(x, axis, by):
@@ -909,56 +984,50 @@
     filt_in,
 ):
     sh = Shape(f_in, rotor_place, marker_cell, pitch_phase, filt_in)
-    f = in_vmem(f_in.reshape(19, sh.levels * sh.xs, LANES))
-    plan = in_smem(make_plan(sh, rotor_place))
+    plan, f, sections = start(sh, rotor_place, f_in)
+    area, twist, speed, angle = [
+        by_group(sh, x[0, 0]) for x in (blade_area, blade_twist, blade_speed, blade_angle)
+    ]
+    filt = by_group(sh, jnp.swapaxes(filt_in[0, 0], 0, 1))
     edges = ()
-    filt = None
     for step in range(sh.steps):
         last = step == sh.steps - 1
-        sections = make_sections(sh, plan, f, edges)
+        if step:
+            sections = make_sections(sh, plan, f, edges)
         sections = [sections[0]] + [
             shifted(sections[by], "gy", by) for by in range(1, sh.tiles)
         ]
-        columns = make_columns(sh, f, edges)
-        columns = (shifted(columns[1], "gy", 1), shifted(columns[0], "gy", -1))
+        columns = [in_vmem(column) for column in make_columns(sh, f, edges)]
         if step == 0:
-            across, upward, info = make_tables(sh, plan, marker_cell)
-            across, upward, info = in_vmem(across), in_vmem(upward), in_smem(info)
-            blades, filt = make_blades(
-                sh,
-                plan,
-                pitch_phase,
-                blade_area[0, 0],
-                blade_twist[0, 0],
-                blade_speed[0, 0],
-                blade_angle[0, 0],
-                filt_in[0, 0],
-            )
-            blades = in_vmem(blades)
+            blades = in_vmem(make_blades(sh, plan, pitch_phase, twist, angle, columns[0]))
+            tables = make_tables(sh, plan, marker_cell, blades)
         filt, loads, forces = do_markers(
             sh,
             step,
             plan,
-            info,
-            across,
-            upward,
+            tables,
+            (area, speed),
             blades,
-            in_vmem(filt),
+            filt,
+            columns,
             [in_vmem(section) for section in sections],
         )
         forces = [forces[0]] + [shifted(forces[by], "gy", by) for by in range(1, sh.tiles)]
         forces = [in_vmem(force) for force in forces]
-        columns = [in_vmem(column) for column in columns]
-        sent = make_edges(sh, plan, f, edges, columns, forces)
-        new_edges = (shifted(sent[0], "gx", 1), shifted(sent[1], "gx", -1))
-        done = do_collide(sh, last, plan, f, edges, columns, forces)
-        edges = tuple(in_vmem(edge) for edge in new_edges)
+        bulk = do_bulk(sh, last, plan, f, edges, loads, filt)
         if last:
-            f = finish(sh, done[0], in_vmem(done[1]), edges)
-        else:
-            f = in_vmem(done[0])
-    loads_out, filt_out = make_outputs(sh, plan, in_vmem(loads), in_vmem(filt))
-    return f, loads_out[None, None], filt_out[None, None]
+            loads_out, filt_out = bulk[1:]
+        bulk = in_vmem(bulk[0])
+        sent = make_edges(sh, plan, f, edges, forces, bulk)
+        arrived = [shifted(sent[0], "gx", 1), shifted(sent[1], "gx", -1)]
+        done = do_patch(sh, last, plan, f, edges, forces, bulk)
+        edges = tuple(in_vmem(edge) for edge in arrived)
+        f = in_vmem(done[0])
+    f = finish(sh, f, done[1], edges)
+    loads_out, filt_out = [
+        jnp.swapaxes(by_slot(sh, x), 0, 1)[None, None] for x in (loads_out, filt_out)
+    ]
+    return f, loads_out, filt_out
 
 
 def solution(mesh):

time: 96.6 us -> 68.5 us (0.71)
  starting transfers between devices: 53.6 us -> 20.8 us
  Pallas kernels: 19.3 us -> 40.5 us
  local copies, waits for them, and re-layouts: 16.5 us -> 2.41 us
  waiting for transfers between devices: 5.68 us -> 3.65 us
    ppermute x20 -> x16, starting transfers between devices: 53.6 us -> 20.8 us  [shifted(): return lax.ppermute(x, axis, [(i, (i + by) % count) for i in range(count)])]
    unnamed x35 -> x18, local copies, waits for them, and re-layouts: 16.5 us -> 2.41 us
    pallas_call x2, Pallas kernels: 1.35 us -> 12 us  [do_markers(): pl.pallas_call(lambda *refs: marker_kernel(sh, step, *refs), out_shape=[d...]
    pallas_call x1, Pallas kernels: 0.07 us -> 6.11 us  [make_tables(): pl.pallas_call(lambda *refs: table_kernel(sh, *refs), out_shape=[pltpu.VM...]
    pallas_call x7, Pallas kernels: 12.8 us -> 17.4 us  [the longest x2 9.36 us: do_patch(): pl.pallas_call(lambda *refs: patch_kernel(sh, bool(edges), last, *refs),...]
    ppermute x20 -> x16, waiting for transfers between devices: 5.68 us -> 3.65 us  [shifted(): return lax.ppermute(x, axis, [(i, (i + by) % count) for i in range(count)])]
  transfers between devices with their start and end apart: 20 -> 16, of which waited for: 4 -> 3; matrix products, arithmetic and copies ran while one was open for 2% -> 0% of each run, Pallas kernels for 14% -> 36%
where the time goes in v2:
time: 68.5 us
  Pallas kernels  40.5 us (59%)
  starting transfers between devices  20.8 us (30%)
  waiting for transfers between devices  3.65 us (5%)
  local copies, waits for them, and re-layouts  2.41 us (4%)
  between operations  1.07 us (2%)
    ppermute x16, starting transfers between devices, shifted(): return lax.ppermute(x, axis, [(i, (i + by) % count) for i in range(count)])  20.8 us
    pallas_call x2, Pallas kernels, do_markers(): pl.pallas_call(lambda *refs: marker_kernel(sh, step, *refs), out_shape=[d...  12 us
    pallas_call x2, Pallas kernels, do_patch(): pl.pallas_call(lambda *refs: patch_kernel(sh, bool(edges), last, *refs),...  9.36 us
    pallas_call x1, Pallas kernels, make_tables(): pl.pallas_call(lambda *refs: table_kernel(sh, *refs), out_shape=[pltpu.VM...  6.11 us
    pallas_call x2, Pallas kernels, do_bulk(): pl.pallas_call(lambda *refs: bulk_kernel(sh, bool(edges), last, *refs), o...  4.69 us
    ppermute x16, waiting for transfers between devices, shifted(): return lax.ppermute(x, axis, [(i, (i + by) % count) for i in range(count)])  3.65 us
    pallas_call x2, Pallas kernels, make_columns(): pl.pallas_call(lambda *refs: column_kernel(sh, bool(edges), *refs), out_s...  3.17 us
    unnamed x18, local copies, waits for them, and re-layouts  2.41 us
  transfers between devices with their start and end apart: 16, of which 3 were waited for; matrix products, arithmetic and copies ran while one was open for 0% of the time, Pallas kernels for 36%

profile of v2, /device:TPU:0, one launch (start us, length us, event | category | flops | bytes accessed | tf_op | source)
XLA Modules:
  0.0 68.5 jit_solution(14692175272454056480)
XLA Ops:
  0.6 1.7 %copy-done = f32[19,16,16,128]{3,2,1,0:T(8,128)S(1)} copy-done((f32[19,16,16,128]{3,2,1,0:T(8,128)S(1)}, f32[19,16,16,128]{3,2,1,0:T(8,128)}, u32[]{:S(2)}) %copy-start) | copy-done | bytes 2490392
  3.0 1.3 %start.1 = (s32[8]{0:T(128)S(4)}, f32[19,256,128]{2,1,0:T(8,128)S(1)}, f32[96,128]{1,0:T(8,128)S(1)}, f32[96,128]{1,0:T(8,128)S(1)}, f32[96,128]{1,0:T(8,128)S(1)}, /*index=5*/f32[96,128]{1,0:T(8,128)S(1)}) custom-call(s32[3,40]{1,0:T(4,128)S(1)} %bitcast.59, f32[19,256,128]{2,1,0:T(8,128)S(1)} %bitcast.51), custom_call_target="tpu_custom_call" | custom-call | tf_op jit(solution)/shard_map/start/pallas_call | solution.py:238
  4.8 2.6 %collective-permute-start.1 = (f32[96,128]{1,0:T(8,128)S(1)}, f32[96,128]{1,0:T(8,128)S(1)}, u32[]{:S(2)}, u32[]{:S(2)}) collective-permute-start(f32[96,128]{1,0:T(8,128)S(1)} %get-tuple-element.50), channel_id=1, source_target_pairs={{0,2},{1,3},{2,0},{3,1},{4,6},{5,7},{6,4},{7,5},{8,10},{9,11},{10,... | collective-permute-start | bytes 147464 | tf_op jit(solution)/shard_map/ppermute | solution.py:972
  7.4 1.4 %collective-permute-start.2 = (f32[96,128]{1,0:T(8,128)S(1)}, f32[96,128]{1,0:T(8,128)S(1)}, u32[]{:S(2)}, u32[]{:S(2)}) collective-permute-start(f32[96,128]{1,0:T(8,128)S(1)} %get-tuple-element.51), channel_id=1, source_target_pairs={{0,3},{1,0},{2,1},{3,2},{4,7},{5,4},{6,5},{7,6},{8,11},{9,8},{10,9... | collective-permute-start | bytes 147464 | tf_op jit(solution)/shard_map/ppermute | solution.py:972
  8.8 1.6 %columns.2 = (f32[64,128]{1,0:T(8,128)S(1)}, f32[64,128]{1,0:T(8,128)S(1)}) custom-call(f32[19,256,128]{2,1,0:T(8,128)S(1)} %get-tuple-element.42.refs_0_.refs_1_), custom_call_target="tpu_custom_call" | custom-call | tf_op jit(solution)/shard_map/columns/pallas_call | solution.py:310
  10.4 1.3 %blades.1.refs_2_.refs_6_ = f32[6,128,128]{2,1,0:T(8,128)S(1)} custom-call(s32[8]{0:T(128)S(4)} %get-tuple-element.41.refs_0_.plan, s32[2,40]{1,0:T(2,128)S(1)} %bitcast.60, f32[128,128]{1,0:T(8,128)S(1)} %bitcast.57, f32[128,128]{1,0:T(8,128)S(1)} %bitcast.58, f32[64,128]{1,0:T(8,128)S(1)} %get-tuple-element.43.refs_4_.refs_8_), custom_call_target="tpu_custom_call" | custom-call | tf_op jit(solution)/shard_map/blades/pallas_call | solution.py:452
  11.8 6.1 %tables.1 = (bf16[2,2,256,8192]{3,2,1,0:T(8,128)(2,1)S(1)}, f32[2,16,8192]{2,1,0:T(8,128)S(1)}, s32[4]{0:T(128)S(4)}) custom-call(s32[8]{0:T(128)S(4)} %get-tuple-element.41.refs_0_.plan, s32[40,8192]{1,0:T(8,128)S(1)} %copy-done.1, f32[6,128,128]{2,1,0:T(8,128)S(1)} %blades.1.refs_2_.refs_6_), custom_call_target="tpu_custom_call" | custom-call | tf_op jit(solution)/shard_map/tables/pallas_call | solution.py:402
  18.0 6.0 %markers.2 = (f32[3,128,128]{2,1,0:T(8,128)S(1)}, f32[3,128,128]{2,1,0:T(8,128)S(1)}, f32[112,128]{1,0:T(8,128)S(1)}, f32[176,128]{1,0:T(8,128)S(1)}, f32[112,128]{1,0:T(8,128)S(1)}, /*index=5*/f32[176,128]{1,0:T(8,128)S(1)}) custom-call(s32[8]{0:T(128)S(4)} %get-tuple-element.41.refs_0_.plan, s32[4]{0:T(128)S(4)} %get-tuple-element.44.refs_1_, ...), custom_call_target="tpu_custom_call" | custom-call | tf_op jit(solution)/shard_map/markers/pallas_call | solution.py:626
  24.0 1.7 %collective-permute-start.5 = (f32[176,128]{1,0:T(8,128)S(1)}, f32[176,128]{1,0:T(8,128)S(1)}, u32[]{:S(2)}, u32[]{:S(2)}) collective-permute-start(f32[176,128]{1,0:T(8,128)S(1)} %get-tuple-element.55), channel_id=1, source_target_pairs={{0,3},{1,0},{2,1},{3,2},{4,7},{5,4},{6,5},{7,6},{8,11},{9,8},{10,9... | collective-permute-start | bytes 270344 | tf_op jit(solution)/shard_map/ppermute | solution.py:972
  25.8 2.0 %bulk.2.refs_6_ = f32[19,256,128]{2,1,0:T(8,128)S(1)} custom-call(s32[8]{0:T(128)S(4)} %get-tuple-element.41.refs_0_.plan, f32[19,256,128]{2,1,0:T(8,128)S(1)} %get-tuple-element.42.refs_0_.refs_1_, f32[3,128,128]{2,1,0:T(8,128)S(1)} %get-tuple-element.56.refs_2_, f32[3,128,128]{2,1,0:T(8,128)S(1)} %get-tuple-element.57.refs_3_.refs_7_), custom_call_target="tpu_custom_call" | custom-call | tf_op jit(solution)/shard_map/bulk/pallas_call | solution.py:771
  27.8 2.1 %collective-permute-done.4.refs_4_ = f32[112,128]{1,0:T(8,128)S(1)} collective-permute-done((f32[112,128]{1,0:T(8,128)S(1)}, f32[112,128]{1,0:T(8,128)S(1)}, u32[]{:S(2)}, u32[]{:S(2)}) %collective-permute-start.4) | collective-permute-done | bytes 57376 | tf_op jit(solution)/shard_map/ppermute | solution.py:972
  30.4 1.0 %collective-permute-start.6 = (f32[5,16,128]{2,1,0:T(8,128)S(1)}, f32[5,16,128]{2,1,0:T(8,128)S(1)}, u32[]{:S(2)}, u32[]{:S(2)}) collective-permute-start(f32[5,16,128]{2,1,0:T(8,128)S(1)} %get-tuple-element.58), channel_id=1, source_target_pairs={{0,4},{4,8},{8,12},{12,16},{16,20},{20,24},{24,28},{28,0},{1,5},{5... | collective-permute-start | bytes 122888 | tf_op jit(solution)/shard_map/ppermute | solution.py:972
  31.5 3.7 %collective-permute-start.7 = (f32[5,16,128]{2,1,0:T(8,128)S(1)}, f32[5,16,128]{2,1,0:T(8,128)S(1)}, u32[]{:S(2)}, u32[]{:S(2)}) collective-permute-start(f32[5,16,128]{2,1,0:T(8,128)S(1)} %get-tuple-element.59), channel_id=1, source_target_pairs={{0,28},{4,0},{8,4},{12,8},{16,12},{20,16},{24,20},{28,24},{1,29},{... | collective-permute-start | bytes 122888 | tf_op jit(solution)/shard_map/ppermute | solution.py:972
  35.2 3.9 %patch.2.refs_0_.f.refs_1_ = f32[19,256,128]{2,1,0:T(8,128)S(1)} custom-call(s32[8]{0:T(128)S(4)} %get-tuple-element.41.refs_0_.plan, f32[19,256,128]{2,1,0:T(8,128)S(1)} %get-tuple-element.42.refs_0_.refs_1_, f32[112,128]{1,0:T(8,128)S(1)} %get-tuple-element.52.refs_2_, ...), custom_call_target="tpu_custom_call", output_to_operand_aliasing={{}: (6, {})} | custom-call | tf_op jit(solution)/shard_map/patch/pallas_call | solution.py:899
  40.0 1.1 %collective-permute-start.9 = (f32[96,128]{1,0:T(8,128)S(1)}, f32[96,128]{1,0:T(8,128)S(1)}, u32[]{:S(2)}, u32[]{:S(2)}) collective-permute-start(f32[96,128]{1,0:T(8,128)S(1)} %get-tuple-element.64), channel_id=1, source_target_pairs={{0,2},{1,3},{2,0},{3,1},{4,6},{5,7},{6,4},{7,5},{8,10},{9,11},{10,... | collective-permute-start | bytes 147464 | tf_op jit(solution)/shard_map/ppermute | solution.py:972
  41.1 1.4 %collective-permute-start.10 = (f32[96,128]{1,0:T(8,128)S(1)}, f32[96,128]{1,0:T(8,128)S(1)}, u32[]{:S(2)}, u32[]{:S(2)}) collective-permute-start(f32[96,128]{1,0:T(8,128)S(1)} %get-tuple-element.65), channel_id=1, source_target_pairs={{0,3},{1,0},{2,1},{3,2},{4,7},{5,4},{6,5},{7,6},{8,11},{9,8},{10,9... | collective-permute-start | bytes 147464 | tf_op jit(solution)/shard_map/ppermute | solution.py:972
  42.5 1.6 %columns.3 = (f32[64,128]{1,0:T(8,128)S(1)}, f32[64,128]{1,0:T(8,128)S(1)}) custom-call(f32[19,256,128]{2,1,0:T(8,128)S(1)} %patch.2.refs_0_.f.refs_1_, f32[5,16,128]{2,1,0:T(8,128)S(1)} %collective-permute-done.6.refs_1_.low.refs_2_, f32[5,16,128]{2,1,0:T(8,128)S(1)} %collective-permute-done.7.refs_2_.high.refs_3_), custom_call_target="tpu_custom_call" | custom-call | tf_op jit(solution)/shard_map/columns/pallas_call | solution.py:310
  44.6 6.0 %markers.3 = (f32[3,128,128]{2,1,0:T(8,128)S(1)}, f32[3,128,128]{2,1,0:T(8,128)S(1)}, f32[112,128]{1,0:T(8,128)S(1)}, f32[176,128]{1,0:T(8,128)S(1)}, f32[112,128]{1,0:T(8,128)S(1)}, /*index=5*/f32[176,128]{1,0:T(8,128)S(1)}) custom-call(s32[8]{0:T(128)S(4)} %get-tuple-element.41.refs_0_.plan, s32[4]{0:T(128)S(4)} %get-tuple-element.44.refs_1_, ...), custom_call_target="tpu_custom_call" | custom-call | tf_op jit(solution)/shard_map/markers/pallas_call | solution.py:626
  51.4 1.0 %collective-permute-start.13 = (f32[176,128]{1,0:T(8,128)S(1)}, f32[176,128]{1,0:T(8,128)S(1)}, u32[]{:S(2)}, u32[]{:S(2)}) collective-permute-start(f32[176,128]{1,0:T(8,128)S(1)} %get-tuple-element.69), channel_id=1, source_target_pairs={{0,3},{1,0},{2,1},{3,2},{4,7},{5,4},{6,5},{7,6},{8,11},{9,8},{10,9... | collective-permute-start | bytes 270344 | tf_op jit(solution)/shard_map/ppermute | solution.py:972
  53.1 2.7 %bulk.3 = (f32[19,256,128]{2,1,0:T(8,128)S(1)}, f32[3,128,128]{2,1,0:T(8,128)}, f32[3,128,128]{2,1,0:T(8,128)}) custom-call(s32[8]{0:T(128)S(4)} %get-tuple-element.41.refs_0_.plan, f32[19,256,128]{2,1,0:T(8,128)S(1)} %patch.2.refs_0_.f.refs_1_, f32[5,16,128]{2,1,0:T(8,128)S(1)} %collective-permute-done.6.refs_1_.low.refs_2_, ...), custom_call_target="tpu_custom_call" | custom-call | tf_op jit(solution)/shard_map/bulk/pallas_call | solution.py:771
  55.7 1.0 %collective-permute-done.12.refs_6_ = f32[112,128]{1,0:T(8,128)S(1)} collective-permute-done((f32[112,128]{1,0:T(8,128)S(1)}, f32[112,128]{1,0:T(8,128)S(1)}, u32[]{:S(2)}, u32[]{:S(2)}) %collective-permute-start.12) | collective-permute-done | bytes 57376 | tf_op jit(solution)/shard_map/ppermute | solution.py:972
  57.2 4.7 %collective-permute-start.15 = (f32[5,16,128]{2,1,0:T(8,128)S(1)}, f32[5,16,128]{2,1,0:T(8,128)S(1)}, u32[]{:S(2)}, u32[]{:S(2)}) collective-permute-start(f32[5,16,128]{2,1,0:T(8,128)S(1)} %get-tuple-element.75), channel_id=1, source_target_pairs={{0,28},{4,0},{8,4},{12,8},{16,12},{20,16},{24,20},{28,24},{1,29},{... | collective-permute-start | bytes 122888 | tf_op jit(solution)/shard_map/ppermute | solution.py:972
  62.0 5.4 %patch.3 = (f32[19,256,128]{2,1,0:T(8,128)S(1)}, f32[19,256,128]{2,1,0:T(8,128)}) custom-call(s32[8]{0:T(128)S(4)} %get-tuple-element.41.refs_0_.plan, f32[19,256,128]{2,1,0:T(8,128)S(1)} %patch.2.refs_0_.f.refs_1_, f32[5,16,128]{2,1,0:T(8,128)S(1)} %collective-permute-done.6.refs_1_.low.refs_2_, ...), custom_call_target="tpu_custom_call", output_to_operand_aliasing={{0}: (8, {})} | custom-call | tf_op jit(solution)/shard_map/patch/pallas_call | solution.py:899
  67.4 0.9 %finish.1 = f32[19,16,16,128]{3,2,1,0:T(8,128)} custom-call(f32[19,256,128]{2,1,0:T(8,128)S(1)} %get-tuple-element.73.refs_0_, f32[5,16,128]{2,1,0:T(8,128)S(1)} %collective-permute-done.14.refs_1_, f32[5,16,128]{2,1,0:T(8,128)S(1)} %collective-permute-done.15.refs_2_, f32[19,16,16,128]{3,2,1,0:T(8,128)} %bitcast.61), custom_call_target="tpu_custom_call", output_to_operand_aliasing={{}: (3, {})} | custom-call | tf_op jit(solution)/shard_map/finish/pallas_call | solution.py:943
  (41 shorter events, 5.1 us)
Async XLA Ops:
  0.6 1.7 %copy-start = (f32[19,16,16,128]{3,2,1,0:T(8,128)S(1)}, f32[19,16,16,128]{3,2,1,0:T(8,128)}, u32[]{:S(2)}) copy-start(f32[19,16,16,128]{3,2,1,0:T(8,128)} %param.9) | copy-start | bytes 7471108
  3.0 7.4 %copy-start.5 = (f32[1,1,2,8192]{3,2,1,0:T(2,128)S(1)}, f32[1,1,2,8192]{3,2,1,0:T(2,128)}, u32[]{:S(2)}) copy-start(f32[1,1,2,8192]{3,2,1,0:T(2,128)} %param.14) | copy-start | bytes 196612
  3.0 7.4 %copy-start.6 = (f32[1,1,2,8192]{3,2,1,0:T(2,128)S(1)}, f32[1,1,2,8192]{3,2,1,0:T(2,128)}, u32[]{:S(2)}) copy-start(f32[1,1,2,8192]{3,2,1,0:T(2,128)} %param.16) | copy-start | bytes 196612
  3.0 7.4 %copy-start.8 = (s32[40,2]{0,1:T(2,128)S(1)}, s32[40,2]{0,1:T(2,128)}, u32[]{:S(2)}) copy-start(s32[40,2]{0,1:T(2,128)} %param.12) | copy-start | bytes 964
  3.0 8.8 %copy-start.1 = (s32[40,8192]{1,0:T(8,128)S(1)}, s32[40,8192]{1,0:T(8,128)}, u32[]{:S(2)}) copy-start(s32[40,8192]{1,0:T(8,128)} %refs_1_.1) | copy-start | bytes 3932164
  4.3 13.6 %copy-start.2 = (f32[1,1,2,8192]{3,2,1,0:T(2,128)S(1)}, f32[1,1,2,8192]{3,2,1,0:T(2,128)}, u32[]{:S(2)}) copy-start(f32[1,1,2,8192]{3,2,1,0:T(2,128)} %param.13) | copy-start | bytes 196612
  4.3 13.6 %copy-start.3 = (f32[1,1,2,8192]{3,2,1,0:T(2,128)S(1)}, f32[1,1,2,8192]{3,2,1,0:T(2,128)}, u32[]{:S(2)}) copy-start(f32[1,1,2,8192]{3,2,1,0:T(2,128)} %param.15) | copy-start | bytes 196612
  4.3 13.6 %copy-start.4 = (f32[1,1,2,3,8192]{4,2,3,1,0:T(2,128)S(1)}, f32[1,1,2,3,8192]{4,2,3,1,0:T(2,128)}, u32[]{:S(2)}) copy-start(f32[1,1,2,3,8192]{4,2,3,1,0:T(2,128)} %param.17) | copy-start | bytes 589828
  4.3 13.6 %collective-permute-start = (f32[96,128]{1,0:T(8,128)S(1)}, f32[96,128]{1,0:T(8,128)S(1)}, u32[]{:S(2)}, u32[]{:S(2)}) collective-permute-start(f32[96,128]{1,0:T(8,128)S(1)} %get-tuple-element.49), channel_id=1, source_target_pairs={{0,1},{1,2},{2,3},{3,0},{4,5},{5,6},{6,7},{7,4},{8,9},{9,10},{10,1... | collective-permute-start | bytes 147464 | tf_op jit(solution)/shard_map/ppermute | solution.py:972
  4.8 13.1 %collective-permute-start.1 = (f32[96,128]{1,0:T(8,128)S(1)}, f32[96,128]{1,0:T(8,128)S(1)}, u32[]{:S(2)}, u32[]{:S(2)}) collective-permute-start(f32[96,128]{1,0:T(8,128)S(1)} %get-tuple-element.50), channel_id=1, source_target_pairs={{0,2},{1,3},{2,0},{3,1},{4,6},{5,7},{6,4},{7,5},{8,10},{9,11},{10,... | collective-permute-start | bytes 147464 | tf_op jit(solution)/shard_map/ppermute | solution.py:972
  7.4 10.5 %collective-permute-start.2 = (f32[96,128]{1,0:T(8,128)S(1)}, f32[96,128]{1,0:T(8,128)S(1)}, u32[]{:S(2)}, u32[]{:S(2)}) collective-permute-start(f32[96,128]{1,0:T(8,128)S(1)} %get-tuple-element.51), channel_id=1, source_target_pairs={{0,3},{1,0},{2,1},{3,2},{4,7},{5,4},{6,5},{7,6},{8,11},{9,8},{10,9... | collective-permute-start | bytes 147464 | tf_op jit(solution)/shard_map/ppermute | solution.py:972
  24.0 6.0 %collective-permute-start.3 = (f32[176,128]{1,0:T(8,128)S(1)}, f32[176,128]{1,0:T(8,128)S(1)}, u32[]{:S(2)}, u32[]{:S(2)}) collective-permute-start(f32[176,128]{1,0:T(8,128)S(1)} %get-tuple-element.53), channel_id=1, source_target_pairs={{0,1},{1,2},{2,3},{3,0},{4,5},{5,6},{6,7},{7,4},{8,9},{9,10},{10,1... | collective-permute-start | bytes 270344 | tf_op jit(solution)/shard_map/ppermute | solution.py:972
  24.0 5.9 %collective-permute-start.5 = (f32[176,128]{1,0:T(8,128)S(1)}, f32[176,128]{1,0:T(8,128)S(1)}, u32[]{:S(2)}, u32[]{:S(2)}) collective-permute-start(f32[176,128]{1,0:T(8,128)S(1)} %get-tuple-element.55), channel_id=1, source_target_pairs={{0,3},{1,0},{2,1},{3,2},{4,7},{5,4},{6,5},{7,6},{8,11},{9,8},{10,9... | collective-permute-start | bytes 270344 | tf_op jit(solution)/shard_map/ppermute | solution.py:972
  25.8 4.2 %collective-permute-start.4 = (f32[112,128]{1,0:T(8,128)S(1)}, f32[112,128]{1,0:T(8,128)S(1)}, u32[]{:S(2)}, u32[]{:S(2)}) collective-permute-start(f32[112,128]{1,0:T(8,128)S(1)} %get-tuple-element.54), channel_id=1, source_target_pairs={{0,2},{1,3},{2,0},{3,1},{4,6},{5,7},{6,4},{7,5},{8,10},{9,11},{10,... | collective-permute-start | bytes 172040 | tf_op jit(solution)/shard_map/ppermute | solution.py:972
  30.4 8.7 %collective-permute-start.6 = (f32[5,16,128]{2,1,0:T(8,128)S(1)}, f32[5,16,128]{2,1,0:T(8,128)S(1)}, u32[]{:S(2)}, u32[]{:S(2)}) collective-permute-start(f32[5,16,128]{2,1,0:T(8,128)S(1)} %get-tuple-element.58), channel_id=1, source_target_pairs={{0,4},{4,8},{8,12},{12,16},{16,20},{20,24},{24,28},{28,0},{1,5},{5... | collective-permute-start | bytes 122888 | tf_op jit(solution)/shard_map/ppermute | solution.py:972
  31.5 7.7 %collective-permute-start.7 = (f32[5,16,128]{2,1,0:T(8,128)S(1)}, f32[5,16,128]{2,1,0:T(8,128)S(1)}, u32[]{:S(2)}, u32[]{:S(2)}) collective-permute-start(f32[5,16,128]{2,1,0:T(8,128)S(1)} %get-tuple-element.59), channel_id=1, source_target_pairs={{0,28},{4,0},{8,4},{12,8},{16,12},{20,16},{24,20},{28,24},{1,29},{... | collective-permute-start | bytes 122888 | tf_op jit(solution)/shard_map/ppermute | solution.py:972
  39.9 4.2 %collective-permute-start.8 = (f32[96,128]{1,0:T(8,128)S(1)}, f32[96,128]{1,0:T(8,128)S(1)}, u32[]{:S(2)}, u32[]{:S(2)}) collective-permute-start(f32[96,128]{1,0:T(8,128)S(1)} %get-tuple-element.63), channel_id=1, source_target_pairs={{0,1},{1,2},{2,3},{3,0},{4,5},{5,6},{6,7},{7,4},{8,9},{9,10},{10,1... | collective-permute-start | bytes 147464 | tf_op jit(solution)/shard_map/ppermute | solution.py:972
  40.0 4.6 %collective-permute-start.9 = (f32[96,128]{1,0:T(8,128)S(1)}, f32[96,128]{1,0:T(8,128)S(1)}, u32[]{:S(2)}, u32[]{:S(2)}) collective-permute-start(f32[96,128]{1,0:T(8,128)S(1)} %get-tuple-element.64), channel_id=1, source_target_pairs={{0,2},{1,3},{2,0},{3,1},{4,6},{5,7},{6,4},{7,5},{8,10},{9,11},{10,... | collective-permute-start | bytes 147464 | tf_op jit(solution)/shard_map/ppermute | solution.py:972
  41.1 3.5 %collective-permute-start.10 = (f32[96,128]{1,0:T(8,128)S(1)}, f32[96,128]{1,0:T(8,128)S(1)}, u32[]{:S(2)}, u32[]{:S(2)}) collective-permute-start(f32[96,128]{1,0:T(8,128)S(1)} %get-tuple-element.65), channel_id=1, source_target_pairs={{0,3},{1,0},{2,1},{3,2},{4,7},{5,4},{6,5},{7,6},{8,11},{9,8},{10,9... | collective-permute-start | bytes 147464 | tf_op jit(solution)/shard_map/ppermute | solution.py:972
  50.5 6.2 %collective-permute-start.11 = (f32[176,128]{1,0:T(8,128)S(1)}, f32[176,128]{1,0:T(8,128)S(1)}, u32[]{:S(2)}, u32[]{:S(2)}) collective-permute-start(f32[176,128]{1,0:T(8,128)S(1)} %get-tuple-element.67), channel_id=1, source_target_pairs={{0,1},{1,2},{2,3},{3,0},{4,5},{5,6},{6,7},{7,4},{8,9},{9,10},{10,1... | collective-permute-start | bytes 270344 | tf_op jit(solution)/shard_map/ppermute | solution.py:972
  51.4 5.4 %collective-permute-start.13 = (f32[176,128]{1,0:T(8,128)S(1)}, f32[176,128]{1,0:T(8,128)S(1)}, u32[]{:S(2)}, u32[]{:S(2)}) collective-permute-start(f32[176,128]{1,0:T(8,128)S(1)} %get-tuple-element.69), channel_id=1, source_target_pairs={{0,3},{1,0},{2,1},{3,2},{4,7},{5,4},{6,5},{7,6},{8,11},{9,8},{10,9... | collective-permute-start | bytes 270344 | tf_op jit(solution)/shard_map/ppermute | solution.py:972
  52.3 4.4 %collective-permute-start.12 = (f32[112,128]{1,0:T(8,128)S(1)}, f32[112,128]{1,0:T(8,128)S(1)}, u32[]{:S(2)}, u32[]{:S(2)}) collective-permute-start(f32[112,128]{1,0:T(8,128)S(1)} %get-tuple-element.68), channel_id=1, source_target_pairs={{0,2},{1,3},{2,0},{3,1},{4,6},{5,7},{6,4},{7,5},{8,10},{9,11},{10,... | collective-permute-start | bytes 172040 | tf_op jit(solution)/shard_map/ppermute | solution.py:972
  57.2 10.2 %collective-permute-start.14 = (f32[5,16,128]{2,1,0:T(8,128)S(1)}, f32[5,16,128]{2,1,0:T(8,128)S(1)}, u32[]{:S(2)}, u32[]{:S(2)}) collective-permute-start(f32[5,16,128]{2,1,0:T(8,128)S(1)} %get-tuple-element.74), channel_id=1, source_target_pairs={{0,4},{4,8},{8,12},{12,16},{16,20},{20,24},{24,28},{28,0},{1,5},{5... | collective-permute-start | bytes 122888 | tf_op jit(solution)/shard_map/ppermute | solution.py:972
  57.2 10.2 %collective-permute-start.15 = (f32[5,16,128]{2,1,0:T(8,128)S(1)}, f32[5,16,128]{2,1,0:T(8,128)S(1)}, u32[]{:S(2)}, u32[]{:S(2)}) collective-permute-start(f32[5,16,128]{2,1,0:T(8,128)S(1)} %get-tuple-element.75), channel_id=1, source_target_pairs={{0,28},{4,0},{8,4},{12,8},{16,12},{20,16},{24,20},{28,24},{1,29},{... | collective-permute-start | bytes 122888 | tf_op jit(solution)/shard_map/ppermute | solution.py:972
  (1 other events, 0.7 us)

commit v3 on v2

--- a/solution.py
+++ b/solution.py
@@ -150,6 +150,10 @@
     return pltpu.with_memory_space_constraint(x, pltpu.VMEM)
 
 
+def in_hbm(x):
+    return pltpu.with_memory_space_constraint(x, pltpu.HBM)
+
+
 def in_smem(x):
     return pltpu.with_memory_space_constraint(x, pltpu.SMEM)
 
@@ -225,96 +229,166 @@
                 outs[shift][at : at + 3 * sh.levels, :] = jnp.zeros((3 * sh.levels, LANES), F32)
 
 
-def start_kernel(sh, place, f_in, plan, f, *refs):
-    outs, sem = refs[:-1], refs[-1]
-    copy = pltpu.make_async_copy(f_in, f, sem)
-    copy.start()
+def sincos(x):
+    turns = jnp.floor(x * (2.0 / math.pi) + 0.5)
+    r = x - turns * 1.5703125
+    r = r - turns * 4.837512969970703125e-4
+    r = r - turns * 7.549789954891882e-8
+    r2 = r * r
+    sin_r = r + r * r2 * (
+        -1.0 / 6 + r2 * (1.0 / 120 + r2 * (-1.0 / 5040 + r2 * (1.0 / 362880)))
+    )
+    cos_r = (
+        1.0
+        - 0.5 * r2
+        + r2
+        * r2
+        * (1.0 / 24 + r2 * (-1.0 / 720 + r2 * (1.0 / 40320 - r2 * (1.0 / 3628800))))
+    )
+    quarter = turns.astype(jnp.int32)
+    swap = (quarter & 1) == 1
+    sin_x = jnp.where(swap, cos_r, sin_r)
+    cos_x = jnp.where(swap, sin_r, cos_r)
+    sin_x = jnp.where((quarter & 2) == 2, -sin_x, sin_x)
+    cos_x = jnp.where(((quarter + 1) & 2) == 2, -cos_x, cos_x)
+    return sin_x, cos_x
+
+
+def write_blades(sh, plan, phases, twist, angle, blades):
+    blades[0], blades[1] = sincos(angle[...])
+    sin_twist, cos_twist = sincos(twist[...])
+    owner = iota((1, LANES), 1)
+    rows = iota((sh.slots * sh.groups, LANES), 0) % sh.slots
+    phase = jnp.zeros((1, LANES), F32)
+    for step in range(sh.steps):
+        for slot in range(sh.slots):
+            rotor = jnp.maximum(rotor_at(sh, plan, slot), 0)
+            here = owner == step * sh.slots + slot
+            phase = jnp.where(here, phases[step, rotor].astype(F32), phase)
+    pitch = PITCH_AMP * sincos((2.0 * math.pi / PHASES) * phase)[0]
+    pitched = sincos(pitch)
+    for step in range(sh.steps):
+        parts = []
+        for part in pitched:
+            total = jnp.zeros((sh.slots * sh.groups, LANES), F32)
+            for slot in range(sh.slots):
+                lane = step * sh.slots + slot
+                total = jnp.where(rows == slot, part[:, lane : lane + 1], total)
+            parts.append(total)
+        blades[2 + 2 * step] = sin_twist * parts[1] + cos_twist * parts[0]
+        blades[3 + 2 * step] = cos_twist * parts[1] - sin_twist * parts[0]
+
+
+def start_kernel(
+    sh, place_in, phases_in, twist_in, angle_in, plan, blades, place, phases, twist, angle, sems
+):
+    pairs = ((place_in, place), (phases_in, phases), (angle_in, angle), (twist_in, twist))
+    copies = [pltpu.make_async_copy(*pair, sems.at[k]) for k, pair in enumerate(pairs)]
+    for copy in copies:
+        copy.start()
+    for copy in copies:
+        copy.wait()
     write_plan(sh, place, plan)
-    copy.wait()
-    write_sections(sh, plan, f, None, None, outs)
-
-
-def start(sh, rotor_place, f_in):
-    out = pl.pallas_call(
+    write_blades(sh, plan, phases, twist, angle, blades)
+
+
+def start(sh, rotor_place, phases, twist, angle):
+    rows = sh.slots * sh.groups
+    plan, blades = pl.pallas_call(
         lambda *refs: start_kernel(sh, *refs),
         out_shape=[
             pltpu.SMEM((sh.tiles * sh.slots,), jnp.int32),
-            pltpu.VMEM((19, sh.levels * sh.xs, LANES), F32),
-        ]
-        + [pltpu.VMEM((sh.section, LANES), F32)] * sh.tiles,
-        in_specs=[VM, HB],
-        out_specs=[SM] + [VM] * (1 + sh.tiles),
-        scratch_shapes=[pltpu.SemaphoreType.DMA],
+            pltpu.VMEM((2 + 2 * sh.steps, rows, LANES), F32),
+        ],
+        in_specs=[HB] * 4,
+        out_specs=[SM, VM],
+        scratch_shapes=[
+            pltpu.VMEM((3, sh.rotors), jnp.int32),
+            pltpu.SMEM((sh.steps, sh.rotors), jnp.int32),
+            pltpu.VMEM((rows, LANES), F32),
+            pltpu.VMEM((rows, LANES), F32),
+            pltpu.SemaphoreType.DMA((4,)),
+        ],
         compiler_params=PARAMS,
         name="start",
-    )(jnp.transpose(rotor_place), f_in.reshape(19, sh.levels * sh.xs, LANES))
-    return in_smem(out[0]), in_vmem(out[1]), out[2:]
-
-
-def make_sections(sh, plan, f, edges):
+    )(
+        in_hbm(jnp.transpose(rotor_place)),
+        in_hbm(jnp.transpose(phases)),
+        in_hbm(twist),
+        in_hbm(angle),
+    )
+    return in_smem(plan), in_vmem(blades)
+
+
+def section_kernel(sh, has_edges, plan, f, *refs):
+    low, high = refs[:2] if has_edges else (None, None)
+    write_sections(sh, plan, f, low, high, refs[-sh.tiles :])
+
+
+def make_sections(sh, plan, f, edges, after):
     return pl.pallas_call(
-        lambda plan, f, low, high, *outs: write_sections(sh, plan, f, low, high, outs),
+        lambda *refs: section_kernel(sh, bool(edges), *refs),
         out_shape=[pltpu.VMEM((sh.section, LANES), F32)] * sh.tiles,
-        in_specs=[SM] + [VM] * 3,
+        in_specs=[SM] + [VM] * (1 + len(edges) + len(after)),
         out_specs=[VM] * sh.tiles,
         compiler_params=PARAMS,
         name="sections",
-    )(plan, f, *edges)
+    )(plan, f, *edges, *after)
 
 
 def column_kernel(sh, has_edges, *refs):
-    f = refs[0]
-    low, high = refs[1:3] if has_edges else (None, None)
-    outs = refs[-2:]
-    lanes = iota((sh.xs, LANES), 1)
+    f = refs[1]
+    low, high = refs[2:4] if has_edges else (None, None)
+    out = refs[-1]
+    pairs = iota((sh.xs, LANES), 1) // 2
     xrows = iota((sh.xs, LANES), 0)
-    per = LANES // sh.levels
+    per = LANES // (2 * sh.levels)
     groups = (19 + per - 1) // per
-    for side, edge in ((0, 0), (1, LANES - 1)):
-        for group in range(groups):
-            total = jnp.zeros((sh.xs, LANES), F32)
-            for q in range(group * per, min(19, (group + 1) * per)):
-                for z in range(sh.levels):
-                    tile = f[q, z * sh.xs : (z + 1) * sh.xs, :]
-                    if has_edges and DIRS[q][0] != 0:
-                        blocked = (DIRS[q][2] == 1 and z == 0) or (
-                            DIRS[q][2] == -1 and z == sh.levels - 1
-                        )
-                        if not blocked:
-                            if DIRS[q][0] == 1:
-                                tile = jnp.where(xrows == 0, low[PLUS.index(q), z : z + 1, :], tile)
-                            else:
-                                tile = jnp.where(
-                                    xrows == sh.xs - 1, high[MINUS.index(q), z : z + 1, :], tile
-                                )
-                    column = jnp.broadcast_to(tile[:, edge : edge + 1], (sh.xs, LANES))
-                    total = jnp.where(lanes == (q % per) * sh.levels + z, column, total)
-            outs[side][group * sh.xs : (group + 1) * sh.xs, :] = total
-    zlanes = iota((sh.levels, LANES), 1)
-    at = groups * sh.xs
-    corners = [jnp.zeros((sh.levels, LANES), F32) for side in range(2)]
+    for group in range(groups):
+        total = jnp.ones((sh.xs, LANES), F32)
+        for q in range(group * per, min(19, (group + 1) * per)):
+            for z in range(sh.levels):
+                tile = f[q, z * sh.xs : (z + 1) * sh.xs, :]
+                if has_edges and DIRS[q][0] != 0:
+                    blocked = (DIRS[q][2] == 1 and z == 0) or (
+                        DIRS[q][2] == -1 and z == sh.levels - 1
+                    )
+                    if not blocked:
+                        if DIRS[q][0] == 1:
+                            tile = jnp.where(xrows == 0, low[PLUS.index(q), z : z + 1, :], tile)
+                        else:
+                            tile = jnp.where(
+                                xrows == sh.xs - 1, high[MINUS.index(q), z : z + 1, :], tile
+                            )
+                pair = (q % per) * sh.levels + z
+                total = jnp.where(
+                    pairs == pair, pltpu.roll(tile, (2 * pair + 1) % LANES, 1), total
+                )
+        out[group * sh.xs : (group + 1) * sh.xs, :] = total
+    zpairs = iota((sh.levels, LANES), 1) // 2
+    corners = jnp.ones((sh.levels, LANES), F32)
     for which, x in ((0, 0), (1, sh.xs - 1)):
         planes = plane_of(sh, f, x, low, high)
         for q in range(19):
-            for side, edge in ((0, 0), (1, LANES - 1)):
-                column = jnp.broadcast_to(planes[q][:, edge : edge + 1], (sh.levels, LANES))
-                corners[side] = jnp.where(zlanes == 2 * q + which, column, corners[side])
-    for side in range(2):
-        outs[side][at : at + sh.levels, :] = corners[side]
-
-
-def make_columns(sh, f, edges):
-    per = LANES // sh.levels
-    groups = (19 + per - 1) // per
-    rows = groups * sh.xs + sh.levels
+            pair = 2 * q + which
+            corners = jnp.where(zpairs == pair, pltpu.roll(planes[q], 2 * pair + 1, 1), corners)
+    out[groups * sh.xs :, :] = corners
+
+
+def column_rows(sh):
+    per = LANES // (2 * sh.levels)
+    return (19 + per - 1) // per * sh.xs
+
+
+def make_columns(sh, plan, f, edges):
     return pl.pallas_call(
         lambda *refs: column_kernel(sh, bool(edges), *refs),
-        out_shape=[pltpu.VMEM((rows, LANES), F32)] * 2,
-        in_specs=[VM] * (1 + len(edges)),
-        out_specs=[VM] * 2,
+        out_shape=pltpu.VMEM((column_rows(sh) + sh.levels, LANES), F32),
+        in_specs=[SM] + [VM] * (1 + len(edges)),
+        out_specs=VM,
         compiler_params=PARAMS,
         name="columns",
-    )(f, *edges)
+    )(plan, f, *edges)
 
 
 def peskin(offsets):
@@ -329,7 +403,7 @@
 TABLE_CHUNK = 1024
 
 
-def table_kernel(sh, plan, cells, after, across, upward, info, codes, sem):
+def table_kernel(sh, plan, cells, after, across, upward, info, codes, lines, sem):
     del after
     ids = [rotor_at(sh, plan, slot) for slot in range(sh.slots)]
     copies = []
@@ -339,18 +413,23 @@
         copy.start()
         copies.append(copy)
     width = min(TABLE_CHUNK, sh.markers)
-    corner = iota((8, width), 0)
-    spanwise = corner < 4
-    place = (corner % 4).astype(F32) - 1.0
-    ycells = iota((LANES, LANES), 0).astype(F32).astype(BF16)
+    part = iota((8, width), 0)
+    spanwise = part < 4
+    cell_bits = 6 + sh.levels.bit_length() - 1
+    quarter = LANES // 4
+    packed = 16
+    ycells = [
+        (iota((packed, LANES), 0) + first).astype(F32).astype(BF16)
+        for first in range(0, quarter, packed)
+    ]
     zcells = iota((sh.levels, LANES), 0)
     for slot in range(sh.slots):
         copies[slot].wait()
 
         @pl.when(ids[slot] >= 0)
         def _():
-            row = ids[slot] % 8
-            every = codes[slot, pl.ds(row, 1), :] // (64 * sh.levels)
+            line = ids[slot] % 8
+            every = codes[slot, pl.ds(line, 1), :] >> cell_bits
             lowest = jnp.min(every)
             highest = jnp.max(every)
             narrow = highest - lowest + 4 <= LANES
@@ -359,30 +438,42 @@
             info[2 * slot + 1] = jnp.where(narrow, 1, 2)
 
             def chunk(window, at):
-                code = codes[slot, pl.ds(row, 1), pl.ds(at, width)]
-                cells_y = code // (64 * sh.levels) - start - window * LANES
-                levels = code // 64 % sh.levels
-                eighths = jnp.where(spanwise, code // 8 % 8, code % 8)
-                weights = peskin(place - eighths.astype(F32) * 0.125)
-                top = weights.astype(BF16)
-                rest = (weights - top.astype(F32)).astype(BF16)
-                cells_y = cells_y.astype(F32)
+                code = codes[slot, pl.ds(line, 1), pl.ds(at, width)]
+                cells = (code >> cell_bits) - (start + window * LANES)
+                levels = (code >> 6) & (sh.levels - 1)
+                eighths = jnp.where(spanwise, code >> 3, code) & 7
+                corner = jnp.where(spanwise, (part - cells) & 3, part - 4)
+                weights = peskin(corner.astype(F32) - 1.0 - eighths.astype(F32) * 0.125)
+                places = ((cells + corner - part) >> 2).astype(F32)
+                top = weights.astype(BF16).astype(F32)
+                rest = weights - top
+                lines[0] = places
+                lines[1] = top
+                lines[2] = rest
+                lines[3] = weights
                 for group in range(width // LANES):
                     lanes = slice(group * LANES, (group + 1) * LANES)
                     to = pl.ds(at + group * LANES, LANES)
                     tall = jnp.zeros((sh.levels, LANES), F32)
                     for j in range(4):
                         tall = jnp.where(
-                            zcells == levels[:, lanes] + j, weights[4 + j : 5 + j, lanes], tall
+                            zcells == levels[:, lanes] + j, lines[3, 4 + j : 5 + j, lanes], tall
                         )
                     upward[slot, :, to] = tall
-                    wide = [jnp.zeros((LANES, LANES), BF16)] * 2
-                    for j in range(4):
-                        here = ycells == (cells_y[:, lanes] + float(j)).astype(BF16)
-                        for part, source in ((0, top), (1, rest)):
-                            wide[part] = jnp.where(here, source[j : j + 1, lanes], wide[part])
-                    for part in range(2):
-                        across[slot, window, part * LANES : (part + 1) * LANES, to] = wide[part]
+
+                    def spread_line(k, kind):
+                        line = lines[k, kind : kind + 1, lanes]
+                        return jnp.broadcast_to(line, (packed, LANES)).astype(BF16)
+
+                    for kind in range(4):
+                        spot, high, low = [spread_line(k, kind) for k in range(3)]
+                        for k, cell in enumerate(ycells):
+                            here = cell == spot
+                            for half, source in ((0, high), (1, low)):
+                                row = half * LANES + kind * quarter + k * packed
+                                across[slot, window, row : row + packed, to] = jnp.where(
+                                    here, source, jnp.zeros((), BF16)
+                                )
 
             def sweep(window):
                 def body(i, carry):
@@ -410,6 +501,7 @@
         out_specs=[VM, VM, SM],
         scratch_shapes=[
             pltpu.VMEM((sh.slots, 8, sh.markers), jnp.int32),
+            pltpu.VMEM((4, 8, min(TABLE_CHUNK, sh.markers)), F32),
             pltpu.SemaphoreType.DMA((sh.slots,)),
         ],
         compiler_params=PARAMS,
@@ -418,49 +510,8 @@
     return in_vmem(across), in_vmem(upward), in_smem(info)
 
 
-def blade_kernel(sh, plan, phases, twist, angle, after, blades):
-    del after
-    blades[0] = jnp.sin(angle[...])
-    blades[1] = jnp.cos(angle[...])
-    sin_twist = jnp.sin(twist[...])
-    cos_twist = jnp.cos(twist[...])
-    owner = iota((1, LANES), 1)
-    rows = iota((sh.slots * sh.groups, LANES), 0) % sh.slots
-    phase = jnp.zeros((1, LANES), F32)
-    for step in range(sh.steps):
-        for slot in range(sh.slots):
-            rotor = jnp.maximum(rotor_at(sh, plan, slot), 0)
-            here = owner == step * sh.slots + slot
-            phase = jnp.where(here, phases[step, rotor].astype(F32), phase)
-    pitch = PITCH_AMP * jnp.sin((2.0 * math.pi / PHASES) * phase)
-    sin_pitch = jnp.sin(pitch)
-    cos_pitch = jnp.cos(pitch)
-    for step in range(sh.steps):
-        parts = []
-        for part in (sin_pitch, cos_pitch):
-            total = jnp.zeros((sh.slots * sh.groups, LANES), F32)
-            for slot in range(sh.slots):
-                lane = step * sh.slots + slot
-                total = jnp.where(rows == slot, part[:, lane : lane + 1], total)
-            parts.append(total)
-        blades[2 + 2 * step] = sin_twist * parts[1] + cos_twist * parts[0]
-        blades[3 + 2 * step] = cos_twist * parts[1] - sin_twist * parts[0]
-
-
-def make_blades(sh, plan, phases, twist, angle, after):
-    rows = sh.slots * sh.groups
-    return pl.pallas_call(
-        lambda *refs: blade_kernel(sh, *refs),
-        out_shape=pltpu.VMEM((2 + 2 * sh.steps, rows, LANES), F32),
-        in_specs=[SM, SM, VM, VM, VM],
-        out_specs=VM,
-        compiler_params=PARAMS,
-        name="blades",
-    )(plan, jnp.transpose(phases), twist, angle, after)
-
-
-SAMPLE_CHUNK = 4096
-SPREAD_CHUNK = 4096
+SAMPLE_CHUNK = 8192
+SPREAD_CHUNK = 8192
 
 
 def split(value):
@@ -469,7 +520,7 @@
 
 
 def marker_kernel(
-    sh, step, plan, info, across, upward, area, speed, blades, filt_old, west, east, *refs
+    sh, step, plan, info, across, upward, area, speed, blades, filt_old, columns, *refs
 ):
     sections = refs[: sh.tiles]
     filt_new, loads = refs[sh.tiles : sh.tiles + 2]
@@ -477,6 +528,11 @@
     around, sampled, weighted, spread = refs[2 * sh.tiles + 2 :]
     me = lax.axis_index("gy")
     tall = 3 * sh.levels
+    quarter = LANES // 4
+    rows = iota((LANES, LANES), 0)
+    kinds = iota((LANES, LANES), 1)
+    by_class = (rows == kinds % quarter * 4 + kinds // quarter).astype(F32).astype(BF16)
+    from_class = (kinds == rows % quarter * 4 + rows // quarter).astype(F32).astype(BF16)
     for shift in range(sh.tiles):
         around[lax.rem(me + sh.tiles - shift, sh.tiles)] = sections[shift][...]
     spread[...] = jnp.zeros(spread.shape, F32)
@@ -504,6 +560,7 @@
             seen = pltpu.roll(both, lax.rem(2 * LANES - offset, 2 * LANES), 1)[:, :LANES]
             top, rest = split(seen)
             left = jnp.concatenate([top, rest], axis=0)
+            left = jnp.dot(left, by_class, preferred_element_type=F32).astype(BF16)
             left = jnp.concatenate([left, left], axis=1)
 
             def chunk(i, carry):
@@ -574,8 +631,8 @@
                     weighted[:tall, group * LANES : (group + 1) * LANES] = top
                     weighted[tall:, group * LANES : (group + 1) * LANES] = rest
                 return total + lax.dot_general(
+                    across[slot, window, :, pl.ds(at, SPREAD_CHUNK)],
                     weighted[...],
-                    across[slot, window, :, pl.ds(at, SPREAD_CHUNK)],
                     (((1,), (1,)), ((), ())),
                     preferred_element_type=F32,
                 )
@@ -584,10 +641,19 @@
                 0,
                 sh.markers // SPREAD_CHUNK,
                 chunk,
-                jnp.zeros((2 * tall, 2 * LANES), F32),
+                jnp.zeros((2 * LANES, 2 * tall), F32),
             )
+            total = jnp.transpose(total)
             total = total[:tall] + total[tall:]
             total = -SPREAD * (total[:, :LANES] + total[:, LANES:])
+            pieces = []
+            for _ in range(3):
+                pieces.append(total.astype(BF16))
+                total = total - pieces[-1].astype(F32)
+            pieces = jnp.dot(
+                jnp.concatenate(pieces, axis=0), from_class, preferred_element_type=F32
+            )
+            total = pieces[:tall] + pieces[tall : 2 * tall] + pieces[2 * tall :]
             both = jnp.concatenate([total, jnp.zeros((tall, LANES), F32)], axis=1)
             both = pltpu.roll(both, offset, 1)
             spread[tile, rows, :] = spread[tile, rows, :] + both[:, :LANES]
@@ -601,24 +667,25 @@
         forces[shift][: sh.section, :] = spread[tile]
         before = lax.rem(tile + sh.tiles - 1, sh.tiles)
         after = lax.rem(tile + 1, sh.tiles)
-        ghosts = jnp.zeros((sh.levels, LANES), F32)
+        beyond = [jnp.zeros((sh.levels, LANES), F32)] * 2
         for k in range(3 * sh.slots):
             at = pl.ds(k * sh.levels, sh.levels)
             left = jnp.broadcast_to(spread[before, at, :][:, LANES - 1 :], (sh.levels, LANES))
             right = jnp.broadcast_to(spread[after, at, :][:, :1], (sh.levels, LANES))
-            ghosts = jnp.where(lanes == 2 * k, left, ghosts)
-            ghosts = jnp.where(lanes == 2 * k + 1, right, ghosts)
-        forces[shift][sh.section : sh.section + sh.levels, :] = ghosts
-    forces[1][sh.section + sh.levels :, :] = east[...]
-    forces[sh.tiles - 1][sh.section + sh.levels :, :] = west[...]
+            beyond[0] = jnp.where(lanes == k, left, beyond[0])
+            beyond[1] = jnp.where(lanes == k, right, beyond[1])
+        for side in range(2):
+            forces[shift][pl.ds(sh.section + side, sh.levels, stride=2), :] = beyond[side]
+    for shift in {1, sh.tiles - 1}:
+        forces[shift][sh.section + 2 * sh.levels :, :] = columns[...]
 
 
 def do_markers(sh, step, plan, tables, fixed, blades, filt, columns, sections):
     across, upward, info = tables
     rows = sh.slots * sh.groups
     dense = pltpu.VMEM((3, rows, LANES), F32)
-    plain = sh.section + sh.levels
-    extra = columns[0].shape[0]
+    plain = sh.section + 2 * sh.levels
+    extra = columns.shape[0]
     forces = [
         pltpu.VMEM((plain + (extra if by in (1, sh.tiles - 1) else 0), LANES), F32)
         for by in range(sh.tiles)
@@ -626,7 +693,7 @@
     out = pl.pallas_call(
         lambda *refs: marker_kernel(sh, step, *refs),
         out_shape=[dense, dense] + forces,
-        in_specs=[SM, SM] + [VM] * (8 + sh.tiles),
+        in_specs=[SM, SM] + [VM] * (7 + sh.tiles),
         out_specs=[VM] * (2 + sh.tiles),
         scratch_shapes=[
             pltpu.VMEM((sh.tiles, sh.section, LANES), F32),
@@ -636,7 +703,7 @@
         ],
         compiler_params=PARAMS,
         name="markers",
-    )(plan, info, across, upward, *fixed, blades, filt, *columns, *sections)
+    )(plan, info, across, upward, *fixed, blades, filt, columns, *sections)
     return in_vmem(out[0]), in_vmem(out[1]), out[2:]
 
 
@@ -645,25 +712,22 @@
     refs = refs[2 * has_edges :]
     forces = refs[: sh.tiles]
     outs = refs[sh.tiles + 1 :]
-    first = sh.section + sh.levels
     me = lax.axis_index("gy")
     lanes = iota((sh.levels, LANES), 1)
-    per = LANES // sh.levels
-    corner_rows = pl.ds(first + (19 + per - 1) // per * sh.xs, sh.levels)
+    corner_rows = pl.ds(sh.section + 2 * sh.levels + column_rows(sh), sh.levels)
     blank = jnp.zeros((sh.levels, LANES), F32)
     planes_at = (0, sh.xs - 1)
-    corner = []
-    from_left = forces[1][corner_rows, :]
-    from_right = forces[sh.tiles - 1][corner_rows, :]
-    for q in range(19):
-        a = pltpu.roll(from_left, (LANES - 2 * q) % LANES, 1)
-        b = pltpu.roll(from_right, (LANES + 2 - 2 * q) % LANES, 1)
-        corner.append(jnp.where(lanes < 2, a, jnp.where(lanes < 4, b, 1.0)))
+    beyond = jnp.where(
+        lanes % 2 == 0, forces[1][corner_rows, :], forces[sh.tiles - 1][corner_rows, :]
+    )
+    corner = [pltpu.roll(beyond, (LANES - 4 * q) % LANES, 1) for q in range(19)]
     corner_force = [blank, blank, blank]
     edge_force = [[blank, blank, blank], [blank, blank, blank]]
     for shift in range(sh.tiles):
         owner = lax.rem(me + sh.tiles - shift, sh.tiles)
-        ghosts = forces[shift][sh.section : sh.section + sh.levels, :]
+        ghosts = [
+            forces[shift][pl.ds(sh.section + side, sh.levels, stride=2), :] for side in range(2)
+        ]
         for slot in range(sh.slots):
             x = plane_at(sh, plan, owner, slot)
             for axis in range(3):
@@ -673,8 +737,8 @@
                     here = jnp.asarray(x == planes_at[which])
                     edge_force[which][axis] = edge_force[which][axis] + jnp.where(here, piece, 0.0)
                     for side in range(2):
-                        lane = 2 * side + which
-                        moved = pltpu.roll(ghosts, (lane - 2 * k - side) % LANES, 1)
+                        lane = 2 * which + side
+                        moved = pltpu.roll(ghosts[side], (lane - k) % LANES, 1)
                         corner_force[axis] = corner_force[axis] + jnp.where(
                             jnp.logical_and(here, lanes == lane), moved, 0.0
                         )
@@ -687,11 +751,11 @@
             value = post[q]
             if DIRS[q][1] == 1:
                 value = pltpu.roll(value, 1, 1)
-                ghost = pltpu.roll(corner_post[q], (LANES - which) % LANES, 1)
+                ghost = pltpu.roll(corner_post[q], (LANES - 2 * which) % LANES, 1)
                 value = jnp.where(lanes == 0, ghost, value)
             elif DIRS[q][1] == -1:
                 value = pltpu.roll(value, LANES - 1, 1)
-                ghost = pltpu.roll(corner_post[q], (LANES - 1 - 2 - which) % LANES, 1)
+                ghost = pltpu.roll(corner_post[q], LANES - 2 - 2 * which, 1)
                 value = jnp.where(lanes == LANES - 1, ghost, value)
             if DIRS[q][2]:
                 value = pltpu.roll(value, DIRS[q][2] % sh.levels, 0)
@@ -783,81 +847,52 @@
     refs = refs[2 * has_edges :]
     forces = refs[: sh.tiles]
     out = refs[sh.tiles + 1]
-    field, ghost_posts = refs[-3:-1]
-    sem = refs[-1]
+    sems = refs[-1]
     me = lax.axis_index("gy")
     xs = sh.xs
     lanes = iota((xs, LANES), 1)
     xrows = iota((xs, LANES), 0)
-    per = LANES // sh.levels
-    field[...] = jnp.zeros(field.shape, F32)
-    ghost_force = [jnp.zeros((xs, LANES), F32) for axis in range(3)]
+    per = LANES // (2 * sh.levels)
+    copies = []
+
+    def send(q):
+        if last:
+            copy = pltpu.make_async_copy(out.at[q], refs[sh.tiles + 2].at[q], sems.at[q])
+            copy.start()
+            copies.append(copy)
+
+    rotors = []
     for shift in range(sh.tiles):
         owner = lax.rem(me + sh.tiles - shift, sh.tiles)
-        ghosts = jnp.transpose(
-            jnp.concatenate(
-                [
-                    forces[shift][sh.section : sh.section + sh.levels, :],
-                    jnp.zeros((LANES - sh.levels, LANES), F32),
-                ],
-                axis=0,
-            )
-        )
         for slot in range(sh.slots):
-            x = plane_at(sh, plan, owner, slot)
-
-            @pl.when(x >= 0)
-            def _():
+            rotors.append((plane_at(sh, plan, owner, slot), forces[shift], slot * 3))
+
+    for x, _, _ in rotors:
+
+        @pl.when(x >= 0)
+        def _():
+            here = plane_of(sh, f, x, low, high)
+            force = [jnp.zeros((sh.levels, LANES), F32)] * 3
+            for other, source, first in rotors:
+                same = (other == x).astype(F32)
                 for axis in range(3):
-                    k = slot * 3 + axis
-                    at = pl.ds(x, sh.levels, stride=xs)
-                    field[axis, at, :] = (
-                        field[axis, at, :] + forces[shift][k * sh.levels : (k + 1) * sh.levels, :]
-                    )
-
-            for axis in range(3):
-                k = slot * 3 + axis
-                far = pltpu.roll(ghosts[2 * k + 1 : 2 * k + 2, :], sh.levels, 1)
-                piece = ghosts[2 * k : 2 * k + 1, :] + far
-                ghost_force[axis] = ghost_force[axis] + jnp.where(xrows == x, piece, 0.0)
-
-    ghost = []
-    left, right = forces[1], forces[sh.tiles - 1]
-    for q in range(19):
-        at = pl.ds(sh.section + sh.levels + q // per * xs, xs)
-        shift = (q % per) * sh.levels
-        a = pltpu.roll(left[at, :], (LANES - shift) % LANES, 1)
-        b = pltpu.roll(right[at, :], (LANES + sh.levels - shift) % LANES, 1)
-        ghost.append(jnp.where(lanes < sh.levels, a, jnp.where(lanes < 2 * sh.levels, b, 1.0)))
-    posted = collide(ghost, ghost_force, SIDEWAYS)
-    for k, q in enumerate(SIDEWAYS):
-        value = posted[q]
-        if DIRS[q][0]:
-            value = pltpu.roll(value, DIRS[q][0] % xs, 0)
-        ghost_posts[k] = value
-
-    def plane(k, carry):
-        key = plan[k]
-
-        @pl.when(key >= 0)
-        def _():
-            x = lax.rem(key, xs)
-            here = plane_of(sh, f, x, low, high)
-            force = [field[axis, pl.ds(x, sh.levels, stride=xs), :] for axis in range(3)]
+                    at = (first + axis) * sh.levels
+                    force[axis] = force[axis] + same * source[at : at + sh.levels, :]
             post = collide(here, force, range(19))
             rows = sh.levels - 1
             for q in range(19):
                 dx, dy, dz = DIRS[q]
                 value = post[q]
                 moved = pltpu.roll(value, dy % LANES, 1) if dy else value
-
-                def put(dx=dx, dz=dz, q=q, moved=moved):
+                to = x + dx
+
+                def put(dz=dz, q=q, moved=moved, to=to):
                     if dz == 0:
-                        out[q, pl.ds(x + dx, sh.levels, stride=xs), :] = moved
+                        out[q, pl.ds(to, sh.levels, stride=xs), :] = moved
                     elif dz == 1:
-                        out[q, pl.ds(x + dx + xs, rows, stride=xs), :] = moved[:rows]
+                        out[q, pl.ds(to + xs, rows, stride=xs), :] = moved[:rows]
                     else:
-                        out[q, pl.ds(x + dx, rows, stride=xs), :] = moved[1:]
+                        out[q, pl.ds(to, rows, stride=xs), :] = moved[1:]
 
                 if dx:
                     pl.when(x != (xs - 1 if dx == 1 else 0))(put)
@@ -868,27 +903,56 @@
                 elif dz == -1:
                     out[OPPOSITE[q], pl.ds(x, 1), :] = value[:1]
 
-        return carry
-
-    lax.fori_loop(0, sh.tiles * sh.slots, plane, 0)
-
+    for q in range(19):
+        if q not in SIDEWAYS:
+            send(q)
+
+    ghost_force = [jnp.zeros((xs, LANES), F32) for axis in range(3)]
+    tall = 2 * sh.levels
+    for shift in range(sh.tiles):
+        ghosts = jnp.transpose(
+            jnp.concatenate(
+                [
+                    forces[shift][sh.section : sh.section + tall, :],
+                    jnp.zeros((LANES - tall, LANES), F32),
+                ],
+                axis=0,
+            )
+        )
+        for x, _, first in rotors[shift * sh.slots : (shift + 1) * sh.slots]:
+            for axis in range(3):
+                k = first + axis
+                ghost_force[axis] = ghost_force[axis] + jnp.where(
+                    xrows == x, ghosts[k : k + 1, :], 0.0
+                )
+    left, right = forces[1], forces[sh.tiles - 1]
+    beyond = []
+    for group in range(column_rows(sh) // xs):
+        at = pl.ds(sh.section + tall + group * xs, xs)
+        beyond.append(jnp.where(lanes % 2 == 0, left[at, :], right[at, :]))
+    ghost = [
+        pltpu.roll(beyond[q // per], (LANES - (q % per) * tall) % LANES, 1) for q in range(19)
+    ]
+    posted = collide(ghost, ghost_force, SIDEWAYS)
     for k, q in enumerate(SIDEWAYS):
-        dy, dz = DIRS[q][1:]
+        dx, dy, dz = DIRS[q]
+        value = posted[q]
+        if dx:
+            value = pltpu.roll(value, dx % xs, 0)
         for z in range(sh.levels):
             if not 0 <= z - dz < sh.levels:
                 continue
             at = pl.ds(z * xs, xs)
-            value = out[q, at, :]
+            here = out[q, at, :]
             if dy == 1:
-                other = pltpu.roll(ghost_posts[k], (LANES - z + dz) % LANES, 1)
-                value = jnp.where(lanes == 0, other, value)
+                other = pltpu.roll(value, (LANES - 2 * (z - dz)) % LANES, 1)
+                here = jnp.where(lanes == 0, other, here)
             else:
-                other = pltpu.roll(ghost_posts[k], LANES - 1 - sh.levels - z + dz, 1)
-                value = jnp.where(lanes == LANES - 1, other, value)
-            out[q, at, :] = value
-    if last:
-        copy = pltpu.make_async_copy(out, refs[sh.tiles + 2], sem)
-        copy.start()
+                other = pltpu.roll(value, LANES - 2 - 2 * (z - dz), 1)
+                here = jnp.where(lanes == LANES - 1, other, here)
+            out[q, at, :] = here
+        send(q)
+    for copy in copies:
         copy.wait()
 
 
@@ -902,9 +966,7 @@
         in_specs=[SM] + [VM] * (2 + len(edges) + sh.tiles),
         out_specs=[VM] + [HB] * last,
         scratch_shapes=[
-            pltpu.VMEM((3, sh.levels * sh.xs, LANES), F32),
-            pltpu.VMEM((len(SIDEWAYS), sh.xs, LANES), F32),
-            pltpu.SemaphoreType.DMA,
+            pltpu.SemaphoreType.DMA((19,)),
         ],
         input_output_aliases={2 + len(edges) + sh.tiles: 0},
         compiler_params=PARAMS,
@@ -984,23 +1046,25 @@
     filt_in,
 ):
     sh = Shape(f_in, rotor_place, marker_cell, pitch_phase, filt_in)
-    plan, f, sections = start(sh, rotor_place, f_in)
     area, twist, speed, angle = [
         by_group(sh, x[0, 0]) for x in (blade_area, blade_twist, blade_speed, blade_angle)
     ]
     filt = by_group(sh, jnp.swapaxes(filt_in[0, 0], 0, 1))
+    f = in_vmem(f_in.reshape(19, sh.levels * sh.xs, LANES))
+    plan, blades = start(sh, rotor_place, pitch_phase, twist, angle)
     edges = ()
     for step in range(sh.steps):
         last = step == sh.steps - 1
-        if step:
-            sections = make_sections(sh, plan, f, edges)
+        if step == 0:
+            columns = in_vmem(make_columns(sh, plan, f, edges))
+            sections = make_sections(sh, plan, f, edges, (columns,))
+            tables = make_tables(sh, plan, marker_cell, in_vmem(sections[0]))
+        else:
+            sections = make_sections(sh, plan, f, edges, ())
+            columns = in_vmem(make_columns(sh, plan, f, edges))
         sections = [sections[0]] + [
             shifted(sections[by], "gy", by) for by in range(1, sh.tiles)
         ]
-        columns = [in_vmem(column) for column in make_columns(sh, f, edges)]
-        if step == 0:
-            blades = in_vmem(make_blades(sh, plan, pitch_phase, twist, angle, columns[0]))
-            tables = make_tables(sh, plan, marker_cell, blades)
         filt, loads, forces = do_markers(
             sh,
             step,

time: 68.5 us -> 63.8 us (0.931)
  Pallas kernels: 40.5 us -> 34.6 us
  waiting for transfers between devices: 3.65 us -> 5.23 us
  local copies, waits for them, and re-layouts: 2.41 us -> 1.72 us
    pallas_call x1, Pallas kernels: 6.11 us -> 4.06 us  [make_tables(): pl.pallas_call(lambda *refs: table_kernel(sh, *refs), out_shape=[pltpu.VM...]
    ppermute x16, waiting for transfers between devices: 3.65 us -> 5.23 us  [shifted(): return lax.ppermute(x, axis, [(i, (i + by) % count) for i in range(count)])]
    pallas_call x2, Pallas kernels: 3.17 us -> 1.67 us  [make_columns(): pl.pallas_call(lambda *refs: column_kernel(sh, bool(edges), *refs), out_s...]
    pallas_call x2, Pallas kernels: 9.36 us -> 7.86 us  [do_patch(): pl.pallas_call(lambda *refs: patch_kernel(sh, bool(edges), last, *refs),...]
    pallas_call x2, Pallas kernels: 2.1 us -> 1.14 us  [make_sections(): pl.pallas_call(lambda *refs: section_kernel(sh, bool(edges), *refs), out_...]
    unnamed x18 -> x12, local copies, waits for them, and re-layouts: 2.41 us -> 1.72 us
  transfers between devices with their start and end apart: 16 -> 16, of which waited for: 3 -> 4; matrix products, arithmetic and copies ran while one was open for 0% -> 0% of each run, Pallas kernels for 36% -> 28%
where the time goes in v3:
time: 63.8 us; the launch traced here: 63.4 us
  Pallas kernels  34.6 us (54%)
  starting transfers between devices  20.9 us (33%)
  waiting for transfers between devices  5.23 us (8%)
  local copies, waits for them, and re-layouts  1.72 us (3%)
  between operations  1.05 us (2%)
    ppermute x16, starting transfers between devices, shifted(): return lax.ppermute(x, axis, [(i, (i + by) % count) for i in range(count)])  20.9 us
    pallas_call x2, Pallas kernels, do_markers(): pl.pallas_call(lambda *refs: marker_kernel(sh, step, *refs), out_shape=[d...  11.7 us
    pallas_call x2, Pallas kernels, do_patch(): pl.pallas_call(lambda *refs: patch_kernel(sh, bool(edges), last, *refs),...  7.86 us
    ppermute x16, waiting for transfers between devices, shifted(): return lax.ppermute(x, axis, [(i, (i + by) % count) for i in range(count)])  5.23 us
    pallas_call x2, Pallas kernels, do_bulk(): pl.pallas_call(lambda *refs: bulk_kernel(sh, bool(edges), last, *refs), o...  4.69 us
    pallas_call x1, Pallas kernels, make_tables(): pl.pallas_call(lambda *refs: table_kernel(sh, *refs), out_shape=[pltpu.VM...  4.06 us
    unnamed x12, local copies, waits for them, and re-layouts  1.72 us
    pallas_call x2, Pallas kernels, make_columns(): pl.pallas_call(lambda *refs: column_kernel(sh, bool(edges), *refs), out_s...  1.67 us
  transfers between devices with their start and end apart: 16, of which 4 were waited for; matrix products, arithmetic and copies ran while one was open for 0% of the time, Pallas kernels for 28%

profile of v3, /device:TPU:0, one launch (start us, length us, event | category | flops | bytes accessed | tf_op | source)
XLA Modules:
  0.0 63.4 jit_solution(12919905375441734345)
XLA Ops:
  0.6 1.6 %start.1 = (s32[8]{0:T(128)S(4)}, f32[6,128,128]{2,1,0:T(8,128)S(1)}) custom-call(s32[3,40]{1,0:T(4,128)} %bitcast.64, s32[2,40]{1,0:T(2,128)} %bitcast.65, f32[128,128]{1,0:T(8,128)} %bitcast.62, f32[128,128]{1,0:T(8,128)} %bitcast.63), custom_call_target="tpu_custom_call" | custom-call | tf_op jit(solution)/shard_map/start/pallas_call | solution.py:297
  2.3 1.7 %copy-done = f32[19,16,16,128]{3,2,1,0:T(8,128)S(1)} copy-done((f32[19,16,16,128]{3,2,1,0:T(8,128)S(1)}, f32[19,16,16,128]{3,2,1,0:T(8,128)}, u32[]{:S(2)}) %copy-start) | copy-done | bytes 2490392
  4.0 0.8 %columns.2.refs_2_.refs_8_ = f32[96,128]{1,0:T(8,128)S(1)} custom-call(s32[8]{0:T(128)S(4)} %get-tuple-element.37.refs_0_, f32[19,256,128]{2,1,0:T(8,128)S(1)} %bitcast.51), custom_call_target="tpu_custom_call" | custom-call | tf_op jit(solution)/shard_map/columns/pallas_call | solution.py:384
  5.9 2.6 %collective-permute-start.1 = (f32[96,128]{1,0:T(8,128)S(1)}, f32[96,128]{1,0:T(8,128)S(1)}, u32[]{:S(2)}, u32[]{:S(2)}) collective-permute-start(f32[96,128]{1,0:T(8,128)S(1)} %get-tuple-element.44), channel_id=1, source_target_pairs={{0,2},{1,3},{2,0},{3,1},{4,6},{5,7},{6,4},{7,5},{8,10},{9,11},{10,... | collective-permute-start | bytes 147464 | tf_op jit(solution)/shard_map/ppermute | solution.py:1034
  8.5 1.4 %collective-permute-start.2 = (f32[96,128]{1,0:T(8,128)S(1)}, f32[96,128]{1,0:T(8,128)S(1)}, u32[]{:S(2)}, u32[]{:S(2)}) collective-permute-start(f32[96,128]{1,0:T(8,128)S(1)} %get-tuple-element.45), channel_id=1, source_target_pairs={{0,3},{1,0},{2,1},{3,2},{4,7},{5,4},{6,5},{7,6},{8,11},{9,8},{10,9... | collective-permute-start | bytes 147464 | tf_op jit(solution)/shard_map/ppermute | solution.py:1034
  9.9 4.1 %tables.1 = (bf16[2,2,256,8192]{3,2,1,0:T(8,128)(2,1)S(1)}, f32[2,16,8192]{2,1,0:T(8,128)S(1)}, s32[4]{0:T(128)S(4)}) custom-call(s32[8]{0:T(128)S(4)} %get-tuple-element.37.refs_0_, s32[40,8192]{1,0:T(8,128)S(1)} %copy-done.2, f32[96,128]{1,0:T(8,128)S(1)} %get-tuple-element.38.refs_2_.refs_9_), custom_call_target="tpu_custom_call" | custom-call | tf_op jit(solution)/shard_map/tables/pallas_call | solution.py:493
  14.0 5.8 %markers.2 = (f32[3,128,128]{2,1,0:T(8,128)S(1)}, f32[3,128,128]{2,1,0:T(8,128)S(1)}, f32[128,128]{1,0:T(8,128)S(1)}, f32[224,128]{1,0:T(8,128)S(1)}, f32[128,128]{1,0:T(8,128)S(1)}, /*index=5*/f32[224,128]{1,0:T(8,128)S(1)}) custom-call(s32[8]{0:T(128)S(4)} %get-tuple-element.37.refs_0_, s32[4]{0:T(128)S(4)} %get-tuple-element.39.refs_1_, ...), custom_call_target="tpu_custom_call" | custom-call | tf_op jit(solution)/shard_map/markers/pallas_call | solution.py:693
  19.9 1.7 %collective-permute-start.5 = (f32[224,128]{1,0:T(8,128)S(1)}, f32[224,128]{1,0:T(8,128)S(1)}, u32[]{:S(2)}, u32[]{:S(2)}) collective-permute-start(f32[224,128]{1,0:T(8,128)S(1)} %get-tuple-element.49), channel_id=1, source_target_pairs={{0,3},{1,0},{2,1},{3,2},{4,7},{5,4},{6,5},{7,6},{8,11},{9,8},{10,9... | collective-permute-start | bytes 344072 | tf_op jit(solution)/shard_map/ppermute | solution.py:1034
  21.6 2.0 %bulk.2.refs_6_ = f32[19,256,128]{2,1,0:T(8,128)S(1)} custom-call(s32[8]{0:T(128)S(4)} %get-tuple-element.37.refs_0_, f32[19,256,128]{2,1,0:T(8,128)S(1)} %bitcast.53, f32[3,128,128]{2,1,0:T(8,128)S(1)} %get-tuple-element.50.refs_2_, f32[3,128,128]{2,1,0:T(8,128)S(1)} %get-tuple-element.51.refs_3_.refs_7_), custom_call_target="tpu_custom_call" | custom-call | tf_op jit(solution)/shard_map/bulk/pallas_call | solution.py:835
  23.6 2.2 %collective-permute-done.4.refs_4_ = f32[128,128]{1,0:T(8,128)S(1)} collective-permute-done((f32[128,128]{1,0:T(8,128)S(1)}, f32[128,128]{1,0:T(8,128)S(1)}, u32[]{:S(2)}, u32[]{:S(2)}) %collective-permute-start.4) | collective-permute-done | bytes 65568 | tf_op jit(solution)/shard_map/ppermute | solution.py:1034
  26.3 1.4 %collective-permute-start.6 = (f32[5,16,128]{2,1,0:T(8,128)S(1)}, f32[5,16,128]{2,1,0:T(8,128)S(1)}, u32[]{:S(2)}, u32[]{:S(2)}) collective-permute-start(f32[5,16,128]{2,1,0:T(8,128)S(1)} %get-tuple-element.52), channel_id=1, source_target_pairs={{0,4},{4,8},{8,12},{12,16},{16,20},{20,24},{24,28},{28,0},{1,5},{5... | collective-permute-start | bytes 122888 | tf_op jit(solution)/shard_map/ppermute | solution.py:1034
  27.7 3.4 %collective-permute-start.7 = (f32[5,16,128]{2,1,0:T(8,128)S(1)}, f32[5,16,128]{2,1,0:T(8,128)S(1)}, u32[]{:S(2)}, u32[]{:S(2)}) collective-permute-start(f32[5,16,128]{2,1,0:T(8,128)S(1)} %get-tuple-element.53), channel_id=1, source_target_pairs={{0,28},{4,0},{8,4},{12,8},{16,12},{20,16},{24,20},{28,24},{1,29},{... | collective-permute-start | bytes 122888 | tf_op jit(solution)/shard_map/ppermute | solution.py:1034
  31.1 3.4 %patch.2.refs_1_ = f32[19,256,128]{2,1,0:T(8,128)S(1)} custom-call(s32[8]{0:T(128)S(4)} %get-tuple-element.37.refs_0_, f32[19,256,128]{2,1,0:T(8,128)S(1)} %bitcast.55, f32[128,128]{1,0:T(8,128)S(1)} %get-tuple-element.46.refs_2_, f32[224,128]{1,0:T(8,128)S(1)} %collective-permute-done.3.refs_3_, ...), custom_call_target="tpu_custom_call", output_to_operand_aliasing={{}: (6, {})} | custom-call | tf_op jit(solution)/shard_map/patch/pallas_call | solution.py:963
  35.2 1.5 %collective-permute-start.9 = (f32[96,128]{1,0:T(8,128)S(1)}, f32[96,128]{1,0:T(8,128)S(1)}, u32[]{:S(2)}, u32[]{:S(2)}) collective-permute-start(f32[96,128]{1,0:T(8,128)S(1)} %get-tuple-element.56), channel_id=1, source_target_pairs={{0,2},{1,3},{2,0},{3,1},{4,6},{5,7},{6,4},{7,5},{8,10},{9,11},{10,... | collective-permute-start | bytes 147464 | tf_op jit(solution)/shard_map/ppermute | solution.py:1034
  36.6 1.4 %collective-permute-start.10 = (f32[96,128]{1,0:T(8,128)S(1)}, f32[96,128]{1,0:T(8,128)S(1)}, u32[]{:S(2)}, u32[]{:S(2)}) collective-permute-start(f32[96,128]{1,0:T(8,128)S(1)} %get-tuple-element.57), channel_id=1, source_target_pairs={{0,3},{1,0},{2,1},{3,2},{4,7},{5,4},{6,5},{7,6},{8,11},{9,8},{10,9... | collective-permute-start | bytes 147464 | tf_op jit(solution)/shard_map/ppermute | solution.py:1034
  38.0 0.8 %columns.3.refs_8_ = f32[96,128]{1,0:T(8,128)S(1)} custom-call(s32[8]{0:T(128)S(4)} %get-tuple-element.37.refs_0_, f32[19,256,128]{2,1,0:T(8,128)S(1)} %patch.2.refs_1_, f32[5,16,128]{2,1,0:T(8,128)S(1)} %collective-permute-done.6.refs_2_, f32[5,16,128]{2,1,0:T(8,128)S(1)} %collective-permute-done.7.refs_3_), custom_call_target="tpu_custom_call" | custom-call | tf_op jit(solution)/shard_map/columns/pallas_call | solution.py:384
  38.9 0.6 %collective-permute-done.9.refs_11_ = f32[96,128]{1,0:T(8,128)S(1)} collective-permute-done((f32[96,128]{1,0:T(8,128)S(1)}, f32[96,128]{1,0:T(8,128)S(1)}, u32[]{:S(2)}, u32[]{:S(2)}) %collective-permute-start.9) | collective-permute-done | bytes 49184 | tf_op jit(solution)/shard_map/ppermute | solution.py:1034
  39.8 6.0 %markers.3 = (f32[3,128,128]{2,1,0:T(8,128)S(1)}, f32[3,128,128]{2,1,0:T(8,128)S(1)}, f32[128,128]{1,0:T(8,128)S(1)}, f32[224,128]{1,0:T(8,128)S(1)}, f32[128,128]{1,0:T(8,128)S(1)}, /*index=5*/f32[224,128]{1,0:T(8,128)S(1)}) custom-call(s32[8]{0:T(128)S(4)} %get-tuple-element.37.refs_0_, s32[4]{0:T(128)S(4)} %get-tuple-element.39.refs_1_, ...), custom_call_target="tpu_custom_call" | custom-call | tf_op jit(solution)/shard_map/markers/pallas_call | solution.py:693
  45.8 1.8 %collective-permute-start.13 = (f32[224,128]{1,0:T(8,128)S(1)}, f32[224,128]{1,0:T(8,128)S(1)}, u32[]{:S(2)}, u32[]{:S(2)}) collective-permute-start(f32[224,128]{1,0:T(8,128)S(1)} %get-tuple-element.61), channel_id=1, source_target_pairs={{0,3},{1,0},{2,1},{3,2},{4,7},{5,4},{6,5},{7,6},{8,11},{9,8},{10,9... | collective-permute-start | bytes 344072 | tf_op jit(solution)/shard_map/ppermute | solution.py:1034
  48.0 2.7 %bulk.3 = (f32[19,256,128]{2,1,0:T(8,128)S(1)}, f32[3,128,128]{2,1,0:T(8,128)}, f32[3,128,128]{2,1,0:T(8,128)}) custom-call(s32[8]{0:T(128)S(4)} %get-tuple-element.37.refs_0_, f32[19,256,128]{2,1,0:T(8,128)S(1)} %patch.2.refs_1_, f32[5,16,128]{2,1,0:T(8,128)S(1)} %collective-permute-done.6.refs_2_, f32[5,16,128]{2,1,0:T(8,128)S(1)} %collective-permute-done.7.refs_3_, ...), custom_call_target="tpu_custom_call" | custom-call | tf_op jit(solution)/shard_map/bulk/pallas_call | solution.py:835
  50.6 2.1 %collective-permute-done.12.refs_6_ = f32[128,128]{1,0:T(8,128)S(1)} collective-permute-done((f32[128,128]{1,0:T(8,128)S(1)}, f32[128,128]{1,0:T(8,128)S(1)}, u32[]{:S(2)}, u32[]{:S(2)}) %collective-permute-start.12) | collective-permute-done | bytes 65568 | tf_op jit(solution)/shard_map/ppermute | solution.py:1034
  53.1 4.7 %collective-permute-start.15 = (f32[5,16,128]{2,1,0:T(8,128)S(1)}, f32[5,16,128]{2,1,0:T(8,128)S(1)}, u32[]{:S(2)}, u32[]{:S(2)}) collective-permute-start(f32[5,16,128]{2,1,0:T(8,128)S(1)} %get-tuple-element.67), channel_id=1, source_target_pairs={{0,28},{4,0},{8,4},{12,8},{16,12},{20,16},{24,20},{28,24},{1,29},{... | collective-permute-start | bytes 122888 | tf_op jit(solution)/shard_map/ppermute | solution.py:1034
  57.9 4.4 %patch.3 = (f32[19,256,128]{2,1,0:T(8,128)S(1)}, f32[19,256,128]{2,1,0:T(8,128)}) custom-call(s32[8]{0:T(128)S(4)} %get-tuple-element.37.refs_0_, f32[19,256,128]{2,1,0:T(8,128)S(1)} %patch.2.refs_1_, f32[5,16,128]{2,1,0:T(8,128)S(1)} %collective-permute-done.6.refs_2_, ...), custom_call_target="tpu_custom_call", output_to_operand_aliasing={{0}: (8, {})} | custom-call | tf_op jit(solution)/shard_map/patch/pallas_call | solution.py:963
  62.3 0.9 %finish.1 = f32[19,16,16,128]{3,2,1,0:T(8,128)} custom-call(f32[19,256,128]{2,1,0:T(8,128)S(1)} %get-tuple-element.65.refs_0_, f32[5,16,128]{2,1,0:T(8,128)S(1)} %collective-permute-done.14.refs_1_, f32[5,16,128]{2,1,0:T(8,128)S(1)} %collective-permute-done.15.refs_2_, f32[19,16,16,128]{3,2,1,0:T(8,128)} %bitcast.61), custom_call_target="tpu_custom_call", output_to_operand_aliasing={{}: (3, {})} | custom-call | tf_op jit(solution)/shard_map/finish/pallas_call | solution.py:1005
  (35 shorter events, 3.4 us)
Async XLA Ops:
  2.3 1.7 %copy-start = (f32[19,16,16,128]{3,2,1,0:T(8,128)S(1)}, f32[19,16,16,128]{3,2,1,0:T(8,128)}, u32[]{:S(2)}) copy-start(f32[19,16,16,128]{3,2,1,0:T(8,128)} %param.9) | copy-start | bytes 7471108
  4.0 5.9 %copy-start.2 = (s32[40,8192]{1,0:T(8,128)S(1)}, s32[40,8192]{1,0:T(8,128)}, u32[]{:S(2)}) copy-start(s32[40,8192]{1,0:T(8,128)} %refs_1_.1) | copy-start | bytes 3932164
  4.8 9.2 %copy-start.3 = (f32[1,1,2,8192]{3,2,1,0:T(2,128)S(1)}, f32[1,1,2,8192]{3,2,1,0:T(2,128)}, u32[]{:S(2)}) copy-start(f32[1,1,2,8192]{3,2,1,0:T(2,128)} %param.13) | copy-start | bytes 196612
  4.8 9.2 %copy-start.4 = (f32[1,1,2,8192]{3,2,1,0:T(2,128)S(1)}, f32[1,1,2,8192]{3,2,1,0:T(2,128)}, u32[]{:S(2)}) copy-start(f32[1,1,2,8192]{3,2,1,0:T(2,128)} %param.15) | copy-start | bytes 196612
  4.8 9.2 %copy-start.5 = (f32[1,1,2,3,8192]{4,2,3,1,0:T(2,128)S(1)}, f32[1,1,2,3,8192]{4,2,3,1,0:T(2,128)}, u32[]{:S(2)}) copy-start(f32[1,1,2,3,8192]{4,2,3,1,0:T(2,128)} %param.17) | copy-start | bytes 589828
  5.4 8.6 %collective-permute-start = (f32[96,128]{1,0:T(8,128)S(1)}, f32[96,128]{1,0:T(8,128)S(1)}, u32[]{:S(2)}, u32[]{:S(2)}) collective-permute-start(f32[96,128]{1,0:T(8,128)S(1)} %get-tuple-element.43), channel_id=1, source_target_pairs={{0,1},{1,2},{2,3},{3,0},{4,5},{5,6},{6,7},{7,4},{8,9},{9,10},{10,1... | collective-permute-start | bytes 147464 | tf_op jit(solution)/shard_map/ppermute | solution.py:1034
  5.9 8.1 %collective-permute-start.1 = (f32[96,128]{1,0:T(8,128)S(1)}, f32[96,128]{1,0:T(8,128)S(1)}, u32[]{:S(2)}, u32[]{:S(2)}) collective-permute-start(f32[96,128]{1,0:T(8,128)S(1)} %get-tuple-element.44), channel_id=1, source_target_pairs={{0,2},{1,3},{2,0},{3,1},{4,6},{5,7},{6,4},{7,5},{8,10},{9,11},{10,... | collective-permute-start | bytes 147464 | tf_op jit(solution)/shard_map/ppermute | solution.py:1034
  8.5 5.5 %collective-permute-start.2 = (f32[96,128]{1,0:T(8,128)S(1)}, f32[96,128]{1,0:T(8,128)S(1)}, u32[]{:S(2)}, u32[]{:S(2)}) collective-permute-start(f32[96,128]{1,0:T(8,128)S(1)} %get-tuple-element.45), channel_id=1, source_target_pairs={{0,3},{1,0},{2,1},{3,2},{4,7},{5,4},{6,5},{7,6},{8,11},{9,8},{10,9... | collective-permute-start | bytes 147464 | tf_op jit(solution)/shard_map/ppermute | solution.py:1034
  14.0 7.6 %copy-start.1 = (f32[19,16,16,128]{3,2,1,0:T(8,128)S(1)}, f32[19,16,16,128]{3,2,1,0:T(8,128)}, u32[]{:S(2)}) copy-start(f32[19,16,16,128]{3,2,1,0:T(8,128)} %param.9) | copy-start | bytes 7471108
  19.8 6.1 %collective-permute-start.3 = (f32[224,128]{1,0:T(8,128)S(1)}, f32[224,128]{1,0:T(8,128)S(1)}, u32[]{:S(2)}, u32[]{:S(2)}) collective-permute-start(f32[224,128]{1,0:T(8,128)S(1)} %get-tuple-element.47), channel_id=1, source_target_pairs={{0,1},{1,2},{2,3},{3,0},{4,5},{5,6},{6,7},{7,4},{8,9},{9,10},{10,1... | collective-permute-start | bytes 344072 | tf_op jit(solution)/shard_map/ppermute | solution.py:1034
  19.9 6.0 %collective-permute-start.5 = (f32[224,128]{1,0:T(8,128)S(1)}, f32[224,128]{1,0:T(8,128)S(1)}, u32[]{:S(2)}, u32[]{:S(2)}) collective-permute-start(f32[224,128]{1,0:T(8,128)S(1)} %get-tuple-element.49), channel_id=1, source_target_pairs={{0,3},{1,0},{2,1},{3,2},{4,7},{5,4},{6,5},{7,6},{8,11},{9,8},{10,9... | collective-permute-start | bytes 344072 | tf_op jit(solution)/shard_map/ppermute | solution.py:1034
  21.6 4.3 %collective-permute-start.4 = (f32[128,128]{1,0:T(8,128)S(1)}, f32[128,128]{1,0:T(8,128)S(1)}, u32[]{:S(2)}, u32[]{:S(2)}) collective-permute-start(f32[128,128]{1,0:T(8,128)S(1)} %get-tuple-element.48), channel_id=1, source_target_pairs={{0,2},{1,3},{2,0},{3,1},{4,6},{5,7},{6,4},{7,5},{8,10},{9,11},{10,... | collective-permute-start | bytes 196616 | tf_op jit(solution)/shard_map/ppermute | solution.py:1034
  26.3 8.2 %collective-permute-start.6 = (f32[5,16,128]{2,1,0:T(8,128)S(1)}, f32[5,16,128]{2,1,0:T(8,128)S(1)}, u32[]{:S(2)}, u32[]{:S(2)}) collective-permute-start(f32[5,16,128]{2,1,0:T(8,128)S(1)} %get-tuple-element.52), channel_id=1, source_target_pairs={{0,4},{4,8},{8,12},{12,16},{16,20},{20,24},{24,28},{28,0},{1,5},{5... | collective-permute-start | bytes 122888 | tf_op jit(solution)/shard_map/ppermute | solution.py:1034
  27.7 6.8 %collective-permute-start.7 = (f32[5,16,128]{2,1,0:T(8,128)S(1)}, f32[5,16,128]{2,1,0:T(8,128)S(1)}, u32[]{:S(2)}, u32[]{:S(2)}) collective-permute-start(f32[5,16,128]{2,1,0:T(8,128)S(1)} %get-tuple-element.53), channel_id=1, source_target_pairs={{0,28},{4,0},{8,4},{12,8},{16,12},{20,16},{24,20},{28,24},{1,29},{... | collective-permute-start | bytes 122888 | tf_op jit(solution)/shard_map/ppermute | solution.py:1034
  35.1 3.7 %collective-permute-start.8 = (f32[96,128]{1,0:T(8,128)S(1)}, f32[96,128]{1,0:T(8,128)S(1)}, u32[]{:S(2)}, u32[]{:S(2)}) collective-permute-start(f32[96,128]{1,0:T(8,128)S(1)} %get-tuple-element.55), channel_id=1, source_target_pairs={{0,1},{1,2},{2,3},{3,0},{4,5},{5,6},{6,7},{7,4},{8,9},{9,10},{10,1... | collective-permute-start | bytes 147464 | tf_op jit(solution)/shard_map/ppermute | solution.py:1034
  35.2 4.3 %collective-permute-start.9 = (f32[96,128]{1,0:T(8,128)S(1)}, f32[96,128]{1,0:T(8,128)S(1)}, u32[]{:S(2)}, u32[]{:S(2)}) collective-permute-start(f32[96,128]{1,0:T(8,128)S(1)} %get-tuple-element.56), channel_id=1, source_target_pairs={{0,2},{1,3},{2,0},{3,1},{4,6},{5,7},{6,4},{7,5},{8,10},{9,11},{10,... | collective-permute-start | bytes 147464 | tf_op jit(solution)/shard_map/ppermute | solution.py:1034
  36.6 3.1 %collective-permute-start.10 = (f32[96,128]{1,0:T(8,128)S(1)}, f32[96,128]{1,0:T(8,128)S(1)}, u32[]{:S(2)}, u32[]{:S(2)}) collective-permute-start(f32[96,128]{1,0:T(8,128)S(1)} %get-tuple-element.57), channel_id=1, source_target_pairs={{0,3},{1,0},{2,1},{3,2},{4,7},{5,4},{6,5},{7,6},{8,11},{9,8},{10,9... | collective-permute-start | bytes 147464 | tf_op jit(solution)/shard_map/ppermute | solution.py:1034
  45.8 6.9 %collective-permute-start.11 = (f32[224,128]{1,0:T(8,128)S(1)}, f32[224,128]{1,0:T(8,128)S(1)}, u32[]{:S(2)}, u32[]{:S(2)}) collective-permute-start(f32[224,128]{1,0:T(8,128)S(1)} %get-tuple-element.59), channel_id=1, source_target_pairs={{0,1},{1,2},{2,3},{3,0},{4,5},{5,6},{6,7},{7,4},{8,9},{9,10},{10,1... | collective-permute-start | bytes 344072 | tf_op jit(solution)/shard_map/ppermute | solution.py:1034
  45.8 6.9 %collective-permute-start.13 = (f32[224,128]{1,0:T(8,128)S(1)}, f32[224,128]{1,0:T(8,128)S(1)}, u32[]{:S(2)}, u32[]{:S(2)}) collective-permute-start(f32[224,128]{1,0:T(8,128)S(1)} %get-tuple-element.61), channel_id=1, source_target_pairs={{0,3},{1,0},{2,1},{3,2},{4,7},{5,4},{6,5},{7,6},{8,11},{9,8},{10,9... | collective-permute-start | bytes 344072 | tf_op jit(solution)/shard_map/ppermute | solution.py:1034
  47.6 5.0 %collective-permute-start.12 = (f32[128,128]{1,0:T(8,128)S(1)}, f32[128,128]{1,0:T(8,128)S(1)}, u32[]{:S(2)}, u32[]{:S(2)}) collective-permute-start(f32[128,128]{1,0:T(8,128)S(1)} %get-tuple-element.60), channel_id=1, source_target_pairs={{0,2},{1,3},{2,0},{3,1},{4,6},{5,7},{6,4},{7,5},{8,10},{9,11},{10,... | collective-permute-start | bytes 196616 | tf_op jit(solution)/shard_map/ppermute | solution.py:1034
  53.1 9.2 %collective-permute-start.14 = (f32[5,16,128]{2,1,0:T(8,128)S(1)}, f32[5,16,128]{2,1,0:T(8,128)S(1)}, u32[]{:S(2)}, u32[]{:S(2)}) collective-permute-start(f32[5,16,128]{2,1,0:T(8,128)S(1)} %get-tuple-element.66), channel_id=1, source_target_pairs={{0,4},{4,8},{8,12},{12,16},{16,20},{20,24},{24,28},{28,0},{1,5},{5... | collective-permute-start | bytes 122888 | tf_op jit(solution)/shard_map/ppermute | solution.py:1034
  53.1 9.2 %collective-permute-start.15 = (f32[5,16,128]{2,1,0:T(8,128)S(1)}, f32[5,16,128]{2,1,0:T(8,128)S(1)}, u32[]{:S(2)}, u32[]{:S(2)}) collective-permute-start(f32[5,16,128]{2,1,0:T(8,128)S(1)} %get-tuple-element.67), channel_id=1, source_target_pairs={{0,28},{4,0},{8,4},{12,8},{16,12},{20,16},{24,20},{28,24},{1,29},{... | collective-permute-start | bytes 122888 | tf_op jit(solution)/shard_map/ppermute | solution.py:1034

commit v4 on v3

--- a/solution.py
+++ b/solution.py
@@ -280,34 +280,38 @@
 
 
 def start_kernel(
-    sh, place_in, phases_in, twist_in, angle_in, plan, blades, place, phases, twist, angle, sems
+    sh, place_in, phases_in, twist_in, angle_in, f_in, plan, blades, f, place, phases, twist, angle, sems
 ):
     pairs = ((place_in, place), (phases_in, phases), (angle_in, angle), (twist_in, twist))
     copies = [pltpu.make_async_copy(*pair, sems.at[k]) for k, pair in enumerate(pairs)]
+    whole = pltpu.make_async_copy(f_in, f, sems.at[4])
     for copy in copies:
         copy.start()
+    whole.start()
     for copy in copies:
         copy.wait()
     write_plan(sh, place, plan)
     write_blades(sh, plan, phases, twist, angle, blades)
-
-
-def start(sh, rotor_place, phases, twist, angle):
+    whole.wait()
+
+
+def start(sh, rotor_place, phases, twist, angle, f_in):
     rows = sh.slots * sh.groups
-    plan, blades = pl.pallas_call(
+    plan, blades, f = pl.pallas_call(
         lambda *refs: start_kernel(sh, *refs),
         out_shape=[
             pltpu.SMEM((sh.tiles * sh.slots,), jnp.int32),
             pltpu.VMEM((2 + 2 * sh.steps, rows, LANES), F32),
+            pltpu.VMEM((19, sh.levels * sh.xs, LANES), F32),
         ],
-        in_specs=[HB] * 4,
-        out_specs=[SM, VM],
+        in_specs=[HB] * 5,
+        out_specs=[SM, VM, VM],
         scratch_shapes=[
             pltpu.VMEM((3, sh.rotors), jnp.int32),
             pltpu.SMEM((sh.steps, sh.rotors), jnp.int32),
             pltpu.VMEM((rows, LANES), F32),
             pltpu.VMEM((rows, LANES), F32),
-            pltpu.SemaphoreType.DMA((4,)),
+            pltpu.SemaphoreType.DMA((5,)),
         ],
         compiler_params=PARAMS,
         name="start",
@@ -316,8 +320,9 @@
         in_hbm(jnp.transpose(phases)),
         in_hbm(twist),
         in_hbm(angle),
+        in_hbm(f_in.reshape(19, sh.levels * sh.xs, LANES)),
     )
-    return in_smem(plan), in_vmem(blades)
+    return in_smem(plan), in_vmem(blades), in_vmem(f)
 
 
 def section_kernel(sh, has_edges, plan, f, *refs):
@@ -339,7 +344,8 @@
 def column_kernel(sh, has_edges, *refs):
     f = refs[1]
     low, high = refs[2:4] if has_edges else (None, None)
-    out = refs[-1]
+    east, west = refs[-2:]
+    packed = []
     pairs = iota((sh.xs, LANES), 1) // 2
     xrows = iota((sh.xs, LANES), 0)
     per = LANES // (2 * sh.levels)
@@ -364,7 +370,7 @@
                 total = jnp.where(
                     pairs == pair, pltpu.roll(tile, (2 * pair + 1) % LANES, 1), total
                 )
-        out[group * sh.xs : (group + 1) * sh.xs, :] = total
+        packed.append(total)
     zpairs = iota((sh.levels, LANES), 1) // 2
     corners = jnp.ones((sh.levels, LANES), F32)
     for which, x in ((0, 0), (1, sh.xs - 1)):
@@ -372,23 +378,42 @@
         for q in range(19):
             pair = 2 * q + which
             corners = jnp.where(zpairs == pair, pltpu.roll(planes[q], 2 * pair + 1, 1), corners)
-    out[groups * sh.xs :, :] = corners
-
-
-def column_rows(sh):
+    packed.append(corners)
+    even = iota((sh.xs, LANES), 1) % 2 == 0
+    for k in range(len(packed) // 2):
+        first, second = packed[2 * k], packed[2 * k + 1]
+        rows = slice(k * sh.xs, (k + 1) * sh.xs)
+        east[rows, :] = jnp.where(even, first, pltpu.roll(second, 1, 1))
+        west[rows, :] = jnp.where(even, pltpu.roll(first, LANES - 1, 1), second)
+
+
+def packed_columns(sh):
     per = LANES // (2 * sh.levels)
-    return (19 + per - 1) // per * sh.xs
+    return (19 + per - 1) // per + 1
+
+
+def unpack_columns(sh, left, right, first):
+    even = iota((sh.xs, LANES), 1) % 2 == 0
+    groups = []
+    for k in range(packed_columns(sh) // 2):
+        rows = pl.ds(first + k * sh.xs, sh.xs)
+        a, b = left[rows, :], right[rows, :]
+        groups.append(jnp.where(even, a, pltpu.roll(b, 1, 1)))
+        groups.append(jnp.where(even, pltpu.roll(a, LANES - 1, 1), b))
+    return groups
 
 
 def make_columns(sh, plan, f, edges):
-    return pl.pallas_call(
+    shape = (packed_columns(sh) // 2 * sh.xs, LANES)
+    out = pl.pallas_call(
         lambda *refs: column_kernel(sh, bool(edges), *refs),
-        out_shape=pltpu.VMEM((column_rows(sh) + sh.levels, LANES), F32),
+        out_shape=[pltpu.VMEM(shape, F32)] * 2,
         in_specs=[SM] + [VM] * (1 + len(edges)),
-        out_specs=VM,
+        out_specs=[VM] * 2,
         compiler_params=PARAMS,
         name="columns",
     )(plan, f, *edges)
+    return [in_vmem(x) for x in out]
 
 
 def peskin(offsets):
@@ -510,6 +535,7 @@
     return in_vmem(across), in_vmem(upward), in_smem(info)
 
 
+GHOST_LANES = 32
 SAMPLE_CHUNK = 8192
 SPREAD_CHUNK = 8192
 
@@ -520,12 +546,12 @@
 
 
 def marker_kernel(
-    sh, step, plan, info, across, upward, area, speed, blades, filt_old, columns, *refs
+    sh, step, plan, info, across, upward, area, speed, blades, filt_old, east, west, *refs
 ):
     sections = refs[: sh.tiles]
     filt_new, loads = refs[sh.tiles : sh.tiles + 2]
     forces = refs[sh.tiles + 2 : 2 * sh.tiles + 2]
-    around, sampled, weighted, spread = refs[2 * sh.tiles + 2 :]
+    around, sampled, weighted, spread, turning = refs[2 * sh.tiles + 2 :]
     me = lax.axis_index("gy")
     tall = 3 * sh.levels
     quarter = LANES // 4
@@ -674,18 +700,29 @@
             right = jnp.broadcast_to(spread[after, at, :][:, :1], (sh.levels, LANES))
             beyond[0] = jnp.where(lanes == k, left, beyond[0])
             beyond[1] = jnp.where(lanes == k, right, beyond[1])
+        at = shift * GHOST_LANES
         for side in range(2):
-            forces[shift][pl.ds(sh.section + side, sh.levels, stride=2), :] = beyond[side]
-    for shift in {1, sh.tiles - 1}:
-        forces[shift][sh.section + 2 * sh.levels :, :] = columns[...]
+            turning[pl.ds(at + side, sh.levels, stride=2), :] = beyond[side]
+        forces[shift][sh.section + 8 : sh.section + 8 + sh.levels, :] = jnp.where(
+            lanes < 8, beyond[0], pltpu.roll(beyond[1], 8, 1)
+        )
+    each = LANES // GHOST_LANES
+    for first in range(0, sh.tiles, each):
+        rows = jnp.transpose(turning[first * GHOST_LANES : (first + each) * GHOST_LANES, :])[:8]
+        for k in range(each):
+            forces[first + k][sh.section : sh.section + 8, :] = pltpu.roll(
+                rows, (LANES - k * GHOST_LANES) % LANES, 1
+            )
+    forces[1][sh.section + 8 + sh.levels :, :] = east[...]
+    forces[sh.tiles - 1][sh.section + 8 + sh.levels :, :] = west[...]
 
 
 def do_markers(sh, step, plan, tables, fixed, blades, filt, columns, sections):
     across, upward, info = tables
     rows = sh.slots * sh.groups
     dense = pltpu.VMEM((3, rows, LANES), F32)
-    plain = sh.section + 2 * sh.levels
-    extra = columns.shape[0]
+    plain = sh.section + 8 + sh.levels
+    extra = columns[0].shape[0]
     forces = [
         pltpu.VMEM((plain + (extra if by in (1, sh.tiles - 1) else 0), LANES), F32)
         for by in range(sh.tiles)
@@ -693,17 +730,18 @@
     out = pl.pallas_call(
         lambda *refs: marker_kernel(sh, step, *refs),
         out_shape=[dense, dense] + forces,
-        in_specs=[SM, SM] + [VM] * (7 + sh.tiles),
+        in_specs=[SM, SM] + [VM] * (8 + sh.tiles),
         out_specs=[VM] * (2 + sh.tiles),
         scratch_shapes=[
             pltpu.VMEM((sh.tiles, sh.section, LANES), F32),
             pltpu.VMEM((3, rows, LANES), F32),
             pltpu.VMEM((6 * sh.levels, SPREAD_CHUNK), BF16),
             pltpu.VMEM((sh.tiles, sh.section, LANES), F32),
+            pltpu.VMEM((sh.tiles * GHOST_LANES, LANES), F32),
         ],
         compiler_params=PARAMS,
         name="markers",
-    )(plan, info, across, upward, *fixed, blades, filt, columns, *sections)
+    )(plan, info, across, upward, *fixed, blades, filt, *columns, *sections)
     return in_vmem(out[0]), in_vmem(out[1]), out[2:]
 
 
@@ -714,20 +752,16 @@
     outs = refs[sh.tiles + 1 :]
     me = lax.axis_index("gy")
     lanes = iota((sh.levels, LANES), 1)
-    corner_rows = pl.ds(sh.section + 2 * sh.levels + column_rows(sh), sh.levels)
     blank = jnp.zeros((sh.levels, LANES), F32)
     planes_at = (0, sh.xs - 1)
-    beyond = jnp.where(
-        lanes % 2 == 0, forces[1][corner_rows, :], forces[sh.tiles - 1][corner_rows, :]
-    )
+    even = lax.rem(lax.axis_index("gx"), 2) == 0
+    beyond = unpack_columns(sh, forces[1], forces[sh.tiles - 1], sh.section + 8 + sh.levels)[-1]
     corner = [pltpu.roll(beyond, (LANES - 4 * q) % LANES, 1) for q in range(19)]
     corner_force = [blank, blank, blank]
     edge_force = [[blank, blank, blank], [blank, blank, blank]]
     for shift in range(sh.tiles):
         owner = lax.rem(me + sh.tiles - shift, sh.tiles)
-        ghosts = [
-            forces[shift][pl.ds(sh.section + side, sh.levels, stride=2), :] for side in range(2)
-        ]
+        ghosts = forces[shift][sh.section + 8 : sh.section + 8 + sh.levels, :]
         for slot in range(sh.slots):
             x = plane_at(sh, plan, owner, slot)
             for axis in range(3):
@@ -738,15 +772,15 @@
                     edge_force[which][axis] = edge_force[which][axis] + jnp.where(here, piece, 0.0)
                     for side in range(2):
                         lane = 2 * which + side
-                        moved = pltpu.roll(ghosts[side], (lane - k) % LANES, 1)
+                        moved = pltpu.roll(ghosts, (lane - side * 8 - k) % LANES, 1)
                         corner_force[axis] = corner_force[axis] + jnp.where(
                             jnp.logical_and(here, lanes == lane), moved, 0.0
                         )
     corner_post = collide(corner, corner_force, [q for q in PLUS + MINUS if DIRS[q][1]])
+    leaving = ([], [])
     for which, wanted in ((1, PLUS), (0, MINUS)):
         planes = plane_of(sh, f, planes_at[which], low, high)
         post = collide(planes, edge_force[which], wanted)
-        out = outs[0] if which else outs[1]
         for k, q in enumerate(wanted):
             value = post[q]
             if DIRS[q][1] == 1:
@@ -759,7 +793,10 @@
                 value = jnp.where(lanes == LANES - 1, ghost, value)
             if DIRS[q][2]:
                 value = pltpu.roll(value, DIRS[q][2] % sh.levels, 0)
-            out[k] = value
+            leaving[which].append(value)
+    for k, (down, up) in enumerate(zip(*leaving)):
+        outs[0][k] = jnp.where(even, up, down)
+        outs[1][k] = jnp.where(even, down, up)
 
 
 def make_edges(sh, plan, f, edges, forces, after):
@@ -776,8 +813,15 @@
 def bulk_kernel(sh, has_edges, last, plan, f, *refs):
     low, high = refs[:2] if has_edges else (None, None)
     refs = refs[2 * has_edges :]
-    loads, filt, out = refs[:3]
+    loads, filt, out, planes = refs[:4]
     xs = sh.xs
+    for k in range(sh.tiles * sh.slots):
+
+        @pl.when(plan[k] >= 0)
+        def _():
+            for q, value in enumerate(plane_of(sh, f, lax.rem(plan[k], xs), low, high)):
+                planes[k, q] = value
+
     xrows = iota((xs, LANES), 0)
     if last:
         rows = iota((sh.slots * sh.groups, LANES), 0) % sh.slots
@@ -785,7 +829,7 @@
         for slot in range(sh.slots):
             there = (rotor_at(sh, plan, slot) >= 0).astype(jnp.int32)
             used = jnp.where(rows == slot, there, used)
-        for source, target in ((loads, refs[3]), (filt, refs[4])):
+        for source, target in ((loads, refs[4]), (filt, refs[5])):
             for axis in range(3):
                 target[axis] = jnp.where(used > 0, source[axis], 0.0)
 
@@ -829,7 +873,10 @@
 
 
 def do_bulk(sh, last, plan, f, edges, loads, filt):
-    out_shape = [pltpu.VMEM((19, sh.levels * sh.xs, LANES), F32)]
+    out_shape = [
+        pltpu.VMEM((19, sh.levels * sh.xs, LANES), F32),
+        pltpu.VMEM((sh.tiles * sh.slots, 19, sh.levels, LANES), F32),
+    ]
     if last:
         out_shape += [jax.ShapeDtypeStruct(loads.shape, F32)] * 2
     return pl.pallas_call(
@@ -842,9 +889,7 @@
     )(plan, f, *edges, loads, filt)
 
 
-def patch_kernel(sh, has_edges, last, plan, f, *refs):
-    low, high = refs[:2] if has_edges else (None, None)
-    refs = refs[2 * has_edges :]
+def patch_kernel(sh, last, plan, planes, *refs):
     forces = refs[: sh.tiles]
     out = refs[sh.tiles + 1]
     sems = refs[-1]
@@ -865,15 +910,17 @@
     for shift in range(sh.tiles):
         owner = lax.rem(me + sh.tiles - shift, sh.tiles)
         for slot in range(sh.slots):
-            rotors.append((plane_at(sh, plan, owner, slot), forces[shift], slot * 3))
-
-    for x, _, _ in rotors:
+            rotors.append(
+                (plane_at(sh, plan, owner, slot), forces[shift], slot * 3, owner * sh.slots + slot)
+            )
+
+    for x, _, _, index in rotors:
 
         @pl.when(x >= 0)
         def _():
-            here = plane_of(sh, f, x, low, high)
+            here = [planes[index, q] for q in range(19)]
             force = [jnp.zeros((sh.levels, LANES), F32)] * 3
-            for other, source, first in rotors:
+            for other, source, first, _ in rotors:
                 same = (other == x).astype(F32)
                 for axis in range(3):
                     at = (first + axis) * sh.levels
@@ -884,20 +931,13 @@
                 dx, dy, dz = DIRS[q]
                 value = post[q]
                 moved = pltpu.roll(value, dy % LANES, 1) if dy else value
-                to = x + dx
-
-                def put(dz=dz, q=q, moved=moved, to=to):
-                    if dz == 0:
-                        out[q, pl.ds(to, sh.levels, stride=xs), :] = moved
-                    elif dz == 1:
-                        out[q, pl.ds(to + xs, rows, stride=xs), :] = moved[:rows]
-                    else:
-                        out[q, pl.ds(to, rows, stride=xs), :] = moved[1:]
-
-                if dx:
-                    pl.when(x != (xs - 1 if dx == 1 else 0))(put)
+                to = lax.rem(x + (dx + xs), xs) if dx else x
+                if dz == 0:
+                    out[q, pl.ds(to, sh.levels, stride=xs), :] = moved
+                elif dz == 1:
+                    out[q, pl.ds(to + xs, rows, stride=xs), :] = moved[:rows]
                 else:
-                    put()
+                    out[q, pl.ds(to, rows, stride=xs), :] = moved[1:]
                 if dz == 1:
                     out[OPPOSITE[q], pl.ds(x + rows * xs, 1), :] = value[rows:]
                 elif dz == -1:
@@ -909,27 +949,14 @@
 
     ghost_force = [jnp.zeros((xs, LANES), F32) for axis in range(3)]
     tall = 2 * sh.levels
-    for shift in range(sh.tiles):
-        ghosts = jnp.transpose(
-            jnp.concatenate(
-                [
-                    forces[shift][sh.section : sh.section + tall, :],
-                    jnp.zeros((LANES - tall, LANES), F32),
-                ],
-                axis=0,
+    for x, source, first, _ in rotors:
+        ghosts = source[sh.section : sh.section + 8, :]
+        for axis in range(3):
+            k = first + axis
+            ghost_force[axis] = ghost_force[axis] + jnp.where(
+                xrows == x, ghosts[k : k + 1, :], 0.0
             )
-        )
-        for x, _, first in rotors[shift * sh.slots : (shift + 1) * sh.slots]:
-            for axis in range(3):
-                k = first + axis
-                ghost_force[axis] = ghost_force[axis] + jnp.where(
-                    xrows == x, ghosts[k : k + 1, :], 0.0
-                )
-    left, right = forces[1], forces[sh.tiles - 1]
-    beyond = []
-    for group in range(column_rows(sh) // xs):
-        at = pl.ds(sh.section + tall + group * xs, xs)
-        beyond.append(jnp.where(lanes % 2 == 0, left[at, :], right[at, :]))
+    beyond = unpack_columns(sh, forces[1], forces[sh.tiles - 1], sh.section + 8 + sh.levels)
     ghost = [
         pltpu.roll(beyond[q // per], (LANES - (q % per) * tall) % LANES, 1) for q in range(19)
     ]
@@ -956,22 +983,22 @@
         copy.wait()
 
 
-def do_patch(sh, last, plan, f, edges, forces, bulk):
+def do_patch(sh, last, plan, planes, forces, bulk):
     out_shape = [pltpu.VMEM(bulk.shape, F32)]
     if last:
         out_shape.append(jax.ShapeDtypeStruct(bulk.shape, F32))
     return pl.pallas_call(
-        lambda *refs: patch_kernel(sh, bool(edges), last, *refs),
+        lambda *refs: patch_kernel(sh, last, *refs),
         out_shape=out_shape,
-        in_specs=[SM] + [VM] * (2 + len(edges) + sh.tiles),
+        in_specs=[SM] + [VM] * (2 + sh.tiles),
         out_specs=[VM] + [HB] * last,
         scratch_shapes=[
             pltpu.SemaphoreType.DMA((19,)),
         ],
-        input_output_aliases={2 + len(edges) + sh.tiles: 0},
+        input_output_aliases={2 + sh.tiles: 0},
         compiler_params=PARAMS,
         name="patch",
-    )(plan, f, *edges, *forces, bulk)
+    )(plan, planes, *forces, bulk)
 
 
 def finish_kernel(sh, held, low, high, f_old, f, merged, sem):
@@ -1034,6 +1061,32 @@
     return lax.ppermute(x, axis, [(i, (i + by) % count) for i in range(count)])
 
 
+def swapped(x, axis, first):
+    count = lax.axis_size(axis)
+    pairs = [(i, (i + 1) % count) for i in range(first, count, 2)]
+    return lax.ppermute(x, axis, pairs + [(b, a) for a, b in pairs])
+
+
+def join_kernel(one, two, low, high):
+    even = lax.rem(lax.axis_index("gx"), 2) == 0
+    low[...] = jnp.where(even, two[...], one[...])
+    high[...] = jnp.where(even, one[...], two[...])
+
+
+def exchange(one, two):
+    two = swapped(two, "gx", 1)
+    one = swapped(one, "gx", 0)
+    out = pl.pallas_call(
+        join_kernel,
+        out_shape=[pltpu.VMEM(one.shape, F32)] * 2,
+        in_specs=[VM, VM],
+        out_specs=[VM, VM],
+        compiler_params=PARAMS,
+        name="join",
+    )(in_vmem(one), in_vmem(two))
+    return tuple(in_vmem(x) for x in out)
+
+
 def local(
     f_in,
     rotor_place,
@@ -1050,18 +1103,17 @@
         by_group(sh, x[0, 0]) for x in (blade_area, blade_twist, blade_speed, blade_angle)
     ]
     filt = by_group(sh, jnp.swapaxes(filt_in[0, 0], 0, 1))
-    f = in_vmem(f_in.reshape(19, sh.levels * sh.xs, LANES))
-    plan, blades = start(sh, rotor_place, pitch_phase, twist, angle)
+    plan, blades, f = start(sh, rotor_place, pitch_phase, twist, angle, f_in)
     edges = ()
     for step in range(sh.steps):
         last = step == sh.steps - 1
         if step == 0:
-            columns = in_vmem(make_columns(sh, plan, f, edges))
-            sections = make_sections(sh, plan, f, edges, (columns,))
+            columns = make_columns(sh, plan, f, edges)
+            sections = make_sections(sh, plan, f, edges, columns)
             tables = make_tables(sh, plan, marker_cell, in_vmem(sections[0]))
         else:
             sections = make_sections(sh, plan, f, edges, ())
-            columns = in_vmem(make_columns(sh, plan, f, edges))
+            columns = make_columns(sh, plan, f, edges)
         sections = [sections[0]] + [
             shifted(sections[by], "gy", by) for by in range(1, sh.tiles)
         ]
@@ -1080,12 +1132,12 @@
         forces = [in_vmem(force) for force in forces]
         bulk = do_bulk(sh, last, plan, f, edges, loads, filt)
         if last:
-            loads_out, filt_out = bulk[1:]
+            loads_out, filt_out = bulk[2:]
+        planes = in_vmem(bulk[1])
         bulk = in_vmem(bulk[0])
         sent = make_edges(sh, plan, f, edges, forces, bulk)
-        arrived = [shifted(sent[0], "gx", 1), shifted(sent[1], "gx", -1)]
-        done = do_patch(sh, last, plan, f, edges, forces, bulk)
-        edges = tuple(in_vmem(edge) for edge in arrived)
+        done = do_patch(sh, last, plan, planes, forces, bulk)
+        edges = exchange(*sent)
         f = in_vmem(done[0])
     f = finish(sh, f, done[1], edges)
     loads_out, filt_out = [

time: 63.8 us -> 59.2 us (0.928)
  local copies, waits for them, and re-layouts: 1.72 us -> 0.02 us
  Pallas kernels: 34.6 us -> 33 us
  starting transfers between devices: 20.9 us -> 20 us
    ppermute x16 -> x12, starting transfers between devices: 20.9 us -> 11.3 us  [shifted(): return lax.ppermute(x, axis, [(i, (i + by) % count) for i in range(count)])]
    ppermute x0 -> x4, starting transfers between devices: none -> 8.76 us  [swapped(): return lax.ppermute(x, axis, pairs + [(b, a) for a, b in pairs])]
    pallas_call x2 -> x4, Pallas kernels: 7.86 us -> 4.15 us  [the longest x2 4.12 us: do_patch(): pl.pallas_call(lambda *refs: patch_kernel(sh, last, *refs), out_shape=out...]
    ppermute x0 -> x4, waiting for transfers between devices: none -> 2.11 us  [swapped(): return lax.ppermute(x, axis, pairs + [(b, a) for a, b in pairs])]
    ppermute x16 -> x12, waiting for transfers between devices: 5.23 us -> 3.19 us  [shifted(): return lax.ppermute(x, axis, [(i, (i + by) % count) for i in range(count)])]
    unnamed x12 -> x8, local copies, waits for them, and re-layouts: 1.72 us -> 0.02 us
    pallas_call x2, Pallas kernels: 4.69 us -> 5.85 us  [do_bulk(): pl.pallas_call(lambda *refs: bulk_kernel(sh, bool(edges), last, *refs), o...]
  transfers between devices with their start and end apart: 16 -> 16, of which waited for: 4 -> 6; matrix products, arithmetic and copies ran while one was open for 0% -> 0% of each run, Pallas kernels for 28% -> 25%
where the time goes in v4:
time: 59.2 us; the launch traced here: 59.3 us
  Pallas kernels  33 us (56%)
  starting transfers between devices  20 us (34%)
  waiting for transfers between devices  5.29 us (9%)
  between operations  0.99 us (2%)
    pallas_call x2, Pallas kernels, do_markers(): pl.pallas_call(lambda *refs: marker_kernel(sh, step, *refs), out_shape=[d...  12.1 us
    ppermute x12, starting transfers between devices, shifted(): return lax.ppermute(x, axis, [(i, (i + by) % count) for i in range(count)])  11.3 us
    ppermute x4, starting transfers between devices, swapped(): return lax.ppermute(x, axis, pairs + [(b, a) for a, b in pairs])  8.76 us
    pallas_call x2, Pallas kernels, do_bulk(): pl.pallas_call(lambda *refs: bulk_kernel(sh, bool(edges), last, *refs), o...  5.85 us
    pallas_call x2, Pallas kernels, do_patch(): pl.pallas_call(lambda *refs: patch_kernel(sh, last, *refs), out_shape=out...  4.12 us
    pallas_call x1, Pallas kernels, make_tables(): pl.pallas_call(lambda *refs: table_kernel(sh, *refs), out_shape=[pltpu.VM...  4.06 us
    ppermute x12, waiting for transfers between devices, shifted(): return lax.ppermute(x, axis, [(i, (i + by) % count) for i in range(count)])  3.19 us
    ppermute x4, waiting for transfers between devices, swapped(): return lax.ppermute(x, axis, pairs + [(b, a) for a, b in pairs])  2.11 us
  transfers between devices with their start and end apart: 16, of which 6 were waited for; matrix products, arithmetic and copies ran while one was open for 0% of the time, Pallas kernels for 25%

profile of v4, /device:TPU:0, one launch (start us, length us, event | category | flops | bytes accessed | tf_op | source)
XLA Modules:
  0.0 59.3 jit_solution(13504652324251425581)
XLA Ops:
  0.6 1.8 %start.1 = (s32[8]{0:T(128)S(4)}, f32[6,128,128]{2,1,0:T(8,128)S(1)}, f32[19,256,128]{2,1,0:T(8,128)S(1)}) custom-call(s32[3,40]{1,0:T(4,128)} %bitcast.60, s32[2,40]{1,0:T(2,128)} %bitcast.61, f32[128,128]{1,0:T(8,128)} %bitcast.58, f32[128,128]{1,0:T(8,128)} %bitcast.59, f32[19,256,128]{2,1,0:T(8,128)} %bitcast.57), custom_call_target="tpu_custom_call" | custom-call | tf_op jit(solution)/shard_map/start/pallas_call | solution.py:300
  2.5 1.0 %columns.2 = (f32[48,128]{1,0:T(8,128)S(1)}, f32[48,128]{1,0:T(8,128)S(1)}) custom-call(s32[8]{0:T(128)S(4)} %get-tuple-element.49.refs_0_, f32[19,256,128]{2,1,0:T(8,128)S(1)} %get-tuple-element.50.refs_1_), custom_call_target="tpu_custom_call" | custom-call | tf_op jit(solution)/shard_map/columns/pallas_call | solution.py:408
  4.6 2.6 %collective-permute-start.1 = (f32[96,128]{1,0:T(8,128)S(1)}, f32[96,128]{1,0:T(8,128)S(1)}, u32[]{:S(2)}, u32[]{:S(2)}) collective-permute-start(f32[96,128]{1,0:T(8,128)S(1)} %get-tuple-element.59), channel_id=1, source_target_pairs={{0,2},{1,3},{2,0},{3,1},{4,6},{5,7},{6,4},{7,5},{8,10},{9,11},{10,... | collective-permute-start | bytes 147464 | tf_op jit(solution)/shard_map/ppermute | solution.py:1061
  7.2 1.4 %collective-permute-start.2 = (f32[96,128]{1,0:T(8,128)S(1)}, f32[96,128]{1,0:T(8,128)S(1)}, u32[]{:S(2)}, u32[]{:S(2)}) collective-permute-start(f32[96,128]{1,0:T(8,128)S(1)} %get-tuple-element.60), channel_id=1, source_target_pairs={{0,3},{1,0},{2,1},{3,2},{4,7},{5,4},{6,5},{7,6},{8,11},{9,8},{10,9... | collective-permute-start | bytes 147464 | tf_op jit(solution)/shard_map/ppermute | solution.py:1061
  8.5 4.1 %tables.1 = (bf16[2,2,256,8192]{3,2,1,0:T(8,128)(2,1)S(1)}, f32[2,16,8192]{2,1,0:T(8,128)S(1)}, s32[4]{0:T(128)S(4)}) custom-call(s32[8]{0:T(128)S(4)} %get-tuple-element.49.refs_0_, s32[40,8192]{1,0:T(8,128)S(1)} %copy-done, f32[96,128]{1,0:T(8,128)S(1)} %get-tuple-element.53.refs_2_.refs_10_), custom_call_target="tpu_custom_call" | custom-call | tf_op jit(solution)/shard_map/tables/pallas_call | solution.py:518
  12.7 5.9 %markers.2 = (f32[3,128,128]{2,1,0:T(8,128)S(1)}, f32[3,128,128]{2,1,0:T(8,128)S(1)}, f32[120,128]{1,0:T(8,128)S(1)}, f32[168,128]{1,0:T(8,128)S(1)}, f32[120,128]{1,0:T(8,128)S(1)}, /*index=5*/f32[168,128]{1,0:T(8,128)S(1)}) custom-call(s32[8]{0:T(128)S(4)} %get-tuple-element.49.refs_0_, s32[4]{0:T(128)S(4)} %get-tuple-element.54.refs_1_, ...), custom_call_target="tpu_custom_call" | custom-call | tf_op jit(solution)/shard_map/markers/pallas_call | solution.py:730
  18.6 1.7 %collective-permute-start.5 = (f32[168,128]{1,0:T(8,128)S(1)}, f32[168,128]{1,0:T(8,128)S(1)}, u32[]{:S(2)}, u32[]{:S(2)}) collective-permute-start(f32[168,128]{1,0:T(8,128)S(1)} %get-tuple-element.67), channel_id=1, source_target_pairs={{0,3},{1,0},{2,1},{3,2},{4,7},{5,4},{6,5},{7,6},{8,11},{9,8},{10,9... | collective-permute-start | bytes 258056 | tf_op jit(solution)/shard_map/ppermute | solution.py:1061
  20.4 2.7 %bulk.2 = (f32[19,256,128]{2,1,0:T(8,128)S(1)}, f32[8,19,16,128]{3,2,1,0:T(8,128)S(1)}) custom-call(s32[8]{0:T(128)S(4)} %get-tuple-element.49.refs_0_, f32[19,256,128]{2,1,0:T(8,128)S(1)} %get-tuple-element.50.refs_1_, f32[3,128,128]{2,1,0:T(8,128)S(1)} %get-tuple-element.61.refs_2_, f32[3,128,128]{2,1,0:T(8,128)S(1)} %get-tuple-element.62.refs_3_.refs_7_), custom_call_target="tpu_custom_call" | custom-call | tf_op jit(solution)/shard_map/bulk/pallas_call | solution.py:882
  23.1 1.5 %collective-permute-done.4.refs_4_ = f32[120,128]{1,0:T(8,128)S(1)} collective-permute-done((f32[120,128]{1,0:T(8,128)S(1)}, f32[120,128]{1,0:T(8,128)S(1)}, u32[]{:S(2)}, u32[]{:S(2)}) %collective-permute-start.4) | collective-permute-done | bytes 61472 | tf_op jit(solution)/shard_map/ppermute | solution.py:1061
  25.1 1.5 %collective-permute-start.6 = (f32[5,16,128]{2,1,0:T(8,128)S(1)}, f32[5,16,128]{2,1,0:T(8,128)S(1)}, u32[]{:S(2)}, u32[]{:S(2)}) collective-permute-start(f32[5,16,128]{2,1,0:T(8,128)S(1)} %get-tuple-element.69), channel_id=1, source_target_pairs={{0,4},{8,12},{16,20},{24,28},{4,0},{12,8},{20,16},{28,24},{1,5},{9... | collective-permute-start | bytes 122888 | tf_op jit(solution)/shard_map/ppermute | solution.py:1067
  26.6 3.6 %collective-permute-start.7 = (f32[5,16,128]{2,1,0:T(8,128)S(1)}, f32[5,16,128]{2,1,0:T(8,128)S(1)}, u32[]{:S(2)}, u32[]{:S(2)}) collective-permute-start(f32[5,16,128]{2,1,0:T(8,128)S(1)} %get-tuple-element.70), channel_id=1, source_target_pairs={{4,8},{12,16},{20,24},{28,0},{8,4},{16,12},{24,20},{0,28},{5,9},{1... | collective-permute-start | bytes 122888 | tf_op jit(solution)/shard_map/ppermute | solution.py:1067
  30.2 1.6 %patch.2.refs_1_ = f32[19,256,128]{2,1,0:T(8,128)S(1)} custom-call(s32[8]{0:T(128)S(4)} %get-tuple-element.49.refs_0_, f32[8,19,16,128]{3,2,1,0:T(8,128)S(1)} %get-tuple-element.63.refs_1_, f32[120,128]{1,0:T(8,128)S(1)} %get-tuple-element.64.refs_2_, f32[168,128]{1,0:T(8,128)S(1)} %collective-permute-done.3.refs_3_, ...), custom_call_target="tpu_custom_call", output_to_operand_aliasing={{}: (6, {})} | custom-call | tf_op jit(solution)/shard_map/patch/pallas_call | solution.py:990
  31.9 1.5 %collective-permute-done.7.two = f32[5,16,128]{2,1,0:T(8,128)S(1)} collective-permute-done((f32[5,16,128]{2,1,0:T(8,128)S(1)}, f32[5,16,128]{2,1,0:T(8,128)S(1)}, u32[]{:S(2)}, u32[]{:S(2)}) %collective-permute-start.7) | collective-permute-done | bytes 40992 | tf_op jit(solution)/shard_map/ppermute | solution.py:1067
  34.0 1.1 %collective-permute-start.9 = (f32[96,128]{1,0:T(8,128)S(1)}, f32[96,128]{1,0:T(8,128)S(1)}, u32[]{:S(2)}, u32[]{:S(2)}) collective-permute-start(f32[96,128]{1,0:T(8,128)S(1)} %get-tuple-element.77), channel_id=1, source_target_pairs={{0,2},{1,3},{2,0},{3,1},{4,6},{5,7},{6,4},{7,5},{8,10},{9,11},{10,... | collective-permute-start | bytes 147464 | tf_op jit(solution)/shard_map/ppermute | solution.py:1061
  35.1 1.4 %collective-permute-start.10 = (f32[96,128]{1,0:T(8,128)S(1)}, f32[96,128]{1,0:T(8,128)S(1)}, u32[]{:S(2)}, u32[]{:S(2)}) collective-permute-start(f32[96,128]{1,0:T(8,128)S(1)} %get-tuple-element.78), channel_id=1, source_target_pairs={{0,3},{1,0},{2,1},{3,2},{4,7},{5,4},{6,5},{7,6},{8,11},{9,8},{10,9... | collective-permute-start | bytes 147464 | tf_op jit(solution)/shard_map/ppermute | solution.py:1061
  36.5 1.0 %columns.3 = (f32[48,128]{1,0:T(8,128)S(1)}, f32[48,128]{1,0:T(8,128)S(1)}) custom-call(s32[8]{0:T(128)S(4)} %get-tuple-element.49.refs_0_, f32[19,256,128]{2,1,0:T(8,128)S(1)} %patch.2.refs_1_, f32[5,16,128]{2,1,0:T(8,128)S(1)} %get-tuple-element.71.refs_2_, f32[5,16,128]{2,1,0:T(8,128)S(1)} %get-tuple-element.72.refs_3_), custom_call_target="tpu_custom_call" | custom-call | tf_op jit(solution)/shard_map/columns/pallas_call | solution.py:408
  37.5 1.1 %collective-permute-done.9.refs_12_ = f32[96,128]{1,0:T(8,128)S(1)} collective-permute-done((f32[96,128]{1,0:T(8,128)S(1)}, f32[96,128]{1,0:T(8,128)S(1)}, u32[]{:S(2)}, u32[]{:S(2)}) %collective-permute-start.9) | collective-permute-done | bytes 49184 | tf_op jit(solution)/shard_map/ppermute | solution.py:1061
  38.6 6.2 %markers.3 = (f32[3,128,128]{2,1,0:T(8,128)S(1)}, f32[3,128,128]{2,1,0:T(8,128)S(1)}, f32[120,128]{1,0:T(8,128)S(1)}, f32[168,128]{1,0:T(8,128)S(1)}, f32[120,128]{1,0:T(8,128)S(1)}, /*index=5*/f32[168,128]{1,0:T(8,128)S(1)}) custom-call(s32[8]{0:T(128)S(4)} %get-tuple-element.49.refs_0_, s32[4]{0:T(128)S(4)} %get-tuple-element.54.refs_1_, ...), custom_call_target="tpu_custom_call" | custom-call | tf_op jit(solution)/shard_map/markers/pallas_call | solution.py:730
  44.7 0.8 %collective-permute-start.11 = (f32[168,128]{1,0:T(8,128)S(1)}, f32[168,128]{1,0:T(8,128)S(1)}, u32[]{:S(2)}, u32[]{:S(2)}) collective-permute-start(f32[168,128]{1,0:T(8,128)S(1)} %get-tuple-element.83), channel_id=1, source_target_pairs={{0,1},{1,2},{2,3},{3,0},{4,5},{5,6},{6,7},{7,4},{8,9},{9,10},{10,1... | collective-permute-start | bytes 258056 | tf_op jit(solution)/shard_map/ppermute | solution.py:1061
  45.5 1.0 %collective-permute-start.13 = (f32[168,128]{1,0:T(8,128)S(1)}, f32[168,128]{1,0:T(8,128)S(1)}, u32[]{:S(2)}, u32[]{:S(2)}) collective-permute-start(f32[168,128]{1,0:T(8,128)S(1)} %get-tuple-element.85), channel_id=1, source_target_pairs={{0,3},{1,0},{2,1},{3,2},{4,7},{5,4},{6,5},{7,6},{8,11},{9,8},{10,9... | collective-permute-start | bytes 258056 | tf_op jit(solution)/shard_map/ppermute | solution.py:1061
  47.2 3.1 %bulk.3 = (f32[19,256,128]{2,1,0:T(8,128)S(1)}, f32[8,19,16,128]{3,2,1,0:T(8,128)S(1)}, f32[3,128,128]{2,1,0:T(8,128)}, f32[3,128,128]{2,1,0:T(8,128)}) custom-call(s32[8]{0:T(128)S(4)} %get-tuple-element.49.refs_0_, f32[19,256,128]{2,1,0:T(8,128)S(1)} %patch.2.refs_1_, f32[5,16,128]{2,1,0:T(8,128)S(1)} %get-tuple-element.71.refs_2_, ...), custom_call_target="tpu_custom_call" | custom-call | tf_op jit(solution)/shard_map/bulk/pallas_call | solution.py:882
  51.4 3.6 %collective-permute-start.15 = (f32[5,16,128]{2,1,0:T(8,128)S(1)}, f32[5,16,128]{2,1,0:T(8,128)S(1)}, u32[]{:S(2)}, u32[]{:S(2)}) collective-permute-start(f32[5,16,128]{2,1,0:T(8,128)S(1)} %get-tuple-element.89), channel_id=1, source_target_pairs={{4,8},{12,16},{20,24},{28,0},{8,4},{16,12},{24,20},{0,28},{5,9},{1... | collective-permute-start | bytes 122888 | tf_op jit(solution)/shard_map/ppermute | solution.py:1067
  55.1 2.5 %patch.3 = (f32[19,256,128]{2,1,0:T(8,128)S(1)}, f32[19,256,128]{2,1,0:T(8,128)}) custom-call(s32[8]{0:T(128)S(4)} %get-tuple-element.49.refs_0_, f32[8,19,16,128]{3,2,1,0:T(8,128)S(1)} %get-tuple-element.81.refs_1_, f32[120,128]{1,0:T(8,128)S(1)} %get-tuple-element.82.refs_2_.refs_4_, ...), custom_call_target="tpu_custom_call", output_to_operand_aliasing={{0}: (6, {})} | custom-call | tf_op jit(solution)/shard_map/patch/pallas_call | solution.py:990
  58.2 0.9 %finish.1 = f32[19,16,16,128]{3,2,1,0:T(8,128)} custom-call(f32[19,256,128]{2,1,0:T(8,128)S(1)} %get-tuple-element.87.refs_0_, f32[5,16,128]{2,1,0:T(8,128)S(1)} %get-tuple-element.90.refs_1_, f32[5,16,128]{2,1,0:T(8,128)S(1)} %get-tuple-element.91.refs_2_, f32[19,16,16,128]{3,2,1,0:T(8,128)} %bitcast.56), custom_call_target="tpu_custom_call", output_to_operand_aliasing={{}: (3, {})} | custom-call | tf_op jit(solution)/shard_map/finish/pallas_call | solution.py:1032
  (33 shorter events, 4.8 us)
Async XLA Ops:
  2.5 6.1 %copy-start = (s32[40,8192]{1,0:T(8,128)S(1)}, s32[40,8192]{1,0:T(8,128)}, u32[]{:S(2)}) copy-start(s32[40,8192]{1,0:T(8,128)} %refs_1_.1) | copy-start | bytes 3932164
  3.5 9.2 %copy-start.1 = (f32[1,1,2,8192]{3,2,1,0:T(2,128)S(1)}, f32[1,1,2,8192]{3,2,1,0:T(2,128)}, u32[]{:S(2)}) copy-start(f32[1,1,2,8192]{3,2,1,0:T(2,128)} %param.13) | copy-start | bytes 196612
  3.5 9.2 %copy-start.2 = (f32[1,1,2,8192]{3,2,1,0:T(2,128)S(1)}, f32[1,1,2,8192]{3,2,1,0:T(2,128)}, u32[]{:S(2)}) copy-start(f32[1,1,2,8192]{3,2,1,0:T(2,128)} %param.15) | copy-start | bytes 196612
  3.5 9.2 %copy-start.3 = (f32[1,1,2,3,8192]{4,2,3,1,0:T(2,128)S(1)}, f32[1,1,2,3,8192]{4,2,3,1,0:T(2,128)}, u32[]{:S(2)}) copy-start(f32[1,1,2,3,8192]{4,2,3,1,0:T(2,128)} %param.17) | copy-start | bytes 589828
  4.1 8.6 %collective-permute-start = (f32[96,128]{1,0:T(8,128)S(1)}, f32[96,128]{1,0:T(8,128)S(1)}, u32[]{:S(2)}, u32[]{:S(2)}) collective-permute-start(f32[96,128]{1,0:T(8,128)S(1)} %get-tuple-element.58), channel_id=1, source_target_pairs={{0,1},{1,2},{2,3},{3,0},{4,5},{5,6},{6,7},{7,4},{8,9},{9,10},{10,1... | collective-permute-start | bytes 147464 | tf_op jit(solution)/shard_map/ppermute | solution.py:1061
  4.6 8.1 %collective-permute-start.1 = (f32[96,128]{1,0:T(8,128)S(1)}, f32[96,128]{1,0:T(8,128)S(1)}, u32[]{:S(2)}, u32[]{:S(2)}) collective-permute-start(f32[96,128]{1,0:T(8,128)S(1)} %get-tuple-element.59), channel_id=1, source_target_pairs={{0,2},{1,3},{2,0},{3,1},{4,6},{5,7},{6,4},{7,5},{8,10},{9,11},{10,... | collective-permute-start | bytes 147464 | tf_op jit(solution)/shard_map/ppermute | solution.py:1061
  7.2 5.5 %collective-permute-start.2 = (f32[96,128]{1,0:T(8,128)S(1)}, f32[96,128]{1,0:T(8,128)S(1)}, u32[]{:S(2)}, u32[]{:S(2)}) collective-permute-start(f32[96,128]{1,0:T(8,128)S(1)} %get-tuple-element.60), channel_id=1, source_target_pairs={{0,3},{1,0},{2,1},{3,2},{4,7},{5,4},{6,5},{7,6},{8,11},{9,8},{10,9... | collective-permute-start | bytes 147464 | tf_op jit(solution)/shard_map/ppermute | solution.py:1061
  18.6 6.0 %collective-permute-start.3 = (f32[168,128]{1,0:T(8,128)S(1)}, f32[168,128]{1,0:T(8,128)S(1)}, u32[]{:S(2)}, u32[]{:S(2)}) collective-permute-start(f32[168,128]{1,0:T(8,128)S(1)} %get-tuple-element.65), channel_id=1, source_target_pairs={{0,1},{1,2},{2,3},{3,0},{4,5},{5,6},{6,7},{7,4},{8,9},{9,10},{10,1... | collective-permute-start | bytes 258056 | tf_op jit(solution)/shard_map/ppermute | solution.py:1061
  18.6 6.0 %collective-permute-start.5 = (f32[168,128]{1,0:T(8,128)S(1)}, f32[168,128]{1,0:T(8,128)S(1)}, u32[]{:S(2)}, u32[]{:S(2)}) collective-permute-start(f32[168,128]{1,0:T(8,128)S(1)} %get-tuple-element.67), channel_id=1, source_target_pairs={{0,3},{1,0},{2,1},{3,2},{4,7},{5,4},{6,5},{7,6},{8,11},{9,8},{10,9... | collective-permute-start | bytes 258056 | tf_op jit(solution)/shard_map/ppermute | solution.py:1061
  20.4 4.2 %collective-permute-start.4 = (f32[120,128]{1,0:T(8,128)S(1)}, f32[120,128]{1,0:T(8,128)S(1)}, u32[]{:S(2)}, u32[]{:S(2)}) collective-permute-start(f32[120,128]{1,0:T(8,128)S(1)} %get-tuple-element.66), channel_id=1, source_target_pairs={{0,2},{1,3},{2,0},{3,1},{4,6},{5,7},{6,4},{7,5},{8,10},{9,11},{10,... | collective-permute-start | bytes 184328 | tf_op jit(solution)/shard_map/ppermute | solution.py:1061
  25.1 6.7 %collective-permute-start.6 = (f32[5,16,128]{2,1,0:T(8,128)S(1)}, f32[5,16,128]{2,1,0:T(8,128)S(1)}, u32[]{:S(2)}, u32[]{:S(2)}) collective-permute-start(f32[5,16,128]{2,1,0:T(8,128)S(1)} %get-tuple-element.69), channel_id=1, source_target_pairs={{0,4},{8,12},{16,20},{24,28},{4,0},{12,8},{20,16},{28,24},{1,5},{9... | collective-permute-start | bytes 122888 | tf_op jit(solution)/shard_map/ppermute | solution.py:1067
  26.6 6.7 %collective-permute-start.7 = (f32[5,16,128]{2,1,0:T(8,128)S(1)}, f32[5,16,128]{2,1,0:T(8,128)S(1)}, u32[]{:S(2)}, u32[]{:S(2)}) collective-permute-start(f32[5,16,128]{2,1,0:T(8,128)S(1)} %get-tuple-element.70), channel_id=1, source_target_pairs={{4,8},{12,16},{20,24},{28,0},{8,4},{16,12},{24,20},{0,28},{5,9},{1... | collective-permute-start | bytes 122888 | tf_op jit(solution)/shard_map/ppermute | solution.py:1067
  33.9 3.6 %collective-permute-start.8 = (f32[96,128]{1,0:T(8,128)S(1)}, f32[96,128]{1,0:T(8,128)S(1)}, u32[]{:S(2)}, u32[]{:S(2)}) collective-permute-start(f32[96,128]{1,0:T(8,128)S(1)} %get-tuple-element.76), channel_id=1, source_target_pairs={{0,1},{1,2},{2,3},{3,0},{4,5},{5,6},{6,7},{7,4},{8,9},{9,10},{10,1... | collective-permute-start | bytes 147464 | tf_op jit(solution)/shard_map/ppermute | solution.py:1061
  34.0 4.6 %collective-permute-start.9 = (f32[96,128]{1,0:T(8,128)S(1)}, f32[96,128]{1,0:T(8,128)S(1)}, u32[]{:S(2)}, u32[]{:S(2)}) collective-permute-start(f32[96,128]{1,0:T(8,128)S(1)} %get-tuple-element.77), channel_id=1, source_target_pairs={{0,2},{1,3},{2,0},{3,1},{4,6},{5,7},{6,4},{7,5},{8,10},{9,11},{10,... | collective-permute-start | bytes 147464 | tf_op jit(solution)/shard_map/ppermute | solution.py:1061
  35.1 3.5 %collective-permute-start.10 = (f32[96,128]{1,0:T(8,128)S(1)}, f32[96,128]{1,0:T(8,128)S(1)}, u32[]{:S(2)}, u32[]{:S(2)}) collective-permute-start(f32[96,128]{1,0:T(8,128)S(1)} %get-tuple-element.78), channel_id=1, source_target_pairs={{0,3},{1,0},{2,1},{3,2},{4,7},{5,4},{6,5},{7,6},{8,11},{9,8},{10,9... | collective-permute-start | bytes 147464 | tf_op jit(solution)/shard_map/ppermute | solution.py:1061
  44.7 6.2 %collective-permute-start.11 = (f32[168,128]{1,0:T(8,128)S(1)}, f32[168,128]{1,0:T(8,128)S(1)}, u32[]{:S(2)}, u32[]{:S(2)}) collective-permute-start(f32[168,128]{1,0:T(8,128)S(1)} %get-tuple-element.83), channel_id=1, source_target_pairs={{0,1},{1,2},{2,3},{3,0},{4,5},{5,6},{6,7},{7,4},{8,9},{9,10},{10,1... | collective-permute-start | bytes 258056 | tf_op jit(solution)/shard_map/ppermute | solution.py:1061
  45.5 5.4 %collective-permute-start.13 = (f32[168,128]{1,0:T(8,128)S(1)}, f32[168,128]{1,0:T(8,128)S(1)}, u32[]{:S(2)}, u32[]{:S(2)}) collective-permute-start(f32[168,128]{1,0:T(8,128)S(1)} %get-tuple-element.85), channel_id=1, source_target_pairs={{0,3},{1,0},{2,1},{3,2},{4,7},{5,4},{6,5},{7,6},{8,11},{9,8},{10,9... | collective-permute-start | bytes 258056 | tf_op jit(solution)/shard_map/ppermute | solution.py:1061
  46.5 4.4 %collective-permute-start.12 = (f32[120,128]{1,0:T(8,128)S(1)}, f32[120,128]{1,0:T(8,128)S(1)}, u32[]{:S(2)}, u32[]{:S(2)}) collective-permute-start(f32[120,128]{1,0:T(8,128)S(1)} %get-tuple-element.84), channel_id=1, source_target_pairs={{0,2},{1,3},{2,0},{3,1},{4,6},{5,7},{6,4},{7,5},{8,10},{9,11},{10,... | collective-permute-start | bytes 184328 | tf_op jit(solution)/shard_map/ppermute | solution.py:1061
  51.4 6.2 %collective-permute-start.14 = (f32[5,16,128]{2,1,0:T(8,128)S(1)}, f32[5,16,128]{2,1,0:T(8,128)S(1)}, u32[]{:S(2)}, u32[]{:S(2)}) collective-permute-start(f32[5,16,128]{2,1,0:T(8,128)S(1)} %get-tuple-element.88), channel_id=1, source_target_pairs={{0,4},{8,12},{16,20},{24,28},{4,0},{12,8},{20,16},{28,24},{1,5},{9... | collective-permute-start | bytes 122888 | tf_op jit(solution)/shard_map/ppermute | solution.py:1067
  51.4 6.8 %collective-permute-start.15 = (f32[5,16,128]{2,1,0:T(8,128)S(1)}, f32[5,16,128]{2,1,0:T(8,128)S(1)}, u32[]{:S(2)}, u32[]{:S(2)}) collective-permute-start(f32[5,16,128]{2,1,0:T(8,128)S(1)} %get-tuple-element.89), channel_id=1, source_target_pairs={{4,8},{12,16},{20,24},{28,0},{8,4},{16,12},{24,20},{0,28},{5,9},{1... | collective-permute-start | bytes 122888 | tf_op jit(solution)/shard_map/ppermute | solution.py:1067

commit v5 on v4

--- a/solution.py
+++ b/solution.py
@@ -207,7 +207,7 @@
     return planes
 
 
-def write_sections(sh, plan, f, low, high, outs):
+def write_sections(sh, plan, f, low, high, outs, held):
     me = lax.axis_index("gy")
     for shift in range(sh.tiles):
         owner = lax.rem(me + shift, sh.tiles)
@@ -217,6 +217,8 @@
             @pl.when(x >= 0)
             def _():
                 planes = plane_of(sh, f, x, low, high)
+                for q, value in enumerate(planes):
+                    held[owner * sh.slots + slot, q] = value
                 density, momentum = moments(planes)
                 inverse = 1.0 / density
                 for axis in range(3):
@@ -327,18 +329,20 @@
 
 def section_kernel(sh, has_edges, plan, f, *refs):
     low, high = refs[:2] if has_edges else (None, None)
-    write_sections(sh, plan, f, low, high, refs[-sh.tiles :])
+    write_sections(sh, plan, f, low, high, refs[-sh.tiles - 1 : -1], refs[-1])
 
 
 def make_sections(sh, plan, f, edges, after):
-    return pl.pallas_call(
+    out = pl.pallas_call(
         lambda *refs: section_kernel(sh, bool(edges), *refs),
-        out_shape=[pltpu.VMEM((sh.section, LANES), F32)] * sh.tiles,
+        out_shape=[pltpu.VMEM((sh.section, LANES), F32)] * sh.tiles
+        + [pltpu.VMEM((sh.tiles * sh.slots, 19, sh.levels, LANES), F32)],
         in_specs=[SM] + [VM] * (1 + len(edges) + len(after)),
-        out_specs=[VM] * sh.tiles,
+        out_specs=[VM] * (sh.tiles + 1),
         compiler_params=PARAMS,
         name="sections",
     )(plan, f, *edges, *after)
+    return out[:-1], in_vmem(out[-1])
 
 
 def column_kernel(sh, has_edges, *refs):
@@ -813,25 +817,23 @@
 def bulk_kernel(sh, has_edges, last, plan, f, *refs):
     low, high = refs[:2] if has_edges else (None, None)
     refs = refs[2 * has_edges :]
-    loads, filt, out, planes = refs[:4]
+    loads, filt, out = refs[:3]
     xs = sh.xs
-    for k in range(sh.tiles * sh.slots):
-
-        @pl.when(plan[k] >= 0)
-        def _():
-            for q, value in enumerate(plane_of(sh, f, lax.rem(plan[k], xs), low, high)):
-                planes[k, q] = value
-
     xrows = iota((xs, LANES), 0)
+    copies = []
     if last:
+        masked, sems = refs[-2:]
         rows = iota((sh.slots * sh.groups, LANES), 0) % sh.slots
         used = jnp.zeros((sh.slots * sh.groups, LANES), jnp.int32)
         for slot in range(sh.slots):
             there = (rotor_at(sh, plan, slot) >= 0).astype(jnp.int32)
             used = jnp.where(rows == slot, there, used)
-        for source, target in ((loads, refs[4]), (filt, refs[5])):
+        for k, source in enumerate((loads, filt)):
             for axis in range(3):
-                target[axis] = jnp.where(used > 0, source[axis], 0.0)
+                masked[k, axis] = jnp.where(used > 0, source[axis], 0.0)
+            copy = pltpu.make_async_copy(masked.at[k], refs[3 + k], sems.at[k])
+            copy.start()
+            copies.append(copy)
 
     def level(z, bottom, top):
         at = aligned(z * xs, xs)
@@ -870,20 +872,22 @@
 
     lax.fori_loop(1, sh.levels - 1, middle, 0)
     level(sh.levels - 1, False, True)
+    for copy in copies:
+        copy.wait()
 
 
 def do_bulk(sh, last, plan, f, edges, loads, filt):
-    out_shape = [
-        pltpu.VMEM((19, sh.levels * sh.xs, LANES), F32),
-        pltpu.VMEM((sh.tiles * sh.slots, 19, sh.levels, LANES), F32),
-    ]
+    out_shape = [pltpu.VMEM((19, sh.levels * sh.xs, LANES), F32)]
+    scratch = []
     if last:
         out_shape += [jax.ShapeDtypeStruct(loads.shape, F32)] * 2
+        scratch = [pltpu.VMEM((2, *loads.shape), F32), pltpu.SemaphoreType.DMA((2,))]
     return pl.pallas_call(
         lambda *refs: bulk_kernel(sh, bool(edges), last, *refs),
         out_shape=out_shape,
         in_specs=[SM] + [VM] * (3 + len(edges)),
-        out_specs=[VM] * len(out_shape),
+        out_specs=[VM] + [HB] * (len(out_shape) - 1),
+        scratch_shapes=scratch,
         compiler_params=PARAMS,
         name="bulk",
     )(plan, f, *edges, loads, filt)
@@ -1109,10 +1113,10 @@
         last = step == sh.steps - 1
         if step == 0:
             columns = make_columns(sh, plan, f, edges)
-            sections = make_sections(sh, plan, f, edges, columns)
+            sections, planes = make_sections(sh, plan, f, edges, columns)
             tables = make_tables(sh, plan, marker_cell, in_vmem(sections[0]))
         else:
-            sections = make_sections(sh, plan, f, edges, ())
+            sections, planes = make_sections(sh, plan, f, edges, ())
             columns = make_columns(sh, plan, f, edges)
         sections = [sections[0]] + [
             shifted(sections[by], "gy", by) for by in range(1, sh.tiles)
@@ -1132,8 +1136,7 @@
         forces = [in_vmem(force) for force in forces]
         bulk = do_bulk(sh, last, plan, f, edges, loads, filt)
         if last:
-            loads_out, filt_out = bulk[2:]
-        planes = in_vmem(bulk[1])
+            loads_out, filt_out = bulk[1:]
         bulk = in_vmem(bulk[0])
         sent = make_edges(sh, plan, f, edges, forces, bulk)
         done = do_patch(sh, last, plan, planes, forces, bulk)

time: 59.2 us -> 59.5 us (level)
  Pallas kernels: 33 us -> 16.6 us
  starting transfers between devices: 20 us -> 33.6 us
  waiting for transfers between devices: 5.29 us -> 8.1 us
    ppermute x12, starting transfers between devices: 11.3 us -> 25.1 us  [shifted(): return lax.ppermute(x, axis, [(i, (i + by) % count) for i in range(count)])]
    pallas_call x2, Pallas kernels: 12.1 us -> 1.36 us  [do_markers(): pl.pallas_call(lambda *refs: marker_kernel(sh, step, *refs), out_shape=[d...]
    pallas_call x1, Pallas kernels: 4.06 us -> 0.07 us  [make_tables(): pl.pallas_call(lambda *refs: table_kernel(sh, *refs), out_shape=[pltpu.VM...]
    ppermute x12, waiting for transfers between devices: 3.19 us -> 5.11 us  [shifted(): return lax.ppermute(x, axis, [(i, (i + by) % count) for i in range(count)])]
    pallas_call x2, Pallas kernels: 5.85 us -> 4.2 us  [do_bulk(): pl.pallas_call(lambda *refs: bulk_kernel(sh, bool(edges), last, *refs), o...]
    ppermute x4, waiting for transfers between devices: 2.11 us -> 3 us  [swapped(): return lax.ppermute(x, axis, pairs + [(b, a) for a, b in pairs])]
  transfers between devices with their start and end apart: 16 -> 16, of which waited for: 6 -> 8; matrix products, arithmetic and copies ran while one was open for 0% -> 0% of each run, Pallas kernels for 25% -> 16%
where the time goes in v5:
time: 59.5 us; the launch traced here: 59.3 us
  starting transfers between devices  33.6 us (56%)
  Pallas kernels  16.6 us (28%)
  waiting for transfers between devices  8.1 us (14%)
  between operations  0.95 us (2%)
    ppermute x12, starting transfers between devices, shifted(): return lax.ppermute(x, axis, [(i, (i + by) % count) for i in range(count)])  25.1 us
    ppermute x4, starting transfers between devices, swapped(): return lax.ppermute(x, axis, pairs + [(b, a) for a, b in pairs])  8.54 us
    ppermute x12, waiting for transfers between devices, shifted(): return lax.ppermute(x, axis, [(i, (i + by) % count) for i in range(count)])  5.11 us
    pallas_call x2, Pallas kernels, do_bulk(): pl.pallas_call(lambda *refs: bulk_kernel(sh, bool(edges), last, *refs), o...  4.2 us
    pallas_call x2, Pallas kernels, do_patch(): pl.pallas_call(lambda *refs: patch_kernel(sh, last, *refs), out_shape=out...  4.12 us
    ppermute x4, waiting for transfers between devices, swapped(): return lax.ppermute(x, axis, pairs + [(b, a) for a, b in pairs])  3 us
    pallas_call x2, Pallas kernels, make_columns(): pl.pallas_call(lambda *refs: column_kernel(sh, bool(edges), *refs), out_s...  1.94 us
    pallas_call x1, Pallas kernels, start(): pl.pallas_call(lambda *refs: start_kernel(sh, *refs), out_shape=[pltpu.SM...  1.84 us
  transfers between devices with their start and end apart: 16, of which 8 were waited for; matrix products, arithmetic and copies ran while one was open for 0% of the time, Pallas kernels for 16%

profile of v5, /device:TPU:0, one launch (start us, length us, event | category | flops | bytes accessed | tf_op | source)
XLA Modules:
  0.0 59.3 jit_solution(11118497954032777276)
XLA Ops:
  0.6 1.8 %start.1 = (s32[8]{0:T(128)S(4)}, f32[6,128,128]{2,1,0:T(8,128)S(1)}, f32[19,256,128]{2,1,0:T(8,128)S(1)}) custom-call(s32[3,40]{1,0:T(4,128)} %bitcast.60, s32[2,40]{1,0:T(2,128)} %bitcast.61, f32[128,128]{1,0:T(8,128)} %bitcast.58, f32[128,128]{1,0:T(8,128)} %bitcast.59, f32[19,256,128]{2,1,0:T(8,128)} %bitcast.57), custom_call_target="tpu_custom_call" | custom-call | tf_op jit(solution)/shard_map/start/pallas_call | solution.py:302
  2.5 1.0 %columns.2 = (f32[48,128]{1,0:T(8,128)S(1)}, f32[48,128]{1,0:T(8,128)S(1)}) custom-call(s32[8]{0:T(128)S(4)} %get-tuple-element.48.refs_0_, f32[19,256,128]{2,1,0:T(8,128)S(1)} %get-tuple-element.49.refs_1_), custom_call_target="tpu_custom_call" | custom-call | tf_op jit(solution)/shard_map/columns/pallas_call | solution.py:412
  4.6 2.6 %collective-permute-start.1 = (f32[96,128]{1,0:T(8,128)S(1)}, f32[96,128]{1,0:T(8,128)S(1)}, u32[]{:S(2)}, u32[]{:S(2)}) collective-permute-start(f32[96,128]{1,0:T(8,128)S(1)} %get-tuple-element.59), channel_id=1, source_target_pairs={{0,2},{1,3},{2,0},{3,1},{4,6},{5,7},{6,4},{7,5},{8,10},{9,11},{10,... | collective-permute-start | bytes 147464 | tf_op jit(solution)/shard_map/ppermute | solution.py:1065
  7.2 1.4 %collective-permute-start.2 = (f32[96,128]{1,0:T(8,128)S(1)}, f32[96,128]{1,0:T(8,128)S(1)}, u32[]{:S(2)}, u32[]{:S(2)}) collective-permute-start(f32[96,128]{1,0:T(8,128)S(1)} %get-tuple-element.60), channel_id=1, source_target_pairs={{0,3},{1,0},{2,1},{3,2},{4,7},{5,4},{6,5},{7,6},{8,11},{9,8},{10,9... | collective-permute-start | bytes 147464 | tf_op jit(solution)/shard_map/ppermute | solution.py:1065
  9.2 1.1 %collective-permute-done.2.refs_13_ = f32[96,128]{1,0:T(8,128)S(1)} collective-permute-done((f32[96,128]{1,0:T(8,128)S(1)}, f32[96,128]{1,0:T(8,128)S(1)}, u32[]{:S(2)}, u32[]{:S(2)}) %collective-permute-start.2) | collective-permute-done | bytes 49184 | tf_op jit(solution)/shard_map/ppermute | solution.py:1065
  10.9 6.9 %collective-permute-start.3 = (f32[168,128]{1,0:T(8,128)S(1)}, f32[168,128]{1,0:T(8,128)S(1)}, u32[]{:S(2)}, u32[]{:S(2)}) collective-permute-start(f32[168,128]{1,0:T(8,128)S(1)} %get-tuple-element.62), channel_id=1, source_target_pairs={{0,1},{1,2},{2,3},{3,0},{4,5},{5,6},{6,7},{7,4},{8,9},{9,10},{10,1... | collective-permute-start | bytes 258056 | tf_op jit(solution)/shard_map/ppermute | solution.py:1065
  17.8 2.9 %collective-permute-start.4 = (f32[120,128]{1,0:T(8,128)S(1)}, f32[120,128]{1,0:T(8,128)S(1)}, u32[]{:S(2)}, u32[]{:S(2)}) collective-permute-start(f32[120,128]{1,0:T(8,128)S(1)} %get-tuple-element.63), channel_id=1, source_target_pairs={{0,2},{1,3},{2,0},{3,1},{4,6},{5,7},{6,4},{7,5},{8,10},{9,11},{10,... | collective-permute-start | bytes 184328 | tf_op jit(solution)/shard_map/ppermute | solution.py:1065
  20.7 2.0 %bulk.2.refs_6_ = f32[19,256,128]{2,1,0:T(8,128)S(1)} custom-call(s32[8]{0:T(128)S(4)} %get-tuple-element.48.refs_0_, f32[19,256,128]{2,1,0:T(8,128)S(1)} %get-tuple-element.49.refs_1_, f32[3,128,128]{2,1,0:T(8,128)S(1)} %get-tuple-element.65.refs_2_, f32[3,128,128]{2,1,0:T(8,128)S(1)} %get-tuple-element.66.refs_3_.refs_7_), custom_call_target="tpu_custom_call" | custom-call | tf_op jit(solution)/shard_map/bulk/pallas_call | solution.py:885
  22.7 1.2 %collective-permute-done.4.refs_4_ = f32[120,128]{1,0:T(8,128)S(1)} collective-permute-done((f32[120,128]{1,0:T(8,128)S(1)}, f32[120,128]{1,0:T(8,128)S(1)}, u32[]{:S(2)}, u32[]{:S(2)}) %collective-permute-start.4) | collective-permute-done | bytes 61472 | tf_op jit(solution)/shard_map/ppermute | solution.py:1065
  24.5 2.2 %collective-permute-start.6 = (f32[5,16,128]{2,1,0:T(8,128)S(1)}, f32[5,16,128]{2,1,0:T(8,128)S(1)}, u32[]{:S(2)}, u32[]{:S(2)}) collective-permute-start(f32[5,16,128]{2,1,0:T(8,128)S(1)} %get-tuple-element.67), channel_id=1, source_target_pairs={{0,4},{8,12},{16,20},{24,28},{4,0},{12,8},{20,16},{28,24},{1,5},{9... | collective-permute-start | bytes 122888 | tf_op jit(solution)/shard_map/ppermute | solution.py:1071
  26.6 3.1 %collective-permute-start.7 = (f32[5,16,128]{2,1,0:T(8,128)S(1)}, f32[5,16,128]{2,1,0:T(8,128)S(1)}, u32[]{:S(2)}, u32[]{:S(2)}) collective-permute-start(f32[5,16,128]{2,1,0:T(8,128)S(1)} %get-tuple-element.68), channel_id=1, source_target_pairs={{4,8},{12,16},{20,24},{28,0},{8,4},{16,12},{24,20},{0,28},{5,9},{1... | collective-permute-start | bytes 122888 | tf_op jit(solution)/shard_map/ppermute | solution.py:1071
  29.8 1.6 %patch.2.refs_1_ = f32[19,256,128]{2,1,0:T(8,128)S(1)} custom-call(s32[8]{0:T(128)S(4)} %get-tuple-element.48.refs_0_, f32[8,19,16,128]{3,2,1,0:T(8,128)S(1)} %get-tuple-element.52.refs_1_, f32[120,128]{1,0:T(8,128)S(1)} %get-tuple-element.61.refs_2_, f32[168,128]{1,0:T(8,128)S(1)} %collective-permute-done.3.refs_3_, ...), custom_call_target="tpu_custom_call", output_to_operand_aliasing={{}: (6, {})} | custom-call | tf_op jit(solution)/shard_map/patch/pallas_call | solution.py:994
  31.4 1.9 %collective-permute-done.7.two = f32[5,16,128]{2,1,0:T(8,128)S(1)} collective-permute-done((f32[5,16,128]{2,1,0:T(8,128)S(1)}, f32[5,16,128]{2,1,0:T(8,128)S(1)}, u32[]{:S(2)}, u32[]{:S(2)}) %collective-permute-start.7) | collective-permute-done | bytes 40992 | tf_op jit(solution)/shard_map/ppermute | solution.py:1071
  34.0 1.1 %collective-permute-start.9 = (f32[96,128]{1,0:T(8,128)S(1)}, f32[96,128]{1,0:T(8,128)S(1)}, u32[]{:S(2)}, u32[]{:S(2)}) collective-permute-start(f32[96,128]{1,0:T(8,128)S(1)} %get-tuple-element.76), channel_id=1, source_target_pairs={{0,2},{1,3},{2,0},{3,1},{4,6},{5,7},{6,4},{7,5},{8,10},{9,11},{10,... | collective-permute-start | bytes 147464 | tf_op jit(solution)/shard_map/ppermute | solution.py:1065
  35.1 1.4 %collective-permute-start.10 = (f32[96,128]{1,0:T(8,128)S(1)}, f32[96,128]{1,0:T(8,128)S(1)}, u32[]{:S(2)}, u32[]{:S(2)}) collective-permute-start(f32[96,128]{1,0:T(8,128)S(1)} %get-tuple-element.77), channel_id=1, source_target_pairs={{0,3},{1,0},{2,1},{3,2},{4,7},{5,4},{6,5},{7,6},{8,11},{9,8},{10,9... | collective-permute-start | bytes 147464 | tf_op jit(solution)/shard_map/ppermute | solution.py:1065
  36.5 1.0 %columns.3 = (f32[48,128]{1,0:T(8,128)S(1)}, f32[48,128]{1,0:T(8,128)S(1)}) custom-call(s32[8]{0:T(128)S(4)} %get-tuple-element.48.refs_0_, f32[19,256,128]{2,1,0:T(8,128)S(1)} %patch.2.refs_1_, f32[5,16,128]{2,1,0:T(8,128)S(1)} %get-tuple-element.69.refs_2_, f32[5,16,128]{2,1,0:T(8,128)S(1)} %get-tuple-element.70.refs_3_), custom_call_target="tpu_custom_call" | custom-call | tf_op jit(solution)/shard_map/columns/pallas_call | solution.py:412
  37.5 1.1 %collective-permute-done.9.refs_12_ = f32[96,128]{1,0:T(8,128)S(1)} collective-permute-done((f32[96,128]{1,0:T(8,128)S(1)}, f32[96,128]{1,0:T(8,128)S(1)}, u32[]{:S(2)}, u32[]{:S(2)}) %collective-permute-start.9) | collective-permute-done | bytes 49184 | tf_op jit(solution)/shard_map/ppermute | solution.py:1065
  39.4 6.2 %collective-permute-start.11 = (f32[168,128]{1,0:T(8,128)S(1)}, f32[168,128]{1,0:T(8,128)S(1)}, u32[]{:S(2)}, u32[]{:S(2)}) collective-permute-start(f32[168,128]{1,0:T(8,128)S(1)} %get-tuple-element.79), channel_id=1, source_target_pairs={{0,1},{1,2},{2,3},{3,0},{4,5},{5,6},{6,7},{7,4},{8,9},{9,10},{10,1... | collective-permute-start | bytes 258056 | tf_op jit(solution)/shard_map/ppermute | solution.py:1065
  45.6 2.1 %collective-permute-start.12 = (f32[120,128]{1,0:T(8,128)S(1)}, f32[120,128]{1,0:T(8,128)S(1)}, u32[]{:S(2)}, u32[]{:S(2)}) collective-permute-start(f32[120,128]{1,0:T(8,128)S(1)} %get-tuple-element.80), channel_id=1, source_target_pairs={{0,2},{1,3},{2,0},{3,1},{4,6},{5,7},{6,4},{7,5},{8,10},{9,11},{10,... | collective-permute-start | bytes 184328 | tf_op jit(solution)/shard_map/ppermute | solution.py:1065
  47.6 2.2 %bulk.3 = (f32[19,256,128]{2,1,0:T(8,128)S(1)}, f32[3,128,128]{2,1,0:T(8,128)}, f32[3,128,128]{2,1,0:T(8,128)}) custom-call(s32[8]{0:T(128)S(4)} %get-tuple-element.48.refs_0_, f32[19,256,128]{2,1,0:T(8,128)S(1)} %patch.2.refs_1_, f32[5,16,128]{2,1,0:T(8,128)S(1)} %get-tuple-element.69.refs_2_, f32[5,16,128]{2,1,0:T(8,128)S(1)} %get-tuple-element.70.refs_3_, ...), custom_call_target="tpu_custom_call" | custom-call | tf_op jit(solution)/shard_map/bulk/pallas_call | solution.py:885
  49.8 1.1 %collective-permute-done.12.refs_4_.refs_6_ = f32[120,128]{1,0:T(8,128)S(1)} collective-permute-done((f32[120,128]{1,0:T(8,128)S(1)}, f32[120,128]{1,0:T(8,128)S(1)}, u32[]{:S(2)}, u32[]{:S(2)}) %collective-permute-start.12) | collective-permute-done | bytes 61472 | tf_op jit(solution)/shard_map/ppermute | solution.py:1065
  51.4 3.2 %collective-permute-start.15 = (f32[5,16,128]{2,1,0:T(8,128)S(1)}, f32[5,16,128]{2,1,0:T(8,128)S(1)}, u32[]{:S(2)}, u32[]{:S(2)}) collective-permute-start(f32[5,16,128]{2,1,0:T(8,128)S(1)} %get-tuple-element.87), channel_id=1, source_target_pairs={{4,8},{12,16},{20,24},{28,0},{8,4},{16,12},{24,20},{0,28},{5,9},{1... | collective-permute-start | bytes 122888 | tf_op jit(solution)/shard_map/ppermute | solution.py:1071
  54.6 2.5 %patch.3 = (f32[19,256,128]{2,1,0:T(8,128)S(1)}, f32[19,256,128]{2,1,0:T(8,128)}) custom-call(s32[8]{0:T(128)S(4)} %get-tuple-element.48.refs_0_, f32[8,19,16,128]{3,2,1,0:T(8,128)S(1)} %get-tuple-element.71.refs_1_, f32[120,128]{1,0:T(8,128)S(1)} %get-tuple-element.78.refs_2_.refs_4_, ...), custom_call_target="tpu_custom_call", output_to_operand_aliasing={{0}: (6, {})} | custom-call | tf_op jit(solution)/shard_map/patch/pallas_call | solution.py:994
  57.1 1.1 %collective-permute-done.15.two = f32[5,16,128]{2,1,0:T(8,128)S(1)} collective-permute-done((f32[5,16,128]{2,1,0:T(8,128)S(1)}, f32[5,16,128]{2,1,0:T(8,128)S(1)}, u32[]{:S(2)}, u32[]{:S(2)}) %collective-permute-start.15) | collective-permute-done | bytes 40992 | tf_op jit(solution)/shard_map/ppermute | solution.py:1071
  (33 shorter events, 5.8 us)
Async XLA Ops:
  2.5 6.1 %copy-start = (s32[40,8192]{1,0:T(8,128)S(1)}, s32[40,8192]{1,0:T(8,128)}, u32[]{:S(2)}) copy-start(s32[40,8192]{1,0:T(8,128)} %refs_1_.1) | copy-start | bytes 3932164
  3.5 6.8 %copy-start.1 = (f32[1,1,2,8192]{3,2,1,0:T(2,128)S(1)}, f32[1,1,2,8192]{3,2,1,0:T(2,128)}, u32[]{:S(2)}) copy-start(f32[1,1,2,8192]{3,2,1,0:T(2,128)} %param.13) | copy-start | bytes 196612
  3.5 6.8 %copy-start.2 = (f32[1,1,2,8192]{3,2,1,0:T(2,128)S(1)}, f32[1,1,2,8192]{3,2,1,0:T(2,128)}, u32[]{:S(2)}) copy-start(f32[1,1,2,8192]{3,2,1,0:T(2,128)} %param.15) | copy-start | bytes 196612
  3.5 6.8 %copy-start.3 = (f32[1,1,2,3,8192]{4,2,3,1,0:T(2,128)S(1)}, f32[1,1,2,3,8192]{4,2,3,1,0:T(2,128)}, u32[]{:S(2)}) copy-start(f32[1,1,2,3,8192]{4,2,3,1,0:T(2,128)} %param.17) | copy-start | bytes 589828
  4.1 4.6 %collective-permute-start = (f32[96,128]{1,0:T(8,128)S(1)}, f32[96,128]{1,0:T(8,128)S(1)}, u32[]{:S(2)}, u32[]{:S(2)}) collective-permute-start(f32[96,128]{1,0:T(8,128)S(1)} %get-tuple-element.58), channel_id=1, source_target_pairs={{0,1},{1,2},{2,3},{3,0},{4,5},{5,6},{6,7},{7,4},{8,9},{9,10},{10,1... | collective-permute-start | bytes 147464 | tf_op jit(solution)/shard_map/ppermute | solution.py:1065
  4.6 4.7 %collective-permute-start.1 = (f32[96,128]{1,0:T(8,128)S(1)}, f32[96,128]{1,0:T(8,128)S(1)}, u32[]{:S(2)}, u32[]{:S(2)}) collective-permute-start(f32[96,128]{1,0:T(8,128)S(1)} %get-tuple-element.59), channel_id=1, source_target_pairs={{0,2},{1,3},{2,0},{3,1},{4,6},{5,7},{6,4},{7,5},{8,10},{9,11},{10,... | collective-permute-start | bytes 147464 | tf_op jit(solution)/shard_map/ppermute | solution.py:1065
  7.2 3.1 %collective-permute-start.2 = (f32[96,128]{1,0:T(8,128)S(1)}, f32[96,128]{1,0:T(8,128)S(1)}, u32[]{:S(2)}, u32[]{:S(2)}) collective-permute-start(f32[96,128]{1,0:T(8,128)S(1)} %get-tuple-element.60), channel_id=1, source_target_pairs={{0,3},{1,0},{2,1},{3,2},{4,7},{5,4},{6,5},{7,6},{8,11},{9,8},{10,9... | collective-permute-start | bytes 147464 | tf_op jit(solution)/shard_map/ppermute | solution.py:1065
  10.9 13.1 %collective-permute-start.3 = (f32[168,128]{1,0:T(8,128)S(1)}, f32[168,128]{1,0:T(8,128)S(1)}, u32[]{:S(2)}, u32[]{:S(2)}) collective-permute-start(f32[168,128]{1,0:T(8,128)S(1)} %get-tuple-element.62), channel_id=1, source_target_pairs={{0,1},{1,2},{2,3},{3,0},{4,5},{5,6},{6,7},{7,4},{8,9},{9,10},{10,1... | collective-permute-start | bytes 258056 | tf_op jit(solution)/shard_map/ppermute | solution.py:1065
  17.8 6.2 %collective-permute-start.5 = (f32[168,128]{1,0:T(8,128)S(1)}, f32[168,128]{1,0:T(8,128)S(1)}, u32[]{:S(2)}, u32[]{:S(2)}) collective-permute-start(f32[168,128]{1,0:T(8,128)S(1)} %get-tuple-element.64), channel_id=1, source_target_pairs={{0,3},{1,0},{2,1},{3,2},{4,7},{5,4},{6,5},{7,6},{8,11},{9,8},{10,9... | collective-permute-start | bytes 258056 | tf_op jit(solution)/shard_map/ppermute | solution.py:1065
  17.8 6.2 %collective-permute-start.4 = (f32[120,128]{1,0:T(8,128)S(1)}, f32[120,128]{1,0:T(8,128)S(1)}, u32[]{:S(2)}, u32[]{:S(2)}) collective-permute-start(f32[120,128]{1,0:T(8,128)S(1)} %get-tuple-element.63), channel_id=1, source_target_pairs={{0,2},{1,3},{2,0},{3,1},{4,6},{5,7},{6,4},{7,5},{8,10},{9,11},{10,... | collective-permute-start | bytes 184328 | tf_op jit(solution)/shard_map/ppermute | solution.py:1065
  24.5 7.0 %collective-permute-start.6 = (f32[5,16,128]{2,1,0:T(8,128)S(1)}, f32[5,16,128]{2,1,0:T(8,128)S(1)}, u32[]{:S(2)}, u32[]{:S(2)}) collective-permute-start(f32[5,16,128]{2,1,0:T(8,128)S(1)} %get-tuple-element.67), channel_id=1, source_target_pairs={{0,4},{8,12},{16,20},{24,28},{4,0},{12,8},{20,16},{28,24},{1,5},{9... | collective-permute-start | bytes 122888 | tf_op jit(solution)/shard_map/ppermute | solution.py:1071
  26.6 6.7 %collective-permute-start.7 = (f32[5,16,128]{2,1,0:T(8,128)S(1)}, f32[5,16,128]{2,1,0:T(8,128)S(1)}, u32[]{:S(2)}, u32[]{:S(2)}) collective-permute-start(f32[5,16,128]{2,1,0:T(8,128)S(1)} %get-tuple-element.68), channel_id=1, source_target_pairs={{4,8},{12,16},{20,24},{28,0},{8,4},{16,12},{24,20},{0,28},{5,9},{1... | collective-permute-start | bytes 122888 | tf_op jit(solution)/shard_map/ppermute | solution.py:1071
  34.0 3.6 %collective-permute-start.8 = (f32[96,128]{1,0:T(8,128)S(1)}, f32[96,128]{1,0:T(8,128)S(1)}, u32[]{:S(2)}, u32[]{:S(2)}) collective-permute-start(f32[96,128]{1,0:T(8,128)S(1)} %get-tuple-element.75), channel_id=1, source_target_pairs={{0,1},{1,2},{2,3},{3,0},{4,5},{5,6},{6,7},{7,4},{8,9},{9,10},{10,1... | collective-permute-start | bytes 147464 | tf_op jit(solution)/shard_map/ppermute | solution.py:1065
  34.0 4.6 %collective-permute-start.9 = (f32[96,128]{1,0:T(8,128)S(1)}, f32[96,128]{1,0:T(8,128)S(1)}, u32[]{:S(2)}, u32[]{:S(2)}) collective-permute-start(f32[96,128]{1,0:T(8,128)S(1)} %get-tuple-element.76), channel_id=1, source_target_pairs={{0,2},{1,3},{2,0},{3,1},{4,6},{5,7},{6,4},{7,5},{8,10},{9,11},{10,... | collective-permute-start | bytes 147464 | tf_op jit(solution)/shard_map/ppermute | solution.py:1065
  35.1 3.5 %collective-permute-start.10 = (f32[96,128]{1,0:T(8,128)S(1)}, f32[96,128]{1,0:T(8,128)S(1)}, u32[]{:S(2)}, u32[]{:S(2)}) collective-permute-start(f32[96,128]{1,0:T(8,128)S(1)} %get-tuple-element.77), channel_id=1, source_target_pairs={{0,3},{1,0},{2,1},{3,2},{4,7},{5,4},{6,5},{7,6},{8,11},{9,8},{10,9... | collective-permute-start | bytes 147464 | tf_op jit(solution)/shard_map/ppermute | solution.py:1065
  39.4 11.5 %collective-permute-start.11 = (f32[168,128]{1,0:T(8,128)S(1)}, f32[168,128]{1,0:T(8,128)S(1)}, u32[]{:S(2)}, u32[]{:S(2)}) collective-permute-start(f32[168,128]{1,0:T(8,128)S(1)} %get-tuple-element.79), channel_id=1, source_target_pairs={{0,1},{1,2},{2,3},{3,0},{4,5},{5,6},{6,7},{7,4},{8,9},{9,10},{10,1... | collective-permute-start | bytes 258056 | tf_op jit(solution)/shard_map/ppermute | solution.py:1065
  45.5 5.3 %collective-permute-start.13 = (f32[168,128]{1,0:T(8,128)S(1)}, f32[168,128]{1,0:T(8,128)S(1)}, u32[]{:S(2)}, u32[]{:S(2)}) collective-permute-start(f32[168,128]{1,0:T(8,128)S(1)} %get-tuple-element.81), channel_id=1, source_target_pairs={{0,3},{1,0},{2,1},{3,2},{4,7},{5,4},{6,5},{7,6},{8,11},{9,8},{10,9... | collective-permute-start | bytes 258056 | tf_op jit(solution)/shard_map/ppermute | solution.py:1065
  45.6 5.3 %collective-permute-start.12 = (f32[120,128]{1,0:T(8,128)S(1)}, f32[120,128]{1,0:T(8,128)S(1)}, u32[]{:S(2)}, u32[]{:S(2)}) collective-permute-start(f32[120,128]{1,0:T(8,128)S(1)} %get-tuple-element.80), channel_id=1, source_target_pairs={{0,2},{1,3},{2,0},{3,1},{4,6},{5,7},{6,4},{7,5},{8,10},{9,11},{10,... | collective-permute-start | bytes 184328 | tf_op jit(solution)/shard_map/ppermute | solution.py:1065
  51.4 5.7 %collective-permute-start.14 = (f32[5,16,128]{2,1,0:T(8,128)S(1)}, f32[5,16,128]{2,1,0:T(8,128)S(1)}, u32[]{:S(2)}, u32[]{:S(2)}) collective-permute-start(f32[5,16,128]{2,1,0:T(8,128)S(1)} %get-tuple-element.86), channel_id=1, source_target_pairs={{0,4},{8,12},{16,20},{24,28},{4,0},{12,8},{20,16},{28,24},{1,5},{9... | collective-permute-start | bytes 122888 | tf_op jit(solution)/shard_map/ppermute | solution.py:1071
  51.4 6.8 %collective-permute-start.15 = (f32[5,16,128]{2,1,0:T(8,128)S(1)}, f32[5,16,128]{2,1,0:T(8,128)S(1)}, u32[]{:S(2)}, u32[]{:S(2)}) collective-permute-start(f32[5,16,128]{2,1,0:T(8,128)S(1)} %get-tuple-element.87), channel_id=1, source_target_pairs={{4,8},{12,16},{20,24},{28,0},{8,4},{16,12},{24,20},{0,28},{5,9},{1... | collective-permute-start | bytes 122888 | tf_op jit(solution)/shard_map/ppermute | solution.py:1071

commit v6 on v5

--- a/solution.py
+++ b/solution.py
@@ -758,7 +758,6 @@
     lanes = iota((sh.levels, LANES), 1)
     blank = jnp.zeros((sh.levels, LANES), F32)
     planes_at = (0, sh.xs - 1)
-    even = lax.rem(lax.axis_index("gx"), 2) == 0
     beyond = unpack_columns(sh, forces[1], forces[sh.tiles - 1], sh.section + 8 + sh.levels)[-1]
     corner = [pltpu.roll(beyond, (LANES - 4 * q) % LANES, 1) for q in range(19)]
     corner_force = [blank, blank, blank]
@@ -799,8 +798,8 @@
                 value = pltpu.roll(value, DIRS[q][2] % sh.levels, 0)
             leaving[which].append(value)
     for k, (down, up) in enumerate(zip(*leaving)):
-        outs[0][k] = jnp.where(even, up, down)
-        outs[1][k] = jnp.where(even, down, up)
+        outs[0][k] = up
+        outs[1][k] = down
 
 
 def make_edges(sh, plan, f, edges, forces, after):
@@ -1063,32 +1062,6 @@
 def shifted(x, axis, by):
     count = lax.axis_size(axis)
     return lax.ppermute(x, axis, [(i, (i + by) % count) for i in range(count)])
-
-
-def swapped(x, axis, first):
-    count = lax.axis_size(axis)
-    pairs = [(i, (i + 1) % count) for i in range(first, count, 2)]
-    return lax.ppermute(x, axis, pairs + [(b, a) for a, b in pairs])
-
-
-def join_kernel(one, two, low, high):
-    even = lax.rem(lax.axis_index("gx"), 2) == 0
-    low[...] = jnp.where(even, two[...], one[...])
-    high[...] = jnp.where(even, one[...], two[...])
-
-
-def exchange(one, two):
-    two = swapped(two, "gx", 1)
-    one = swapped(one, "gx", 0)
-    out = pl.pallas_call(
-        join_kernel,
-        out_shape=[pltpu.VMEM(one.shape, F32)] * 2,
-        in_specs=[VM, VM],
-        out_specs=[VM, VM],
-        compiler_params=PARAMS,
-        name="join",
-    )(in_vmem(one), in_vmem(two))
-    return tuple(in_vmem(x) for x in out)
 
 
 def local(
@@ -1140,7 +1113,7 @@
         bulk = in_vmem(bulk[0])
         sent = make_edges(sh, plan, f, edges, forces, bulk)
         done = do_patch(sh, last, plan, planes, forces, bulk)
-        edges = exchange(*sent)
+        edges = (in_vmem(shifted(sent[0], "gx", 1)), in_vmem(shifted(sent[1], "gx", -1)))
         f = in_vmem(done[0])
     f = finish(sh, f, done[1], edges)
     loads_out, filt_out = [

time: 59.5 us -> 58.4 us (0.982)
  Pallas kernels: 16.6 us -> 31.3 us
  starting transfers between devices: 33.6 us -> 20.1 us
  waiting for transfers between devices: 8.1 us -> 5.88 us
    pallas_call x2, Pallas kernels: 1.36 us -> 12.1 us  [do_markers(): pl.pallas_call(lambda *refs: marker_kernel(sh, step, *refs), out_shape=[d...]
    ppermute x4 -> x0, starting transfers between devices: 8.54 us -> none  [swapped(): return lax.ppermute(x, axis, pairs + [(b, a) for a, b in pairs])]
    ppermute x12 -> x16, starting transfers between devices: 25.1 us -> 20.1 us  [shifted(): return lax.ppermute(x, axis, [(i, (i + by) % count) for i in range(count)])]
    pallas_call x1, Pallas kernels: 0.07 us -> 4.06 us  [make_tables(): pl.pallas_call(lambda *refs: table_kernel(sh, *refs), out_shape=[pltpu.VM...]
    ppermute x4 -> x0, waiting for transfers between devices: 3 us -> none  [swapped(): return lax.ppermute(x, axis, pairs + [(b, a) for a, b in pairs])]
    ppermute x12 -> x16, waiting for transfers between devices: 5.11 us -> 5.88 us  [shifted(): return lax.ppermute(x, axis, [(i, (i + by) % count) for i in range(count)])]
  transfers between devices with their start and end apart: 16 -> 16, of which waited for: 8 -> 5; matrix products, arithmetic and copies ran while one was open for 0% -> 0% of each run, Pallas kernels for 16% -> 23%
where the time goes in v6:
time: 58.4 us; the launch traced here: 58.3 us
  Pallas kernels  31.3 us (54%)
  starting transfers between devices  20.1 us (34%)
  waiting for transfers between devices  5.88 us (10%)
  between operations  0.99 us (2%)
    ppermute x16, starting transfers between devices, shifted(): return lax.ppermute(x, axis, [(i, (i + by) % count) for i in range(count)])  20.1 us
    pallas_call x2, Pallas kernels, do_markers(): pl.pallas_call(lambda *refs: marker_kernel(sh, step, *refs), out_shape=[d...  12.1 us
    ppermute x16, waiting for transfers between devices, shifted(): return lax.ppermute(x, axis, [(i, (i + by) % count) for i in range(count)])  5.88 us
    pallas_call x2, Pallas kernels, do_bulk(): pl.pallas_call(lambda *refs: bulk_kernel(sh, bool(edges), last, *refs), o...  4.2 us
    pallas_call x2, Pallas kernels, do_patch(): pl.pallas_call(lambda *refs: patch_kernel(sh, last, *refs), out_shape=out...  4.14 us
    pallas_call x1, Pallas kernels, make_tables(): pl.pallas_call(lambda *refs: table_kernel(sh, *refs), out_shape=[pltpu.VM...  4.06 us
    pallas_call x2, Pallas kernels, make_columns(): pl.pallas_call(lambda *refs: column_kernel(sh, bool(edges), *refs), out_s...  1.94 us
    pallas_call x1, Pallas kernels, start(): pl.pallas_call(lambda *refs: start_kernel(sh, *refs), out_shape=[pltpu.SM...  1.84 us
  transfers between devices with their start and end apart: 16, of which 5 were waited for; matrix products, arithmetic and copies ran while one was open for 0% of the time, Pallas kernels for 23%

profile of v6, /device:TPU:0, one launch (start us, length us, event | category | flops | bytes accessed | tf_op | source)
XLA Modules:
  0.0 58.3 jit_solution(3840148019366034540)
XLA Ops:
  0.6 1.8 %start.1 = (s32[8]{0:T(128)S(4)}, f32[6,128,128]{2,1,0:T(8,128)S(1)}, f32[19,256,128]{2,1,0:T(8,128)S(1)}) custom-call(s32[3,40]{1,0:T(4,128)} %bitcast.60, s32[2,40]{1,0:T(2,128)} %bitcast.61, f32[128,128]{1,0:T(8,128)} %bitcast.58, f32[128,128]{1,0:T(8,128)} %bitcast.59, f32[19,256,128]{2,1,0:T(8,128)} %bitcast.57), custom_call_target="tpu_custom_call" | custom-call | tf_op jit(solution)/shard_map/start/pallas_call | solution.py:302
  2.5 1.0 %columns.2 = (f32[48,128]{1,0:T(8,128)S(1)}, f32[48,128]{1,0:T(8,128)S(1)}) custom-call(s32[8]{0:T(128)S(4)} %get-tuple-element.44.refs_0_, f32[19,256,128]{2,1,0:T(8,128)S(1)} %get-tuple-element.45.refs_1_), custom_call_target="tpu_custom_call" | custom-call | tf_op jit(solution)/shard_map/columns/pallas_call | solution.py:412
  4.6 2.6 %collective-permute-start.1 = (f32[96,128]{1,0:T(8,128)S(1)}, f32[96,128]{1,0:T(8,128)S(1)}, u32[]{:S(2)}, u32[]{:S(2)}) collective-permute-start(f32[96,128]{1,0:T(8,128)S(1)} %get-tuple-element.55), channel_id=1, source_target_pairs={{0,2},{1,3},{2,0},{3,1},{4,6},{5,7},{6,4},{7,5},{8,10},{9,11},{10,... | collective-permute-start | bytes 147464 | tf_op jit(solution)/shard_map/ppermute | solution.py:1064
  7.2 1.4 %collective-permute-start.2 = (f32[96,128]{1,0:T(8,128)S(1)}, f32[96,128]{1,0:T(8,128)S(1)}, u32[]{:S(2)}, u32[]{:S(2)}) collective-permute-start(f32[96,128]{1,0:T(8,128)S(1)} %get-tuple-element.56), channel_id=1, source_target_pairs={{0,3},{1,0},{2,1},{3,2},{4,7},{5,4},{6,5},{7,6},{8,11},{9,8},{10,9... | collective-permute-start | bytes 147464 | tf_op jit(solution)/shard_map/ppermute | solution.py:1064
  8.6 4.1 %tables.1 = (bf16[2,2,256,8192]{3,2,1,0:T(8,128)(2,1)S(1)}, f32[2,16,8192]{2,1,0:T(8,128)S(1)}, s32[4]{0:T(128)S(4)}) custom-call(s32[8]{0:T(128)S(4)} %get-tuple-element.44.refs_0_, s32[40,8192]{1,0:T(8,128)S(1)} %copy-done, f32[96,128]{1,0:T(8,128)S(1)} %get-tuple-element.49.refs_2_.refs_10_), custom_call_target="tpu_custom_call" | custom-call | tf_op jit(solution)/shard_map/tables/pallas_call | solution.py:522
  12.7 5.9 %markers.2 = (f32[3,128,128]{2,1,0:T(8,128)S(1)}, f32[3,128,128]{2,1,0:T(8,128)S(1)}, f32[120,128]{1,0:T(8,128)S(1)}, f32[168,128]{1,0:T(8,128)S(1)}, f32[120,128]{1,0:T(8,128)S(1)}, /*index=5*/f32[168,128]{1,0:T(8,128)S(1)}) custom-call(s32[8]{0:T(128)S(4)} %get-tuple-element.44.refs_0_, s32[4]{0:T(128)S(4)} %get-tuple-element.50.refs_1_, ...), custom_call_target="tpu_custom_call" | custom-call | tf_op jit(solution)/shard_map/markers/pallas_call | solution.py:734
  18.7 1.7 %collective-permute-start.5 = (f32[168,128]{1,0:T(8,128)S(1)}, f32[168,128]{1,0:T(8,128)S(1)}, u32[]{:S(2)}, u32[]{:S(2)}) collective-permute-start(f32[168,128]{1,0:T(8,128)S(1)} %get-tuple-element.60), channel_id=1, source_target_pairs={{0,3},{1,0},{2,1},{3,2},{4,7},{5,4},{6,5},{7,6},{8,11},{9,8},{10,9... | collective-permute-start | bytes 258056 | tf_op jit(solution)/shard_map/ppermute | solution.py:1064
  20.4 2.0 %bulk.2.refs_6_ = f32[19,256,128]{2,1,0:T(8,128)S(1)} custom-call(s32[8]{0:T(128)S(4)} %get-tuple-element.44.refs_0_, f32[19,256,128]{2,1,0:T(8,128)S(1)} %get-tuple-element.45.refs_1_, f32[3,128,128]{2,1,0:T(8,128)S(1)} %get-tuple-element.61.refs_2_, f32[3,128,128]{2,1,0:T(8,128)S(1)} %get-tuple-element.62.refs_3_.refs_7_), custom_call_target="tpu_custom_call" | custom-call | tf_op jit(solution)/shard_map/bulk/pallas_call | solution.py:884
  22.4 2.2 %collective-permute-done.4.refs_4_ = f32[120,128]{1,0:T(8,128)S(1)} collective-permute-done((f32[120,128]{1,0:T(8,128)S(1)}, f32[120,128]{1,0:T(8,128)S(1)}, u32[]{:S(2)}, u32[]{:S(2)}) %collective-permute-start.4) | collective-permute-done | bytes 61472 | tf_op jit(solution)/shard_map/ppermute | solution.py:1064
  25.1 1.0 %collective-permute-start.6 = (f32[5,16,128]{2,1,0:T(8,128)S(1)}, f32[5,16,128]{2,1,0:T(8,128)S(1)}, u32[]{:S(2)}, u32[]{:S(2)}) collective-permute-start(f32[5,16,128]{2,1,0:T(8,128)S(1)} %get-tuple-element.63), channel_id=1, source_target_pairs={{0,4},{4,8},{8,12},{12,16},{16,20},{20,24},{24,28},{28,0},{1,5},{5... | collective-permute-start | bytes 122888 | tf_op jit(solution)/shard_map/ppermute | solution.py:1064
  26.1 3.7 %collective-permute-start.7 = (f32[5,16,128]{2,1,0:T(8,128)S(1)}, f32[5,16,128]{2,1,0:T(8,128)S(1)}, u32[]{:S(2)}, u32[]{:S(2)}) collective-permute-start(f32[5,16,128]{2,1,0:T(8,128)S(1)} %get-tuple-element.64), channel_id=1, source_target_pairs={{0,28},{4,0},{8,4},{12,8},{16,12},{20,16},{24,20},{28,24},{1,29},{... | collective-permute-start | bytes 122888 | tf_op jit(solution)/shard_map/ppermute | solution.py:1064
  29.9 1.6 %patch.2.refs_1_ = f32[19,256,128]{2,1,0:T(8,128)S(1)} custom-call(s32[8]{0:T(128)S(4)} %get-tuple-element.44.refs_0_, f32[8,19,16,128]{3,2,1,0:T(8,128)S(1)} %get-tuple-element.48.refs_1_, f32[120,128]{1,0:T(8,128)S(1)} %get-tuple-element.57.refs_2_, f32[168,128]{1,0:T(8,128)S(1)} %collective-permute-done.3.refs_3_, ...), custom_call_target="tpu_custom_call", output_to_operand_aliasing={{}: (6, {})} | custom-call | tf_op jit(solution)/shard_map/patch/pallas_call | solution.py:993
  32.5 1.1 %collective-permute-start.9 = (f32[96,128]{1,0:T(8,128)S(1)}, f32[96,128]{1,0:T(8,128)S(1)}, u32[]{:S(2)}, u32[]{:S(2)}) collective-permute-start(f32[96,128]{1,0:T(8,128)S(1)} %get-tuple-element.70), channel_id=1, source_target_pairs={{0,2},{1,3},{2,0},{3,1},{4,6},{5,7},{6,4},{7,5},{8,10},{9,11},{10,... | collective-permute-start | bytes 147464 | tf_op jit(solution)/shard_map/ppermute | solution.py:1064
  33.6 1.4 %collective-permute-start.10 = (f32[96,128]{1,0:T(8,128)S(1)}, f32[96,128]{1,0:T(8,128)S(1)}, u32[]{:S(2)}, u32[]{:S(2)}) collective-permute-start(f32[96,128]{1,0:T(8,128)S(1)} %get-tuple-element.71), channel_id=1, source_target_pairs={{0,3},{1,0},{2,1},{3,2},{4,7},{5,4},{6,5},{7,6},{8,11},{9,8},{10,9... | collective-permute-start | bytes 147464 | tf_op jit(solution)/shard_map/ppermute | solution.py:1064
  34.9 1.0 %columns.3 = (f32[48,128]{1,0:T(8,128)S(1)}, f32[48,128]{1,0:T(8,128)S(1)}) custom-call(s32[8]{0:T(128)S(4)} %get-tuple-element.44.refs_0_, f32[19,256,128]{2,1,0:T(8,128)S(1)} %patch.2.refs_1_, f32[5,16,128]{2,1,0:T(8,128)S(1)} %collective-permute-done.6.refs_2_, f32[5,16,128]{2,1,0:T(8,128)S(1)} %collective-permute-done.7.refs_3_), custom_call_target="tpu_custom_call" | custom-call | tf_op jit(solution)/shard_map/columns/pallas_call | solution.py:412
  36.0 1.1 %collective-permute-done.9.refs_12_ = f32[96,128]{1,0:T(8,128)S(1)} collective-permute-done((f32[96,128]{1,0:T(8,128)S(1)}, f32[96,128]{1,0:T(8,128)S(1)}, u32[]{:S(2)}, u32[]{:S(2)}) %collective-permute-start.9) | collective-permute-done | bytes 49184 | tf_op jit(solution)/shard_map/ppermute | solution.py:1064
  37.1 6.2 %markers.3 = (f32[3,128,128]{2,1,0:T(8,128)S(1)}, f32[3,128,128]{2,1,0:T(8,128)S(1)}, f32[120,128]{1,0:T(8,128)S(1)}, f32[168,128]{1,0:T(8,128)S(1)}, f32[120,128]{1,0:T(8,128)S(1)}, /*index=5*/f32[168,128]{1,0:T(8,128)S(1)}) custom-call(s32[8]{0:T(128)S(4)} %get-tuple-element.44.refs_0_, s32[4]{0:T(128)S(4)} %get-tuple-element.50.refs_1_, ...), custom_call_target="tpu_custom_call" | custom-call | tf_op jit(solution)/shard_map/markers/pallas_call | solution.py:734
  43.2 1.7 %collective-permute-start.13 = (f32[168,128]{1,0:T(8,128)S(1)}, f32[168,128]{1,0:T(8,128)S(1)}, u32[]{:S(2)}, u32[]{:S(2)}) collective-permute-start(f32[168,128]{1,0:T(8,128)S(1)} %get-tuple-element.75), channel_id=1, source_target_pairs={{0,3},{1,0},{2,1},{3,2},{4,7},{5,4},{6,5},{7,6},{8,11},{9,8},{10,9... | collective-permute-start | bytes 258056 | tf_op jit(solution)/shard_map/ppermute | solution.py:1064
  45.0 2.2 %bulk.3 = (f32[19,256,128]{2,1,0:T(8,128)S(1)}, f32[3,128,128]{2,1,0:T(8,128)}, f32[3,128,128]{2,1,0:T(8,128)}) custom-call(s32[8]{0:T(128)S(4)} %get-tuple-element.44.refs_0_, f32[19,256,128]{2,1,0:T(8,128)S(1)} %patch.2.refs_1_, f32[5,16,128]{2,1,0:T(8,128)S(1)} %collective-permute-done.6.refs_2_, f32[5,16,128]{2,1,0:T(8,128)S(1)} %collective-permute-done.7.refs_3_, ...), custom_call_target="tpu_custom_call" | custom-call | tf_op jit(solution)/shard_map/bulk/pallas_call | solution.py:884
  47.2 2.2 %collective-permute-done.12.refs_4_.refs_6_ = f32[120,128]{1,0:T(8,128)S(1)} collective-permute-done((f32[120,128]{1,0:T(8,128)S(1)}, f32[120,128]{1,0:T(8,128)S(1)}, u32[]{:S(2)}, u32[]{:S(2)}) %collective-permute-start.12) | collective-permute-done | bytes 61472 | tf_op jit(solution)/shard_map/ppermute | solution.py:1064
  49.9 1.2 %collective-permute-start.14 = (f32[5,16,128]{2,1,0:T(8,128)S(1)}, f32[5,16,128]{2,1,0:T(8,128)S(1)}, u32[]{:S(2)}, u32[]{:S(2)}) collective-permute-start(f32[5,16,128]{2,1,0:T(8,128)S(1)} %get-tuple-element.80), channel_id=1, source_target_pairs={{0,4},{4,8},{8,12},{12,16},{16,20},{20,24},{24,28},{28,0},{1,5},{5... | collective-permute-start | bytes 122888 | tf_op jit(solution)/shard_map/ppermute | solution.py:1064
  51.0 3.6 %collective-permute-start.15 = (f32[5,16,128]{2,1,0:T(8,128)S(1)}, f32[5,16,128]{2,1,0:T(8,128)S(1)}, u32[]{:S(2)}, u32[]{:S(2)}) collective-permute-start(f32[5,16,128]{2,1,0:T(8,128)S(1)} %get-tuple-element.81), channel_id=1, source_target_pairs={{0,28},{4,0},{8,4},{12,8},{16,12},{20,16},{24,20},{28,24},{1,29},{... | collective-permute-start | bytes 122888 | tf_op jit(solution)/shard_map/ppermute | solution.py:1064
  54.7 2.5 %patch.3 = (f32[19,256,128]{2,1,0:T(8,128)S(1)}, f32[19,256,128]{2,1,0:T(8,128)}) custom-call(s32[8]{0:T(128)S(4)} %get-tuple-element.44.refs_0_, f32[8,19,16,128]{3,2,1,0:T(8,128)S(1)} %get-tuple-element.65.refs_1_, f32[120,128]{1,0:T(8,128)S(1)} %get-tuple-element.72.refs_2_.refs_4_, ...), custom_call_target="tpu_custom_call", output_to_operand_aliasing={{0}: (6, {})} | custom-call | tf_op jit(solution)/shard_map/patch/pallas_call | solution.py:993
  57.2 0.9 %finish.1 = f32[19,16,16,128]{3,2,1,0:T(8,128)} custom-call(f32[19,256,128]{2,1,0:T(8,128)S(1)} %get-tuple-element.79.refs_0_, f32[5,16,128]{2,1,0:T(8,128)S(1)} %collective-permute-done.14.refs_1_, f32[5,16,128]{2,1,0:T(8,128)S(1)} %collective-permute-done.15.refs_2_, f32[19,16,16,128]{3,2,1,0:T(8,128)} %bitcast.56), custom_call_target="tpu_custom_call", output_to_operand_aliasing={{}: (3, {})} | custom-call | tf_op jit(solution)/shard_map/finish/pallas_call | solution.py:1035
  (31 shorter events, 3.2 us)
Async XLA Ops:
  2.5 6.1 %copy-start = (s32[40,8192]{1,0:T(8,128)S(1)}, s32[40,8192]{1,0:T(8,128)}, u32[]{:S(2)}) copy-start(s32[40,8192]{1,0:T(8,128)} %refs_1_.1) | copy-start | bytes 3932164
  3.5 9.2 %copy-start.1 = (f32[1,1,2,8192]{3,2,1,0:T(2,128)S(1)}, f32[1,1,2,8192]{3,2,1,0:T(2,128)}, u32[]{:S(2)}) copy-start(f32[1,1,2,8192]{3,2,1,0:T(2,128)} %param.13) | copy-start | bytes 196612
  3.5 9.2 %copy-start.2 = (f32[1,1,2,8192]{3,2,1,0:T(2,128)S(1)}, f32[1,1,2,8192]{3,2,1,0:T(2,128)}, u32[]{:S(2)}) copy-start(f32[1,1,2,8192]{3,2,1,0:T(2,128)} %param.15) | copy-start | bytes 196612
  3.5 9.2 %copy-start.3 = (f32[1,1,2,3,8192]{4,2,3,1,0:T(2,128)S(1)}, f32[1,1,2,3,8192]{4,2,3,1,0:T(2,128)}, u32[]{:S(2)}) copy-start(f32[1,1,2,3,8192]{4,2,3,1,0:T(2,128)} %param.17) | copy-start | bytes 589828
  4.1 8.6 %collective-permute-start = (f32[96,128]{1,0:T(8,128)S(1)}, f32[96,128]{1,0:T(8,128)S(1)}, u32[]{:S(2)}, u32[]{:S(2)}) collective-permute-start(f32[96,128]{1,0:T(8,128)S(1)} %get-tuple-element.54), channel_id=1, source_target_pairs={{0,1},{1,2},{2,3},{3,0},{4,5},{5,6},{6,7},{7,4},{8,9},{9,10},{10,1... | collective-permute-start | bytes 147464 | tf_op jit(solution)/shard_map/ppermute | solution.py:1064
  4.6 8.1 %collective-permute-start.1 = (f32[96,128]{1,0:T(8,128)S(1)}, f32[96,128]{1,0:T(8,128)S(1)}, u32[]{:S(2)}, u32[]{:S(2)}) collective-permute-start(f32[96,128]{1,0:T(8,128)S(1)} %get-tuple-element.55), channel_id=1, source_target_pairs={{0,2},{1,3},{2,0},{3,1},{4,6},{5,7},{6,4},{7,5},{8,10},{9,11},{10,... | collective-permute-start | bytes 147464 | tf_op jit(solution)/shard_map/ppermute | solution.py:1064
  7.2 5.5 %collective-permute-start.2 = (f32[96,128]{1,0:T(8,128)S(1)}, f32[96,128]{1,0:T(8,128)S(1)}, u32[]{:S(2)}, u32[]{:S(2)}) collective-permute-start(f32[96,128]{1,0:T(8,128)S(1)} %get-tuple-element.56), channel_id=1, source_target_pairs={{0,3},{1,0},{2,1},{3,2},{4,7},{5,4},{6,5},{7,6},{8,11},{9,8},{10,9... | collective-permute-start | bytes 147464 | tf_op jit(solution)/shard_map/ppermute | solution.py:1064
  18.6 6.0 %collective-permute-start.3 = (f32[168,128]{1,0:T(8,128)S(1)}, f32[168,128]{1,0:T(8,128)S(1)}, u32[]{:S(2)}, u32[]{:S(2)}) collective-permute-start(f32[168,128]{1,0:T(8,128)S(1)} %get-tuple-element.58), channel_id=1, source_target_pairs={{0,1},{1,2},{2,3},{3,0},{4,5},{5,6},{6,7},{7,4},{8,9},{9,10},{10,1... | collective-permute-start | bytes 258056 | tf_op jit(solution)/shard_map/ppermute | solution.py:1064
  18.7 6.0 %collective-permute-start.5 = (f32[168,128]{1,0:T(8,128)S(1)}, f32[168,128]{1,0:T(8,128)S(1)}, u32[]{:S(2)}, u32[]{:S(2)}) collective-permute-start(f32[168,128]{1,0:T(8,128)S(1)} %get-tuple-element.60), channel_id=1, source_target_pairs={{0,3},{1,0},{2,1},{3,2},{4,7},{5,4},{6,5},{7,6},{8,11},{9,8},{10,9... | collective-permute-start | bytes 258056 | tf_op jit(solution)/shard_map/ppermute | solution.py:1064
  20.4 4.2 %collective-permute-start.4 = (f32[120,128]{1,0:T(8,128)S(1)}, f32[120,128]{1,0:T(8,128)S(1)}, u32[]{:S(2)}, u32[]{:S(2)}) collective-permute-start(f32[120,128]{1,0:T(8,128)S(1)} %get-tuple-element.59), channel_id=1, source_target_pairs={{0,2},{1,3},{2,0},{3,1},{4,6},{5,7},{6,4},{7,5},{8,10},{9,11},{10,... | collective-permute-start | bytes 184328 | tf_op jit(solution)/shard_map/ppermute | solution.py:1064
  25.1 6.7 %collective-permute-start.6 = (f32[5,16,128]{2,1,0:T(8,128)S(1)}, f32[5,16,128]{2,1,0:T(8,128)S(1)}, u32[]{:S(2)}, u32[]{:S(2)}) collective-permute-start(f32[5,16,128]{2,1,0:T(8,128)S(1)} %get-tuple-element.63), channel_id=1, source_target_pairs={{0,4},{4,8},{8,12},{12,16},{16,20},{20,24},{24,28},{28,0},{1,5},{5... | collective-permute-start | bytes 122888 | tf_op jit(solution)/shard_map/ppermute | solution.py:1064
  26.1 5.7 %collective-permute-start.7 = (f32[5,16,128]{2,1,0:T(8,128)S(1)}, f32[5,16,128]{2,1,0:T(8,128)S(1)}, u32[]{:S(2)}, u32[]{:S(2)}) collective-permute-start(f32[5,16,128]{2,1,0:T(8,128)S(1)} %get-tuple-element.64), channel_id=1, source_target_pairs={{0,28},{4,0},{8,4},{12,8},{16,12},{20,16},{24,20},{28,24},{1,29},{... | collective-permute-start | bytes 122888 | tf_op jit(solution)/shard_map/ppermute | solution.py:1064
  32.4 3.6 %collective-permute-start.8 = (f32[96,128]{1,0:T(8,128)S(1)}, f32[96,128]{1,0:T(8,128)S(1)}, u32[]{:S(2)}, u32[]{:S(2)}) collective-permute-start(f32[96,128]{1,0:T(8,128)S(1)} %get-tuple-element.69), channel_id=1, source_target_pairs={{0,1},{1,2},{2,3},{3,0},{4,5},{5,6},{6,7},{7,4},{8,9},{9,10},{10,1... | collective-permute-start | bytes 147464 | tf_op jit(solution)/shard_map/ppermute | solution.py:1064
  32.5 4.6 %collective-permute-start.9 = (f32[96,128]{1,0:T(8,128)S(1)}, f32[96,128]{1,0:T(8,128)S(1)}, u32[]{:S(2)}, u32[]{:S(2)}) collective-permute-start(f32[96,128]{1,0:T(8,128)S(1)} %get-tuple-element.70), channel_id=1, source_target_pairs={{0,2},{1,3},{2,0},{3,1},{4,6},{5,7},{6,4},{7,5},{8,10},{9,11},{10,... | collective-permute-start | bytes 147464 | tf_op jit(solution)/shard_map/ppermute | solution.py:1064
  33.6 3.5 %collective-permute-start.10 = (f32[96,128]{1,0:T(8,128)S(1)}, f32[96,128]{1,0:T(8,128)S(1)}, u32[]{:S(2)}, u32[]{:S(2)}) collective-permute-start(f32[96,128]{1,0:T(8,128)S(1)} %get-tuple-element.71), channel_id=1, source_target_pairs={{0,3},{1,0},{2,1},{3,2},{4,7},{5,4},{6,5},{7,6},{8,11},{9,8},{10,9... | collective-permute-start | bytes 147464 | tf_op jit(solution)/shard_map/ppermute | solution.py:1064
  43.2 6.2 %collective-permute-start.11 = (f32[168,128]{1,0:T(8,128)S(1)}, f32[168,128]{1,0:T(8,128)S(1)}, u32[]{:S(2)}, u32[]{:S(2)}) collective-permute-start(f32[168,128]{1,0:T(8,128)S(1)} %get-tuple-element.73), channel_id=1, source_target_pairs={{0,1},{1,2},{2,3},{3,0},{4,5},{5,6},{6,7},{7,4},{8,9},{9,10},{10,1... | collective-permute-start | bytes 258056 | tf_op jit(solution)/shard_map/ppermute | solution.py:1064
  43.2 6.1 %collective-permute-start.13 = (f32[168,128]{1,0:T(8,128)S(1)}, f32[168,128]{1,0:T(8,128)S(1)}, u32[]{:S(2)}, u32[]{:S(2)}) collective-permute-start(f32[168,128]{1,0:T(8,128)S(1)} %get-tuple-element.75), channel_id=1, source_target_pairs={{0,3},{1,0},{2,1},{3,2},{4,7},{5,4},{6,5},{7,6},{8,11},{9,8},{10,9... | collective-permute-start | bytes 258056 | tf_op jit(solution)/shard_map/ppermute | solution.py:1064
  45.0 4.4 %collective-permute-start.12 = (f32[120,128]{1,0:T(8,128)S(1)}, f32[120,128]{1,0:T(8,128)S(1)}, u32[]{:S(2)}, u32[]{:S(2)}) collective-permute-start(f32[120,128]{1,0:T(8,128)S(1)} %get-tuple-element.74), channel_id=1, source_target_pairs={{0,2},{1,3},{2,0},{3,1},{4,6},{5,7},{6,4},{7,5},{8,10},{9,11},{10,... | collective-permute-start | bytes 184328 | tf_op jit(solution)/shard_map/ppermute | solution.py:1064
  49.9 7.3 %collective-permute-start.14 = (f32[5,16,128]{2,1,0:T(8,128)S(1)}, f32[5,16,128]{2,1,0:T(8,128)S(1)}, u32[]{:S(2)}, u32[]{:S(2)}) collective-permute-start(f32[5,16,128]{2,1,0:T(8,128)S(1)} %get-tuple-element.80), channel_id=1, source_target_pairs={{0,4},{4,8},{8,12},{12,16},{16,20},{20,24},{24,28},{28,0},{1,5},{5... | collective-permute-start | bytes 122888 | tf_op jit(solution)/shard_map/ppermute | solution.py:1064
  51.0 6.2 %collective-permute-start.15 = (f32[5,16,128]{2,1,0:T(8,128)S(1)}, f32[5,16,128]{2,1,0:T(8,128)S(1)}, u32[]{:S(2)}, u32[]{:S(2)}) collective-permute-start(f32[5,16,128]{2,1,0:T(8,128)S(1)} %get-tuple-element.81), channel_id=1, source_target_pairs={{0,28},{4,0},{8,4},{12,8},{16,12},{20,16},{24,20},{28,24},{1,29},{... | collective-permute-start | bytes 122888 | tf_op jit(solution)/shard_map/ppermute | solution.py:1064
